TPU v7x, 32 devices: a whole 2x2x4 slice. The times are simulated.
32 devices in a mesh: groups: 2 (over y), devs: 8 (over z, x), pair: 2 (over core).
Axes of the slice: x: 2, y: 2, z: 4, core: 2. Of those that a mesh axis runs over, the one named last changes fastest.
Arguments:
- query: bfloat16 [2, 64, 3072], P(None, ('groups', 'devs'), 'pair'), parts along dimension 1, may hold values from -66 to 66
- key_cache: bfloat16 [2, 64, 256, 512], P(None, ('groups', 'devs'), None, 'pair'), parts along dimension 1, may hold values from -7 to 7
- value_cache: bfloat16 [2, 64, 256, 512], P(None, ('groups', 'devs'), None, 'pair'), parts along dimension 1, may hold values from -18 to 18
- lengths: int32 [2, 64], P(None, ('groups', 'devs')), parts along dimension 1, may hold values from 2 to 256, as said below
- residual: bfloat16 [2, 64, 3072], P(None, ('groups', 'devs'), 'pair'), parts along dimension 1, may hold values from -180 to 180
- router: bfloat16 [3072, 4], P('pair'), may hold values from -0.109375 to 0.109375
- routes: int32 [2, 64, 2], P(None, ('groups', 'devs')), parts along dimension 1, may hold values from 0 to 3, all different within a row; in each aligned block of 4 rows (0 to 3, 4 to 7, ..., all dimensions but the last counted through in order) at most 3 rows name the same one
- w_gate: bfloat16 [3072, 32768], P(None, ('devs', 'pair')), may hold values from -0.109375 to 0.109375
- w_up: bfloat16 [3072, 32768], P(None, ('devs', 'pair')), may hold values from -0.109375 to 0.109375
- w_down: bfloat16 [32768, 3072], P(('devs', 'pair')), may hold values from -0.0625 to 0.0625
Outputs:
- mixed: bfloat16 [2, 64, 3072], P(None, ('groups', 'devs'), 'pair'), parts along dimension 1
There are 2 independent parts, one for each index of `groups`. A program takes and returns all parts, laid end to end along the dimension named above; an argument that names none is the same for every part. Nothing has to cross between parts.
Inputs may be any that keep to these rules, and one draw needn't show every extreme that they name: `lengths`: at least one request of each draw has all 256 entries live. `routes`: among the requests of one index of devs in one micro-batch no expert is named more than 3 times, a bound that some such block reaches.
All inputs are finite; a program needn't handle non-finite values.
Results may differ from a plain program's by a relative error of at most 0.0056.
Values may be sent and summed in bfloat16 or wider, within the bound.
No kernel may reach another device: no remote copies, remote signals or barrier semaphores. Data moves between devices by JAX's collectives and lax.ppermute only.
A program may use at most 128 MiB of HBM per device.

v0:
```python
import math

import jax
import jax.numpy as jnp
from jax import lax
from jax.sharding import PartitionSpec as P

HD = 128


def attend_local(query, key_cache, value_cache, lengths):
    requests = query.shape[0]
    kv_local = key_cache.shape[-1] // HD
    group_size = query.shape[-1] // key_cache.shape[-1]
    cache_len = key_cache.shape[1]
    queries = query.reshape(requests, kv_local, group_size, HD)
    keys_all = key_cache.reshape(requests, cache_len, kv_local, HD)
    values_all = value_cache.reshape(requests, cache_len, kv_local, HD)
    scores = jnp.einsum(
        "rkgd,rtkd->rkgt", queries, keys_all, preferred_element_type=jnp.float32
    ) * (1.0 / math.sqrt(HD))
    live_mask = (jnp.arange(cache_len, dtype=jnp.int32)[None, :] < lengths[:, None])[
        :, None, None, :
    ]
    scores = jnp.where(live_mask, scores, -jnp.inf)
    peak_score = jnp.max(scores, axis=-1, keepdims=True)
    weights_exp = jnp.where(live_mask, jnp.exp(scores - peak_score), 0.0)
    total_weight = jnp.sum(weights_exp, axis=-1, keepdims=True)
    mixed_heads = (
        jnp.einsum(
            "rkgt,rtkd->rkgd",
            weights_exp.astype(jnp.bfloat16),
            values_all,
            preferred_element_type=jnp.float32,
        )
        / total_weight
    )
    return mixed_heads.reshape(requests, -1)


def on_device(
    query, key_cache, value_cache, lengths, residual, router, routes, w_gate, w_up, w_down
):
    devices = lax.axis_size("devs")
    experts = router.shape[1]
    owners = devices // experts
    requests = routes.shape[1]
    capacity = max(2, 3 * requests // 4)
    width_half = residual.shape[-1]
    width_full = 2 * width_half
    slot_index = jnp.arange(capacity, dtype=jnp.int32)
    expert_index = jnp.arange(experts, dtype=jnp.int32)
    outputs = []
    for batch_index in range(query.shape[0]):
        attended = attend_local(
            query[batch_index],
            key_cache[batch_index],
            value_cache[batch_index],
            lengths[batch_index],
        )
        hidden = (residual[batch_index].astype(jnp.float32) + attended).astype(jnp.bfloat16)
        hidden_wide = hidden.astype(jnp.float32)
        squares, partial_logits = lax.psum(
            (
                jnp.sum(hidden_wide * hidden_wide, axis=-1),
                jnp.dot(hidden, router, preferred_element_type=jnp.float32),
            ),
            "pair",
        )
        inv_rms = lax.rsqrt(squares / width_full + 1e-05)[:, None]
        normed = (hidden_wide * inv_rms).astype(jnp.bfloat16)
        logits = partial_logits * inv_rms
        chosen = routes[batch_index]
        onehot = (chosen.reshape(-1)[:, None] == expert_index[None, :]).astype(jnp.int32)
        rank_before = jnp.cumsum(onehot, axis=0) - onehot
        slot_of = jnp.sum(rank_before * onehot, axis=1)
        placed = onehot.T[:, None, :] * (
            slot_of[None, None, :] == slot_index[None, :, None]
        ).astype(jnp.int32)
        placed = placed.reshape(experts, capacity, requests, 2)
        route_logit = jnp.sum(
            onehot.reshape(requests, 2, experts).astype(jnp.float32) * logits[:, None, :], axis=-1
        )
        gate_values = jax.nn.sigmoid(route_logit - route_logit[:, ::-1])
        picker = jnp.sum(placed, axis=-1).astype(jnp.bfloat16)
        weighted = jnp.sum(placed.astype(jnp.float32) * gate_values[None, None], axis=-1)
        full_rows = lax.all_gather(normed, "pair", axis=1, tiled=True)
        blocks = jnp.einsum(
            "ecr,rd->ecd", picker, full_rows, preferred_element_type=jnp.float32
        ).astype(jnp.bfloat16)
        outgoing = jnp.broadcast_to(
            blocks[:, None], (experts, owners, capacity, width_full)
        ).reshape(devices, capacity, width_full)
        arrived = lax.all_to_all(outgoing, "devs", split_axis=0, concat_axis=0, tiled=True)
        flat_rows = arrived.reshape(-1, arrived.shape[-1])
        gate_proj = jnp.dot(flat_rows, w_gate, preferred_element_type=jnp.float32)
        up_proj = jnp.dot(flat_rows, w_up, preferred_element_type=jnp.float32)
        hidden_units = (jax.nn.silu(gate_proj) * up_proj).astype(jnp.bfloat16)
        produced = jnp.dot(hidden_units, w_down, preferred_element_type=jnp.float32)
        partial_value = produced.reshape(arrived.shape[0], arrived.shape[1], -1)
        returned = lax.all_to_all(
            lax.all_to_all(
                partial_value.astype(jnp.bfloat16), "devs", split_axis=0, concat_axis=0, tiled=True
            ),
            "pair",
            split_axis=2,
            concat_axis=1,
            tiled=True,
        ).astype(partial_value.dtype)
        summed = jnp.sum(returned.reshape(experts, owners, 2, capacity, width_half), axis=(1, 2))
        contrib = jnp.einsum("ecr,ecd->rd", weighted, summed, precision=lax.Precision.HIGHEST)
        outputs.append((hidden_wide + contrib).astype(jnp.bfloat16))
    return jnp.stack(outputs)


def solution(mesh):
    in_specs = (
        P(None, ("groups", "devs"), "pair"),
        P(None, ("groups", "devs"), None, "pair"),
        P(None, ("groups", "devs"), None, "pair"),
        P(None, ("groups", "devs")),
        P(None, ("groups", "devs"), "pair"),
        P("pair", None),
        P(None, ("groups", "devs"), None),
        P(None, ("devs", "pair")),
        P(None, ("devs", "pair")),
        P(("devs", "pair"), None),
    )
    out_specs = P(None, ("groups", "devs"), "pair")
    return jax.shard_map(
        on_device, mesh=mesh, in_specs=in_specs, out_specs=out_specs, check_vma=False
    )
```

profile of v0, /device:TPU:0, one launch (start us, length us, event | category | flops | bytes accessed | tf_op | source)
XLA Modules:
  0.0 121.5 jit_solution(11169553519349990576)
XLA Ops:
  1.5 1.3 %fusion.50 = (bf16[1,4,256,256]{3,2,1,0:T(8,128)(2,1)S(1)}, bf16[1,4,256,256]{3,2,1,0:T(8,128)(2,1)S(1)}) fusion(bf16[2,4,256,256]{3,2,1,0:T(8,128)(2,1)} %param.11), kind=kLoop, calls=%fused_computation.101 | loop fusion | bytes 2097152 | tf_op jit(solution)/shard_map/slice | solution.py:57
  4.2 1.3 %fusion.51 = (bf16[1,4,256,256]{3,2,1,0:T(8,128)(2,1)S(1)}, bf16[1,4,256,256]{3,2,1,0:T(8,128)(2,1)S(1)}) fusion(bf16[2,4,256,256]{3,2,1,0:T(8,128)(2,1)} %param.12), kind=kLoop, calls=%fused_computation.102 | loop fusion | bytes 2097152 | tf_op jit(solution)/shard_map/slice | solution.py:58
  8.4 2.6 %all-reduce = (f32[4]{0:T(128)S(1)}, f32[4]{0:T(128)S(1)}, f32[4,4]{1,0:T(4,128)S(1)}, f32[4,4]{1,0:T(4,128)S(1)}) all-reduce(f32[4]{0:T(128)S(1)} %get-tuple-element.25, f32[4]{0:T(128)S(1)} %get-tuple-element.27, f32[4,4]{1,0:T(4,128)S(1)} %fusion.58, f32[4,4]{1,0:T(4,128)S(1)} %fusion.56), channel_id=1, replica_groups=mesh['groups'=2,'devs'=8,'pair'=2] {'pair'}, use_global_device_ids=true, to_apply=%region_6.7 | all-reduce | flops 40 | bytes 320 | tf_op jit(solution)/shard_map/psum | solution.py:63
  12.3 1.8 %all_gather.7 = bf16[4,3072]{1,0:T(4,128)(2,1)S(1)} all-gather(bf16[4,1536]{1,0:T(4,128)(2,1)S(1)} %fusion.33), channel_id=1, replica_groups=mesh['groups'=2,'devs'=8,'pair'=2] {'pair'}, dimensions={1}, use_global_device_ids=true | all-gather | bytes 36864 | tf_op jit(solution)/shard_map/all_gather | solution.py:87
  15.1 7.1 %all-to-all-start.3 = ((bf16[8,3,3072]{2,1,0:T(4,128)(2,1)}), bf16[8,3,3072]{2,1,0:T(4,128)(2,1)S(1)}, u32[]{:S(2)}, u32[]{:S(2)}) async-start(bf16[8,3,3072]{2,1,0:T(4,128)(2,1)} %bitcast.15), calls=%async_computation.3 | async-start | bytes 393216 | tf_op jit(solution)/shard_map/all_to_all | solution.py:94
  23.2 1.8 %all_gather.6 = bf16[4,3072]{1,0:T(4,128)(2,1)S(1)} all-gather(bf16[4,1536]{1,0:T(4,128)(2,1)S(1)} %fusion.32), channel_id=1, replica_groups=mesh['groups'=2,'devs'=8,'pair'=2] {'pair'}, dimensions={1}, use_global_device_ids=true | all-gather | bytes 36864 | tf_op jit(solution)/shard_map/all_gather | solution.py:87
  25.5 5.0 %all-to-all-done.3 = bf16[8,3,3072]{2,1,0:T(4,128)(2,1)S(1)} async-done(((bf16[8,3,3072]{2,1,0:T(4,128)(2,1)}), bf16[8,3,3072]{2,1,0:T(4,128)(2,1)S(1)}, u32[]{:S(2)}, u32[]{:S(2)}) %all-to-all-start.3) | async-done | bytes 147488 | tf_op jit(solution)/shard_map/all_to_all | solution.py:94
  31.3 3.4 %all-to-all-start = ((bf16[8,3,3072]{2,1,0:T(4,128)(2,1)}), bf16[8,3,3072]{2,1,0:T(4,128)(2,1)S(1)}, u32[]{:S(2)}, u32[]{:S(2)}) async-start(bf16[8,3,3072]{2,1,0:T(4,128)(2,1)} %bitcast.6), calls=%async_computation | async-start | bytes 393216 | tf_op jit(solution)/shard_map/all_to_all | solution.py:94
  34.8 6.3 %fusion.59 = f32[24,2048]{1,0:T(8,128)S(1)} fusion(bf16[24,3072]{1,0:T(8,128)(2,1)S(1)} %reshape.227, bf16[3072,2048]{1,0:T(8,128)(2,1)} %param.17), kind=kOutput, calls=%fused_computation.110 | convolution fusion | flops 301989888 | bytes 12926976 | tf_op jit(solution)/shard_map/dot_general | solution.py:96
  41.1 11.6 %convolution_convert_fusion = bf16[24,3072]{1,0:T(8,128)(2,1)S(1)} fusion(bf16[2048,3072]{1,0:T(8,128)(2,1)} %param.19, bf16[24,3072]{1,0:T(8,128)(2,1)S(1)} %reshape.227, bf16[3072,2048]{1,0:T(8,128)(2,1)} %param.18, f32[24,2048]{1,0:T(8,128)S(1)} %fusion.59), kind=kOutput, calls=%fused_computation.2 | convolution fusion | flops 604348416 | bytes 25657344 | tf_op jit(solution)/shard_map/dot_general | solution.py:99
  53.5 5.9 %all-to-all-start.4 = ((bf16[8,3,3072]{2,1,0:T(4,128)(2,1)}), bf16[8,3,3072]{2,1,0:T(4,128)(2,1)S(1)}, u32[]{:S(2)}, u32[]{:S(2)}) async-start(bf16[8,3,3072]{2,1,0:T(4,128)(2,1)} %convert_element_type.212), calls=%async_computation.4 | async-start | bytes 393216 | tf_op jit(solution)/shard_map/all_to_all | solution.py:102
  59.5 6.3 %fusion.57 = f32[24,2048]{1,0:T(8,128)S(1)} fusion(bf16[24,3072]{1,0:T(8,128)(2,1)S(1)} %reshape.224, bf16[3072,2048]{1,0:T(8,128)(2,1)} %param.17), kind=kOutput, calls=%fused_computation.108 | convolution fusion | flops 301989888 | bytes 12926976 | tf_op jit(solution)/shard_map/dot_general | solution.py:96
  65.8 11.6 %convolution_convert_fusion.1 = bf16[24,3072]{1,0:T(8,128)(2,1)S(1)} fusion(bf16[2048,3072]{1,0:T(8,128)(2,1)} %param.19, bf16[24,3072]{1,0:T(8,128)(2,1)S(1)} %reshape.224, bf16[3072,2048]{1,0:T(8,128)(2,1)} %param.18, f32[24,2048]{1,0:T(8,128)S(1)} %fusion.57), kind=kOutput, calls=%fused_computation.3 | convolution fusion | flops 604348416 | bytes 25657344 | tf_op jit(solution)/shard_map/dot_general | solution.py:99
  78.2 3.1 %copy.114 = bf16[8,3,3072]{0,1,2:T(4,128)(2,1)S(1)} copy(bf16[8,3,3072]{2,1,0:T(4,128)(2,1)S(1)} %all-to-all-done.4) | data formatting | bytes 294912 | tf_op jit(solution)/shard_map/all_to_all | solution.py:102
  81.3 2.9 %reshape.240 = bf16[2,2,18432]{2,1,0:T(2,128)(2,1)S(1)} reshape(bf16[3072,3,8]{2,1,0:T(4,128)(2,1)S(1)} %bitcast.88) | data formatting | bytes 294912
  84.3 3.8 %all_to_all.38 = bf16[2,2,18432]{2,1,0:T(2,128)(2,1)S(1)} all-to-all(bf16[2,2,18432]{2,1,0:T(2,128)(2,1)S(1)} %reshape.240), channel_id=1, replica_groups=mesh['groups'=2,'devs'=8,'pair'=2] {'pair'}, dimensions={0} | all-to-all | bytes 294912 | tf_op jit(solution)/shard_map/all_to_all | solution.py:101
  88.1 6.0 %all-to-all-start.1 = ((bf16[8,3,3072]{2,1,0:T(4,128)(2,1)}), bf16[8,3,3072]{2,1,0:T(4,128)(2,1)S(1)}, u32[]{:S(2)}, u32[]{:S(2)}) async-start(bf16[8,3,3072]{2,1,0:T(4,128)(2,1)} %convert_element_type.188), calls=%async_computation.1 | async-start | bytes 393216 | tf_op jit(solution)/shard_map/all_to_all | solution.py:102
  95.3 3.0 %reshape.241 = bf16[3072,3,8]{2,1,0:T(4,128)(2,1)S(1)} reshape(bf16[2,2,18432]{2,1,0:T(2,128)(2,1)S(1)} %all_to_all.38) | data formatting | bytes 294912
  98.3 2.8 %copy.115 = bf16[8,3,3072]{2,0,1:T(8,128)(2,1)S(1)} copy(bf16[8,3,3072]{0,1,2:T(4,128)(2,1)S(1)} %bitcast.89) | data formatting | bytes 294912 | tf_op jit(solution)/shard_map/all_to_all | solution.py:101
  102.4 3.1 %copy.104 = bf16[8,3,3072]{0,1,2:T(4,128)(2,1)S(1)} copy(bf16[8,3,3072]{2,1,0:T(4,128)(2,1)S(1)} %all-to-all-done.1) | data formatting | bytes 294912 | tf_op jit(solution)/shard_map/all_to_all | solution.py:102
  105.5 2.9 %reshape.238 = bf16[2,2,18432]{2,1,0:T(2,128)(2,1)S(1)} reshape(bf16[3072,3,8]{2,1,0:T(4,128)(2,1)S(1)} %bitcast.90) | data formatting | bytes 294912
  108.4 3.8 %all_to_all.39 = bf16[2,2,18432]{2,1,0:T(2,128)(2,1)S(1)} all-to-all(bf16[2,2,18432]{2,1,0:T(2,128)(2,1)S(1)} %reshape.238), channel_id=1, replica_groups=mesh['groups'=2,'devs'=8,'pair'=2] {'pair'}, dimensions={0} | all-to-all | bytes 294912 | tf_op jit(solution)/shard_map/all_to_all | solution.py:101
  112.2 3.0 %reshape.239 = bf16[3072,3,8]{2,1,0:T(4,128)(2,1)S(1)} reshape(bf16[2,2,18432]{2,1,0:T(2,128)(2,1)S(1)} %all_to_all.39) | data formatting | bytes 294912
  115.2 2.8 %copy.105 = bf16[8,3,3072]{2,0,1:T(8,128)(2,1)S(1)} copy(bf16[8,3,3072]{0,1,2:T(4,128)(2,1)S(1)} %bitcast.91) | data formatting | bytes 294912 | tf_op jit(solution)/shard_map/all_to_all | solution.py:101
  (84 shorter events, 18.0 us)
Async XLA Ops:
  0.0 8.1 %copy-start = (bf16[1536,4]{0,1:T(4,128)(2,1)S(1)}, bf16[1536,4]{0,1:T(4,128)(2,1)}, u32[]{:S(2)}) copy-start(bf16[1536,4]{0,1:T(4,128)(2,1)} %param.15) | copy-start | bytes 36868
  15.1 15.4 %all-to-all-start.3 = ((bf16[8,3,3072]{2,1,0:T(4,128)(2,1)}), bf16[8,3,3072]{2,1,0:T(4,128)(2,1)S(1)}, u32[]{:S(2)}, u32[]{:S(2)}) async-start(bf16[8,3,3072]{2,1,0:T(4,128)(2,1)} %bitcast.15), calls=%async_computation.3 | async-start | bytes 393216 | tf_op jit(solution)/shard_map/all_to_all | solution.py:94
  31.3 22.2 %all-to-all-start = ((bf16[8,3,3072]{2,1,0:T(4,128)(2,1)}), bf16[8,3,3072]{2,1,0:T(4,128)(2,1)S(1)}, u32[]{:S(2)}, u32[]{:S(2)}) async-start(bf16[8,3,3072]{2,1,0:T(4,128)(2,1)} %bitcast.6), calls=%async_computation | async-start | bytes 393216 | tf_op jit(solution)/shard_map/all_to_all | solution.py:94
  53.5 24.7 %all-to-all-start.4 = ((bf16[8,3,3072]{2,1,0:T(4,128)(2,1)}), bf16[8,3,3072]{2,1,0:T(4,128)(2,1)S(1)}, u32[]{:S(2)}, u32[]{:S(2)}) async-start(bf16[8,3,3072]{2,1,0:T(4,128)(2,1)} %convert_element_type.212), calls=%async_computation.4 | async-start | bytes 393216 | tf_op jit(solution)/shard_map/all_to_all | solution.py:102
  88.1 14.3 %all-to-all-start.1 = ((bf16[8,3,3072]{2,1,0:T(4,128)(2,1)}), bf16[8,3,3072]{2,1,0:T(4,128)(2,1)S(1)}, u32[]{:S(2)}, u32[]{:S(2)}) async-start(bf16[8,3,3072]{2,1,0:T(4,128)(2,1)} %convert_element_type.188), calls=%async_computation.1 | async-start | bytes 393216 | tf_op jit(solution)/shard_map/all_to_all | solution.py:102
where the time goes:
time: 123 us; the launch traced here: 122 us
  matrix products  39.4 us (32%)
  local copies, waits for them, and re-layouts  34.2 us (28%)
  starting transfers between devices  22.4 us (18%)
  blocking collectives  13.9 us (11%)
  other arithmetic  6.01 us (5%)
  waiting for transfers between devices  5.36 us (4%)
    dot_general x2, matrix products, on_device(): produced = jnp.dot(hidden_units, w_down, preferred_element_type=jnp.float32)  23.1 us
    unnamed x10, local copies, waits for them, and re-layouts  12.7 us
    dot_general x2, matrix products, on_device(): gate_proj = jnp.dot(flat_rows, w_gate, preferred_element_type=jnp.float32)  12.6 us
    all_to_all x2, starting transfers between devices, on_device(): lax.all_to_all(partial_value.astype(jnp.bfloat16), 'devs', split_axis=0,...  11.9 us
    all_to_all x2, starting transfers between devices, on_device(): lax.all_to_all(outgoing, 'devs', split_axis=0, concat_axis=0, tiled=True)  10.5 us
    all_to_all x2, blocking collectives, on_device(): lax.all_to_all(lax.all_to_all(partial_value.astype(jnp.bfloat16), 'devs',...  7.65 us
    all_to_all x2, local copies, waits for them, and re-layouts, on_device(): lax.all_to_all(partial_value.astype(jnp.bfloat16), 'devs', split_axis=0,...  6.21 us
    all_to_all x2, local copies, waits for them, and re-layouts, on_device(): lax.all_to_all(lax.all_to_all(partial_value.astype(jnp.bfloat16), 'devs',...  5.52 us
  transfers between devices with their start and end apart: 4, of which 2 were waited for; matrix products, arithmetic and copies ran while one was open for 39% of the time, Pallas kernels for 0%

commit v1 on v0

v1 whole, which is shorter than its diff:
```python
import functools
import math

import jax
import jax.numpy as jnp
from jax import lax
from jax.experimental import pallas as pl
from jax.experimental.pallas import tpu as pltpu
from jax.sharding import PartitionSpec as P

HD = 128
LANES = 128


def attend_kernel(
    query_ref, key_ref, value_ref, lengths_ref, residual_ref, router_ref, outgoing_ref, meta_ref
):
    batches, per_batch, width = query_ref.shape
    rows = batches * per_batch
    cache_len = key_ref.shape[2]
    kv_local = key_ref.shape[3] // HD
    group = width // key_ref.shape[3]

    def stacked(ref):
        return jnp.concatenate([ref[b].astype(jnp.float32) for b in range(batches)], axis=0)

    queries = stacked(query_ref)
    residual = stacked(residual_ref)
    tall = group * rows
    row_of = lax.rem(lax.broadcasted_iota(jnp.int32, (tall, 1), 0), rows)
    position = lax.broadcasted_iota(jnp.int32, (tall, cache_len), 1)
    limit = jnp.zeros((tall, 1), jnp.int32)
    for r in range(rows):
        limit = jnp.where(row_of == r, lengths_ref[r // per_batch, r % per_batch], limit)
    live = position < limit
    pieces = []
    for k in range(kv_local):
        heads = jnp.concatenate(
            [queries[:, (k * group + j) * HD : (k * group + j + 1) * HD] for j in range(group)],
            axis=0,
        ).astype(jnp.bfloat16)
        columns = slice(k * HD, (k + 1) * HD)
        scores = jnp.zeros((tall, cache_len), jnp.float32)
        for r in range(rows):
            keys = key_ref[r // per_batch, r % per_batch, :, columns]
            part = lax.dot_general(
                heads, keys, (((1,), (1,)), ((), ())), preferred_element_type=jnp.float32
            )
            scores = jnp.where(row_of == r, part, scores)
        scores = jnp.where(live, scores * (1.0 / math.sqrt(HD)), -jnp.inf)
        peak = jnp.max(scores, axis=-1, keepdims=True)
        weights = jnp.where(live, jnp.exp(scores - peak), 0.0)
        total = jnp.sum(weights, axis=-1, keepdims=True)
        weights_bf = weights.astype(jnp.bfloat16)
        mixed = jnp.zeros((tall, HD), jnp.float32)
        for r in range(rows):
            values = value_ref[r // per_batch, r % per_batch, :, columns]
            part = jnp.dot(weights_bf, values, preferred_element_type=jnp.float32)
            mixed = jnp.where(row_of == r, part, mixed)
        mixed = mixed / total
        pieces += [mixed[j * rows : (j + 1) * rows] for j in range(group)]
    attended = jnp.concatenate(pieces, axis=1)
    hidden = (residual + attended).astype(jnp.bfloat16)
    wide = hidden.astype(jnp.float32)
    logits = jnp.dot(hidden, router_ref[...], preferred_element_type=jnp.float32)
    squares = jnp.sum(wide * wide, axis=-1, keepdims=True)
    experts = router_ref.shape[1]
    meta_ref[...] = jnp.zeros_like(meta_ref)
    meta_ref[:, :experts] = logits
    meta_ref[:, experts : experts + 1] = squares
    for d in range(outgoing_ref.shape[0]):
        outgoing_ref[d] = hidden


def expert_kernel(
    side_ref, own_ref, other_ref, gate_ref, up_ref, down_ref, kept_ref, sent_ref, normed, total
):
    step = pl.program_id(0)
    half = own_ref.shape[-1]
    side = side_ref[0]
    own_columns = pl.ds(pl.multiple_of(side * half, LANES), half)
    other_columns = pl.ds(pl.multiple_of((1 - side) * half, LANES), half)
    count = normed.shape[0]

    @pl.when(step == 0)
    def _():
        own = own_ref[...].astype(jnp.float32).reshape(count, half)
        other = other_ref[...].astype(jnp.float32).reshape(count, half)
        squares = jnp.sum(own * own, axis=-1, keepdims=True) + jnp.sum(
            other * other, axis=-1, keepdims=True
        )
        inv_rms = lax.rsqrt(squares / (2 * half) + 1e-05)
        normed[:, own_columns] = (own * inv_rms).astype(jnp.bfloat16)
        normed[:, other_columns] = (other * inv_rms).astype(jnp.bfloat16)
        total[...] = jnp.zeros_like(total)

    rows = normed[...]
    gate = jnp.dot(rows, gate_ref[...], preferred_element_type=jnp.float32)
    up = jnp.dot(rows, up_ref[...], preferred_element_type=jnp.float32)
    units = (jax.nn.silu(gate) * up).astype(jnp.bfloat16)
    total[...] += jnp.dot(units, down_ref[...], preferred_element_type=jnp.float32)

    @pl.when(step == pl.num_programs(0) - 1)
    def _():
        kept_ref[...] = total[:, own_columns].reshape(kept_ref.shape)
        sent_ref[...] = total[:, other_columns].reshape(sent_ref.shape).astype(jnp.bfloat16)


def combine_kernel(
    experts, returned_ref, outgoing_ref, meta_ref, meta_other_ref, routes_ref, out_ref
):
    devices, rows, half = returned_ref.shape
    batches, per_batch, _ = out_ref.shape
    owners = devices // experts
    meta = meta_ref[...] + meta_other_ref[...]
    squares = meta[:, experts : experts + 1]
    inv_rms = lax.rsqrt(squares / (2 * half) + 1e-05)
    logits = meta * inv_rms
    chosen = jnp.concatenate([routes_ref[b] for b in range(batches)], axis=0)
    lane = lax.broadcasted_iota(jnp.int32, (rows, LANES), 1)
    first, second = chosen[:, 0:1], chosen[:, 1:2]
    logit_first = jnp.sum(jnp.where(lane == first, logits, 0.0), axis=-1, keepdims=True)
    logit_second = jnp.sum(jnp.where(lane == second, logits, 0.0), axis=-1, keepdims=True)
    gate_first = jax.nn.sigmoid(logit_first - logit_second)
    gate_second = jax.nn.sigmoid(logit_second - logit_first)
    result = outgoing_ref[0].astype(jnp.float32)
    for e in range(experts):
        expert_out = returned_ref[e * owners].astype(jnp.float32)
        for o in range(1, owners):
            expert_out += returned_ref[e * owners + o].astype(jnp.float32)
        weight = jnp.where(first == e, gate_first, 0.0) + jnp.where(second == e, gate_second, 0.0)
        result += weight * expert_out
    for b in range(batches):
        out_ref[b] = result[b * per_batch : (b + 1) * per_batch].astype(jnp.bfloat16)


VMEM = pl.BlockSpec(memory_space=pltpu.VMEM)
SMEM = pl.BlockSpec(memory_space=pltpu.SMEM)


def swap_cores(value):
    return lax.ppermute(value, "pair", [(0, 1), (1, 0)])


def on_device(
    query, key_cache, value_cache, lengths, residual, router, routes, w_gate, w_up, w_down
):
    devices = lax.axis_size("devs")
    experts = router.shape[1]
    batches, per_batch, half = query.shape
    rows = batches * per_batch
    outgoing, meta = pl.pallas_call(
        attend_kernel,
        in_specs=[VMEM, VMEM, VMEM, SMEM, VMEM, VMEM],
        out_specs=[VMEM, VMEM],
        out_shape=[
            jax.ShapeDtypeStruct((devices, rows, half), jnp.bfloat16),
            jax.ShapeDtypeStruct((rows, LANES), jnp.float32),
        ],
        compiler_params=pltpu.CompilerParams(vmem_limit_bytes=16 << 20),
    )(query, key_cache, value_cache, lengths, residual, router)
    meta_other = swap_cores(meta)
    arrived = lax.all_to_all(outgoing, "devs", split_axis=0, concat_axis=0, tiled=True)
    arrived_other = swap_cores(arrived)

    units = w_gate.shape[1]
    block = min(512, units)
    whole = pl.BlockSpec(arrived.shape, lambda i, side: (0, 0, 0))
    kept, sent = pl.pallas_call(
        expert_kernel,
        grid_spec=pltpu.PrefetchScalarGridSpec(
            num_scalar_prefetch=1,
            grid=(units // block,),
            in_specs=[
                whole,
                whole,
                pl.BlockSpec((2 * half, block), lambda i, side: (0, i)),
                pl.BlockSpec((2 * half, block), lambda i, side: (0, i)),
                pl.BlockSpec((block, 2 * half), lambda i, side: (i, 0)),
            ],
            out_specs=[whole, whole],
            scratch_shapes=[
                pltpu.VMEM((devices * rows, 2 * half), jnp.bfloat16),
                pltpu.VMEM((devices * rows, 2 * half), jnp.float32),
            ],
        ),
        out_shape=[
            jax.ShapeDtypeStruct(arrived.shape, jnp.float32),
            jax.ShapeDtypeStruct(arrived.shape, jnp.bfloat16),
        ],
        compiler_params=pltpu.CompilerParams(vmem_limit_bytes=50 << 20),
    )(
        lax.axis_index("pair").astype(jnp.int32).reshape(1),
        arrived,
        arrived_other,
        w_gate,
        w_up,
        w_down,
    )
    received = swap_cores(sent)
    summed = (kept + received.astype(jnp.float32)).astype(jnp.bfloat16)
    returned = lax.all_to_all(summed, "devs", split_axis=0, concat_axis=0, tiled=True)
    return pl.pallas_call(
        functools.partial(combine_kernel, experts),
        in_specs=[VMEM] * 5,
        out_specs=VMEM,
        out_shape=jax.ShapeDtypeStruct(query.shape, jnp.bfloat16),
        compiler_params=pltpu.CompilerParams(vmem_limit_bytes=16 << 20),
    )(returned, outgoing, meta, meta_other, routes)


def solution(mesh):
    in_specs = (
        P(None, ("groups", "devs"), "pair"),
        P(None, ("groups", "devs"), None, "pair"),
        P(None, ("groups", "devs"), None, "pair"),
        P(None, ("groups", "devs")),
        P(None, ("groups", "devs"), "pair"),
        P("pair", None),
        P(None, ("groups", "devs"), None),
        P(None, ("devs", "pair")),
        P(None, ("devs", "pair")),
        P(("devs", "pair"), None),
    )
    out_specs = P(None, ("groups", "devs"), "pair")
    return jax.shard_map(
        on_device, mesh=mesh, in_specs=in_specs, out_specs=out_specs, check_vma=False
    )
```

time: 123 us -> 53.7 us (0.44)
  matrix products: 39.4 us -> 0 us
  local copies, waits for them, and re-layouts: 34.2 us -> 5.69 us
  starting transfers between devices: 22.4 us -> 3.8 us
  Pallas kernels: 0 us -> 17 us
  waiting for transfers between devices: 5.36 us -> 10.9 us
  other arithmetic: 6.01 us -> 0.71 us
    dot_general x14 -> x0, matrix products: 39.4 us -> none  [the longest x2 23.1 us: on_device(): produced = jnp.dot(hidden_units, w_down, preferred_element_type=jnp.float32)]
    all_to_all x4 -> x1, starting transfers between devices: 22.4 us -> 3.39 us  [on_device(): lax.all_to_all(summed, 'devs', split_axis=0, concat_axis=0, tiled=True)]
    pallas_call x0 -> x3, Pallas kernels: none -> 17 us  [the longest x1 14.4 us: on_device(): pl.pallas_call(expert_kernel, grid_spec=pltpu.PrefetchScalarGridSpec(num_...]
    all_to_all x4 -> x0, local copies, waits for them, and re-layouts: 11.7 us -> none  [the longest x2 6.21 us: on_device(): lax.all_to_all(partial_value.astype(jnp.bfloat16), 'devs', split_axis=0,...]
    all_to_all x2 -> x1, blocking collectives: 7.65 us -> 15 us  [on_device(): lax.all_to_all(outgoing, 'devs', split_axis=0, concat_axis=0, tiled=True)]
    unnamed x10 -> x14, local copies, waits for them, and re-layouts: 12.7 us -> 5.69 us
    slice x6 -> x0, local copies, waits for them, and re-layouts: 4.17 us -> none  [the longest x1 1.27 us: on_device(): key_cache[batch_index]]
    ppermute x0 -> x3, waiting for transfers between devices: none -> 3.67 us  [swap_cores(): return lax.ppermute(value, 'pair', [(0, 1), (1, 0)])]
  transfers between devices with their start and end apart: 4 -> 4, of which waited for: 2 -> 4; matrix products, arithmetic and copies ran while one was open for 39% -> 0% of each run, Pallas kernels for 0% -> 0%
where the time goes in v1:
time: 53.7 us; the launch traced here: 53.2 us
  Pallas kernels  17 us (32%)
  blocking collectives  15 us (28%)
  waiting for transfers between devices  10.9 us (20%)
  local copies, waits for them, and re-layouts  5.69 us (11%)
  starting transfers between devices  3.8 us (7%)
  other arithmetic  0.71 us (1%)
    all_to_all x1, blocking collectives, on_device(): lax.all_to_all(outgoing, 'devs', split_axis=0, concat_axis=0, tiled=True)  15 us
    pallas_call x1, Pallas kernels, on_device(): pl.pallas_call(expert_kernel, grid_spec=pltpu.PrefetchScalarGridSpec(num_...  14.4 us
    all_to_all x1, waiting for transfers between devices, on_device(): lax.all_to_all(summed, 'devs', split_axis=0, concat_axis=0, tiled=True)  7.24 us
    unnamed x14, local copies, waits for them, and re-layouts  5.69 us
    ppermute x3, waiting for transfers between devices, swap_cores(): return lax.ppermute(value, 'pair', [(0, 1), (1, 0)])  3.67 us
    all_to_all x1, starting transfers between devices, on_device(): lax.all_to_all(summed, 'devs', split_axis=0, concat_axis=0, tiled=True)  3.39 us
    pallas_call x1, Pallas kernels, on_device(): pl.pallas_call(attend_kernel, in_specs=[VMEM, VMEM, VMEM, SMEM, VMEM, VME...  1.65 us
  transfers between devices with their start and end apart: 4, of which 4 were waited for; matrix products, arithmetic and copies ran while one was open for 0% of the time, Pallas kernels for 0%

profile of v1, /device:TPU:0, one launch (start us, length us, event | category | flops | bytes accessed | tf_op | source)
XLA Modules:
  0.0 53.2 jit_solution(10565150924862687355)
XLA Ops:
  0.0 1.0 %copy.11.router_ref = bf16[1536,4]{1,0:T(8,128)(2,1)S(1)} copy(bf16[1536,4]{0,1:T(4,128)(2,1)} %param.15) | data formatting | bytes 24576 | tf_op args[5]
  1.0 0.0 copy-start
  1.0 1.2 %copy-done = bf16[2,4,256,256]{3,2,1,0:T(8,128)(2,1)S(1)} copy-done((bf16[2,4,256,256]{3,2,1,0:T(8,128)(2,1)S(1)}, bf16[2,4,256,256]{3,2,1,0:T(8,128)(2,1)}, u32[]{:S(2)}) %copy-start) | copy-done | bytes 1048600
  2.2 0.0 copy-start.1
  2.2 1.2 %copy-done.1 = bf16[2,4,256,256]{3,2,1,0:T(8,128)(2,1)S(1)} copy-done((bf16[2,4,256,256]{3,2,1,0:T(8,128)(2,1)S(1)}, bf16[2,4,256,256]{3,2,1,0:T(8,128)(2,1)}, u32[]{:S(2)}) %copy-start.1) | copy-done | bytes 1048600
  3.5 0.0 copy-start.2
  3.5 0.7 %copy-done.2 = bf16[2,4,1536]{2,1,0:T(4,128)(2,1)S(1)} copy-done((bf16[2,4,1536]{2,1,0:T(4,128)(2,1)S(1)}, bf16[2,4,1536]{2,1,0:T(4,128)(2,1)}, u32[]{:S(2)}) %copy-start.2) | copy-done | bytes 24600
  4.2 0.7 %copy-done.3 = bf16[2,4,1536]{2,1,0:T(4,128)(2,1)S(1)} copy-done((bf16[2,4,1536]{2,1,0:T(4,128)(2,1)S(1)}, bf16[2,4,1536]{2,1,0:T(4,128)(2,1)}, u32[]{:S(2)}) %copy-start.3) | copy-done | bytes 24600
  4.9 0.7 %copy-done.4 = s32[2,4]{1,0:T(2,128)S(1)} copy-done((s32[2,4]{1,0:T(2,128)S(1)}, s32[2,4]{1,0:T(2,128)}, u32[]{:S(2)}) %copy-start.4) | copy-done | bytes 56
  5.6 1.6 %shard_map.100 = (bf16[8,8,1536]{2,1,0:T(8,128)(2,1)S(1)}, f32[8,128]{1,0:T(8,128)S(1)}) custom-call(bf16[2,4,1536]{2,1,0:T(4,128)(2,1)S(1)} %copy-done.2, bf16[2,4,256,256]{3,2,1,0:T(8,128)(2,1)S(1)} %copy-done, bf16[2,4,256,256]{3,2,1,0:T(8,128)(2,1)S(1)} %copy-done.1, s32[2,4]{1,0:T(2,128)S(1)} %copy-done.4, bf16[2,4,1536]{2,1,0:T(4,128)(2,1)S(1)} %copy-done.3, ...), custom_call_target="tpu_custom_call" | custom-call | tf_op jit(solution)/shard_map/pallas_call | solution.py:152
  7.3 15.0 %all_to_all.10.own_ref = bf16[8,8,1536]{2,1,0:T(8,128)(2,1)S(1)} all-to-all(bf16[8,8,1536]{2,1,0:T(8,128)(2,1)S(1)} %get-tuple-element.9.outgoing_ref), channel_id=1, replica_groups=mesh['groups'=2,'devs'=8,'pair'=2] {'devs'}, dimensions={0} | all-to-all | bytes 393216 | tf_op jit(solution)/shard_map/all_to_all | solution.py:163
  22.3 0.0 collective-permute-start
  22.3 1.4 %collective-permute-done.other_ref = bf16[8,8,1536]{2,1,0:T(8,128)(2,1)S(1)} collective-permute-done((bf16[8,8,1536]{2,1,0:T(8,128)(2,1)S(1)}, bf16[8,8,1536]{2,1,0:T(8,128)(2,1)S(1)}, u32[]{:S(2)}, u32[]{:S(2)}) %collective-permute-start) | collective-permute-done | bytes 196640 | tf_op jit(solution)/shard_map/ppermute | solution.py:142
  23.7 14.4 %shard_map.101 = (f32[8,8,1536]{2,1,0:T(8,128)S(1)}, bf16[8,8,1536]{2,1,0:T(8,128)(2,1)S(1)}) custom-call(s32[1]{0:T(128)} %bitcast.side_ref, bf16[8,8,1536]{2,1,0:T(8,128)(2,1)S(1)} %all_to_all.10.own_ref, bf16[8,8,1536]{2,1,0:T(8,128)(2,1)S(1)} %collective-permute-done.other_ref, bf16[3072,2048]{1,0:T(8,128)(2,1)} %gate_ref.1, bf16[3072,2048]{1,0:T(8,128)(2,1)} %up_ref.1, ...), custom_call_target="tpu_custom_call" | custom-call | tf_op jit(solution)/shard_map/pallas_call | solution.py:169
  38.1 0.2 collective-permute-start.1
  38.3 1.3 %collective-permute-done.1 = bf16[8,8,1536]{2,1,0:T(8,128)(2,1)S(1)} collective-permute-done((bf16[8,8,1536]{2,1,0:T(8,128)(2,1)S(1)}, bf16[8,8,1536]{2,1,0:T(8,128)(2,1)S(1)}, u32[]{:S(2)}, u32[]{:S(2)}) %collective-permute-start.1) | collective-permute-done | bytes 196640 | tf_op jit(solution)/shard_map/ppermute | solution.py:142
  39.7 0.7 %add_convert_fusion = bf16[8,8,1536]{2,1,0:T(8,128)(2,1)} fusion(f32[8,8,1536]{2,1,0:T(8,128)S(1)} %get-tuple-element.10, bf16[8,8,1536]{2,1,0:T(8,128)(2,1)S(1)} %collective-permute-done.1), kind=kLoop, calls=%fused_computation | loop fusion | flops 294912 | bytes 786432 | tf_op jit(solution)/shard_map/convert_element_type | solution.py:201
  40.4 3.4 %all-to-all-start.1 = ((bf16[8,8,1536]{2,1,0:T(8,128)(2,1)}), bf16[8,8,1536]{2,1,0:T(8,128)(2,1)S(1)}, u32[]{:S(2)}, u32[]{:S(2)}) async-start(bf16[8,8,1536]{2,1,0:T(8,128)(2,1)} %add_convert_fusion), calls=%async_computation.1 | async-start | bytes 393216 | tf_op jit(solution)/shard_map/all_to_all | solution.py:202
  43.8 0.2 collective-permute-start.2
  44.0 0.0 copy-done.5
  44.0 0.1 copy.12.routes_ref
  44.1 0.9 %collective-permute-done.2.meta_other_ref = f32[8,128]{1,0:T(8,128)S(1)} collective-permute-done((f32[8,128]{1,0:T(8,128)S(1)}, f32[8,128]{1,0:T(8,128)S(1)}, u32[]{:S(2)}, u32[]{:S(2)}) %collective-permute-start.2) | collective-permute-done | bytes 4128 | tf_op jit(solution)/shard_map/ppermute | solution.py:142
  45.0 7.2 %all-to-all-done.1.returned_ref = bf16[8,8,1536]{2,1,0:T(8,128)(2,1)S(1)} async-done(((bf16[8,8,1536]{2,1,0:T(8,128)(2,1)}), bf16[8,8,1536]{2,1,0:T(8,128)(2,1)S(1)}, u32[]{:S(2)}, u32[]{:S(2)}) %all-to-all-start.1) | async-done | bytes 196640 | tf_op jit(solution)/shard_map/all_to_all | solution.py:202
  52.2 0.9 %shard_map.102 = bf16[2,4,1536]{2,1,0:T(4,128)(2,1)} custom-call(bf16[8,8,1536]{2,1,0:T(8,128)(2,1)S(1)} %all-to-all-done.1.returned_ref, bf16[8,8,1536]{2,1,0:T(8,128)(2,1)S(1)} %get-tuple-element.9.outgoing_ref, f32[8,128]{1,0:T(8,128)S(1)} %get-tuple-element.12.meta_ref, f32[8,128]{1,0:T(8,128)S(1)} %collective-permute-done.2.meta_other_ref, ...), custom_call_target="tpu_custom_call" | custom-call | tf_op jit(solution)/shard_map/pallas_call | solution.py:203
  (3 shorter events, 0.0 us)
Async XLA Ops:
  1.0 1.2 %copy-start = (bf16[2,4,256,256]{3,2,1,0:T(8,128)(2,1)S(1)}, bf16[2,4,256,256]{3,2,1,0:T(8,128)(2,1)}, u32[]{:S(2)}) copy-start(bf16[2,4,256,256]{3,2,1,0:T(8,128)(2,1)} %key_ref.1) | copy-start | bytes 3145732
  2.2 1.2 %copy-start.1 = (bf16[2,4,256,256]{3,2,1,0:T(8,128)(2,1)S(1)}, bf16[2,4,256,256]{3,2,1,0:T(8,128)(2,1)}, u32[]{:S(2)}) copy-start(bf16[2,4,256,256]{3,2,1,0:T(8,128)(2,1)} %value_ref.1) | copy-start | bytes 3145732
  3.5 0.7 %copy-start.2 = (bf16[2,4,1536]{2,1,0:T(4,128)(2,1)S(1)}, bf16[2,4,1536]{2,1,0:T(4,128)(2,1)}, u32[]{:S(2)}) copy-start(bf16[2,4,1536]{2,1,0:T(4,128)(2,1)} %query_ref.1) | copy-start | bytes 73732
  4.2 0.7 %copy-start.3 = (bf16[2,4,1536]{2,1,0:T(4,128)(2,1)S(1)}, bf16[2,4,1536]{2,1,0:T(4,128)(2,1)}, u32[]{:S(2)}) copy-start(bf16[2,4,1536]{2,1,0:T(4,128)(2,1)} %residual_ref.1) | copy-start | bytes 73732
  4.9 0.7 %copy-start.4 = (s32[2,4]{1,0:T(2,128)S(1)}, s32[2,4]{1,0:T(2,128)}, u32[]{:S(2)}) copy-start(s32[2,4]{1,0:T(2,128)} %lengths_ref.1) | copy-start | bytes 100
  22.3 1.4 %collective-permute-start = (bf16[8,8,1536]{2,1,0:T(8,128)(2,1)S(1)}, bf16[8,8,1536]{2,1,0:T(8,128)(2,1)S(1)}, u32[]{:S(2)}, u32[]{:S(2)}) collective-permute-start(bf16[8,8,1536]{2,1,0:T(8,128)(2,1)S(1)} %all_to_all.10.own_ref), channel_id=1, source_target_pairs={{0,1},{1,0},{2,3},{3,2},{4,5},{5,4},{6,7},{7,6},{8,9},{9,8},{10,11... | collective-permute-start | bytes 589832 | tf_op jit(solution)/shard_map/ppermute | solution.py:142
  23.7 20.2 %copy-start.5 = (s32[2,4,2]{1,2,0:T(2,128)S(1)}, s32[2,4,2]{1,2,0:T(2,128)}, u32[]{:S(2)}) copy-start(s32[2,4,2]{1,2,0:T(2,128)} %param.16) | copy-start | bytes 196
  38.1 1.5 %collective-permute-start.1 = (bf16[8,8,1536]{2,1,0:T(8,128)(2,1)S(1)}, bf16[8,8,1536]{2,1,0:T(8,128)(2,1)S(1)}, u32[]{:S(2)}, u32[]{:S(2)}) collective-permute-start(bf16[8,8,1536]{2,1,0:T(8,128)(2,1)S(1)} %get-tuple-element.11), channel_id=1, source_target_pairs={{0,1},{1,0},{2,3},{3,2},{4,5},{5,4},{6,7},{7,6},{8,9},{9,8},{10,11... | collective-permute-start | bytes 589832 | tf_op jit(solution)/shard_map/ppermute | solution.py:142
  40.4 11.9 %all-to-all-start.1 = ((bf16[8,8,1536]{2,1,0:T(8,128)(2,1)}), bf16[8,8,1536]{2,1,0:T(8,128)(2,1)S(1)}, u32[]{:S(2)}, u32[]{:S(2)}) async-start(bf16[8,8,1536]{2,1,0:T(8,128)(2,1)} %add_convert_fusion), calls=%async_computation.1 | async-start | bytes 393216 | tf_op jit(solution)/shard_map/all_to_all | solution.py:202
  43.8 1.2 %collective-permute-start.2 = (f32[8,128]{1,0:T(8,128)S(1)}, f32[8,128]{1,0:T(8,128)S(1)}, u32[]{:S(2)}, u32[]{:S(2)}) collective-permute-start(f32[8,128]{1,0:T(8,128)S(1)} %get-tuple-element.12.meta_ref), channel_id=1, source_target_pairs={{0,1},{1,0},{2,3},{3,2},{4,5},{5,4},{6,7},{7,6},{8,9},{9,8},{10,11... | collective-permute-start | bytes 12296 | tf_op jit(solution)/shard_map/ppermute | solution.py:142

commit v2 on v1

v2 whole, which is shorter than its diff:
```python
import functools
import math

import jax
import jax.numpy as jnp
from jax import lax
from jax.experimental import pallas as pl
from jax.experimental.pallas import tpu as pltpu
from jax.sharding import PartitionSpec as P

HD = 128
AHEAD = 2
LANES = 128


def attend_kernel(
    query_hbm,
    key_hbm,
    value_hbm,
    lengths_hbm,
    residual_hbm,
    router_hbm,
    routes_hbm,
    hidden_ref,
    meta_ref,
    query_ref,
    key_ref,
    value_ref,
    lengths_ref,
    residual_ref,
    router_ref,
    routes_ref,
    arrival,
):
    batches, per_batch, width = query_ref.shape
    rows = batches * per_batch
    cache_len = key_ref.shape[2]
    kv_local = key_ref.shape[3] // HD
    group = width // key_ref.shape[3]
    early = [(query_hbm, query_ref), (lengths_hbm, lengths_ref), (key_hbm, key_ref)]
    late = [
        (value_hbm, value_ref),
        (residual_hbm, residual_ref),
        (router_hbm, router_ref),
        (routes_hbm, routes_ref),
    ]
    copies = [
        pltpu.make_async_copy(source, target, arrival.at[i])
        for i, (source, target) in enumerate(early + late)
    ]
    for copy in copies:
        copy.start()
    for copy in copies[: len(early)]:
        copy.wait()

    def stacked(ref):
        return jnp.concatenate([ref[b].astype(jnp.float32) for b in range(batches)], axis=0)

    queries = stacked(query_ref)
    tall = group * rows
    row_of = lax.rem(lax.broadcasted_iota(jnp.int32, (tall, 1), 0), rows)
    position = lax.broadcasted_iota(jnp.int32, (tall, cache_len), 1)
    limit = jnp.zeros((tall, 1), jnp.int32)
    for r in range(rows):
        limit = jnp.where(row_of == r, lengths_ref[r // per_batch, r % per_batch], limit)
    live = position < limit
    pieces = []
    for k in range(kv_local):
        heads = jnp.concatenate(
            [queries[:, (k * group + j) * HD : (k * group + j + 1) * HD] for j in range(group)],
            axis=0,
        ).astype(jnp.bfloat16)
        columns = slice(k * HD, (k + 1) * HD)
        scores = jnp.zeros((tall, cache_len), jnp.float32)
        for r in range(rows):
            keys = key_ref[r // per_batch, r % per_batch, :, columns]
            part = lax.dot_general(
                heads, keys, (((1,), (1,)), ((), ())), preferred_element_type=jnp.float32
            )
            scores = jnp.where(row_of == r, part, scores)
        scores = jnp.where(live, scores * (1.0 / math.sqrt(HD)), -jnp.inf)
        peak = jnp.max(scores, axis=-1, keepdims=True)
        weights = jnp.where(live, jnp.exp(scores - peak), 0.0)
        total = jnp.sum(weights, axis=-1, keepdims=True)
        weights_bf = weights.astype(jnp.bfloat16)
        if k == 0:
            for copy in copies[len(early) :]:
                copy.wait()
        mixed = jnp.zeros((tall, HD), jnp.float32)
        for r in range(rows):
            values = value_ref[r // per_batch, r % per_batch, :, columns]
            part = jnp.dot(weights_bf, values, preferred_element_type=jnp.float32)
            mixed = jnp.where(row_of == r, part, mixed)
        mixed = mixed / total
        pieces += [mixed[j * rows : (j + 1) * rows] for j in range(group)]
    attended = jnp.concatenate(pieces, axis=1)
    hidden = (stacked(residual_ref) + attended).astype(jnp.bfloat16)
    wide = hidden.astype(jnp.float32)
    logits = lax.dot_general(
        hidden, router_ref[...], (((1,), (1,)), ((), ())), preferred_element_type=jnp.float32
    )
    squares = jnp.sum(wide * wide, axis=-1, keepdims=True)
    experts = router_ref.shape[0]
    row = lax.broadcasted_iota(jnp.int32, (rows, 1), 0)
    meta_ref[...] = jnp.zeros_like(meta_ref)
    meta_ref[:, :experts] = logits
    meta_ref[:, experts : experts + 1] = squares
    for which in range(2):
        route = jnp.zeros((rows, 1), jnp.int32)
        for r in range(rows):
            route = jnp.where(row == r, routes_ref[r // per_batch, which, r % per_batch], route)
        lane = experts + 1 + which
        meta_ref[:, lane : lane + 1] = route.astype(jnp.float32)
    hidden_ref[...] = hidden


def fetch_kernel(after_ref, meta_ref, source_hbm, target_ref, meta_out_ref, arrival):
    copy = pltpu.make_async_copy(
        source_hbm.at[:, pl.ds(0, target_ref.shape[1])], target_ref, arrival
    )
    copy.start()
    meta_out_ref[...] = meta_ref[...]
    copy.wait()


def stack_kernel(*refs):
    for i, ref in enumerate(refs[:-2]):
        refs[-1][i] = ref[...]


def expert_kernel(
    offsets,
    *refs,
):
    parts = (len(refs) - 13) // 2
    own_refs, other_refs = refs[:parts], refs[parts : 2 * parts]
    (
        gate_ref,
        first_up_ref,
        up_hbm,
        down_hbm,
        kept_ref,
        sent_ref,
        normed,
        gates,
        units_bf,
        up_ref,
        down_ref,
        up_arrival,
        down_arrival,
    ) = refs[2 * parts :]
    count, width = normed.shape
    half = width // 2
    units = gate_ref.shape[1]
    block = min(512, units)
    first = first_up_ref.shape[1]
    me = lax.axis_index("devs")
    side = lax.axis_index("pair")
    own_start = pl.multiple_of(side * half, LANES)
    other_start = pl.multiple_of((1 - side) * half, LANES)

    up_copies = []
    for i, start in enumerate(range(first, units, block)):
        up_copies.append(
            pltpu.make_async_copy(
                up_hbm.at[:, pl.ds(start, block)], up_ref.at[i], up_arrival.at[i]
            )
        )
    down_copies = []
    slices = down_ref.shape[0]
    piece = down_ref.shape[2]
    for i in range(slices):
        base = other_start if i < slices // 2 else own_start
        start = pl.multiple_of(base + (i % (slices // 2)) * piece, LANES)
        down_copies.append(
            pltpu.make_async_copy(
                down_hbm.at[:, pl.ds(start, piece)], down_ref.at[i], down_arrival.at[i]
            )
        )
    copies = up_copies + down_copies
    for copy in copies[:AHEAD]:
        copy.start()

    def wait(i):
        copies[i].wait()
        if i + AHEAD < len(copies):
            copies[i + AHEAD].start()

    def rows_of(refs):
        tall = [ref[...].astype(jnp.float32).reshape(-1, half) for ref in refs]
        return jnp.concatenate(tall, axis=0)

    own, other = rows_of(own_refs), rows_of(other_refs)
    squares = jnp.sum(own * own, axis=-1, keepdims=True) + jnp.sum(
        other * other, axis=-1, keepdims=True
    )
    inv_rms = lax.rsqrt(squares / width + 1e-05)
    normed[:, pl.ds(own_start, half)] = (own * inv_rms).astype(jnp.bfloat16)
    normed[:, pl.ds(other_start, half)] = (other * inv_rms).astype(jnp.bfloat16)

    for start in range(0, units, block):
        part = slice(start, start + block)
        gate = jnp.dot(normed[...], gate_ref[:, part], preferred_element_type=jnp.float32)
        gates[:, part] = jax.nn.silu(gate)
    for start in range(0, units, block):
        part = slice(start, start + block)
        if start < first:
            held = first_up_ref[:, part]
        else:
            i = (start - first) // block
            wait(i)
            held = up_ref[i]
        up = jnp.dot(normed[...], held, preferred_element_type=jnp.float32)
        units_bf[:, part] = (gates[:, part] * up).astype(jnp.bfloat16)
    rows = count // len(offsets)
    for i in range(slices):
        wait(len(up_copies) + i)
        product = jnp.dot(units_bf[...], down_ref[i], preferred_element_type=jnp.float32)
        columns = slice(i % (slices // 2) * piece, (i % (slices // 2) + 1) * piece)
        target = sent_ref if i < slices // 2 else kept_ref
        for j, offset in enumerate(offsets):
            target[lax.bitwise_xor(me, offset), :, columns] = product[
                j * rows : (j + 1) * rows
            ].astype(target.dtype)


def combine_kernel(
    experts, returned_ref, hidden_ref, meta_ref, meta_other_ref, out_ref
):
    devices, rows, half = returned_ref.shape
    batches, per_batch, _ = out_ref.shape
    owners = devices // experts
    meta = meta_ref[...] + meta_other_ref[...]
    squares = meta[:, experts : experts + 1]
    inv_rms = lax.rsqrt(squares / (2 * half) + 1e-05)
    logits = meta * inv_rms
    chosen = meta_ref[:, experts + 1 : experts + 3].astype(jnp.int32)
    lane = lax.broadcasted_iota(jnp.int32, (rows, LANES), 1)
    first, second = chosen[:, 0:1], chosen[:, 1:2]
    logit_first = jnp.sum(jnp.where(lane == first, logits, 0.0), axis=-1, keepdims=True)
    logit_second = jnp.sum(jnp.where(lane == second, logits, 0.0), axis=-1, keepdims=True)
    gate_first = jax.nn.sigmoid(logit_first - logit_second)
    gate_second = jax.nn.sigmoid(logit_second - logit_first)
    result = hidden_ref[...].astype(jnp.float32)
    for e in range(experts):
        expert_out = returned_ref[e * owners].astype(jnp.float32)
        for o in range(1, owners):
            expert_out += returned_ref[e * owners + o].astype(jnp.float32)
        weight = jnp.where(first == e, gate_first, 0.0) + jnp.where(second == e, gate_second, 0.0)
        result += weight * expert_out
    for b in range(batches):
        out_ref[b] = result[b * per_batch : (b + 1) * per_batch].astype(jnp.bfloat16)


VMEM = pl.BlockSpec(memory_space=pltpu.VMEM)
HBM = pl.BlockSpec(memory_space=pltpu.HBM)


def far(array):
    return pltpu.with_memory_space_constraint(array, pltpu.HBM)


def fetch(meta, weights, columns, after=None):
    after = meta if after is None else after
    near = jax.ShapeDtypeStruct((weights.shape[0], columns), weights.dtype)
    return pl.pallas_call(
        fetch_kernel,
        in_specs=[VMEM, VMEM, HBM],
        out_specs=[VMEM, VMEM],
        out_shape=[near, jax.ShapeDtypeStruct(meta.shape, meta.dtype)],
        scratch_shapes=[pltpu.SemaphoreType.DMA],
        compiler_params=pltpu.CompilerParams(vmem_limit_bytes=1 << 20),
        cost_estimate=pl.CostEstimate(
            flops=0, bytes_accessed=2 * near.size, transcendentals=0
        ),
    )(after, meta, far(weights))


def swap_devices(value, offset, devices):
    return lax.ppermute(value, "devs", [(d, d ^ offset) for d in range(devices)])


def swap_cores(value):
    return lax.ppermute(value, "pair", [(0, 1), (1, 0)])


def on_device(
    query, key_cache, value_cache, lengths, residual, router, routes, w_gate, w_up, w_down
):
    devices = lax.axis_size("devs")
    experts = router.shape[1]
    batches, per_batch, half = query.shape
    rows = batches * per_batch
    inputs = (
        query,
        key_cache,
        value_cache,
        lengths,
        residual,
        jnp.transpose(router),
        jnp.transpose(routes, (0, 2, 1)),
    )
    hidden, meta = pl.pallas_call(
        attend_kernel,
        in_specs=[HBM] * 7,
        out_specs=[VMEM, VMEM],
        out_shape=[
            jax.ShapeDtypeStruct((rows, half), jnp.bfloat16),
            jax.ShapeDtypeStruct((rows, LANES), jnp.float32),
        ],
        scratch_shapes=[
            (pltpu.SMEM if array.dtype == jnp.int32 else pltpu.VMEM)(array.shape, array.dtype)
            for array in inputs
        ]
        + [pltpu.SemaphoreType.DMA((7,))],
        compiler_params=pltpu.CompilerParams(vmem_limit_bytes=16 << 20),
    )(*[far(array) for array in inputs])
    width, units = w_gate.shape
    block = min(512, units)
    first = min(1024, units)
    piece = min(512, half)
    count = devices * rows
    owners = devices // experts

    offsets = [k * owners for k in range(experts)]
    crossed = [swap_devices(hidden, offset, devices) for offset in offsets[1:]]
    gate_near, meta = fetch(meta, w_gate, units)
    held = [
        pl.pallas_call(
            stack_kernel,
            in_specs=[VMEM] * (experts + 1),
            out_specs=VMEM,
            out_shape=jax.ShapeDtypeStruct((experts, rows, half), jnp.bfloat16),
            compiler_params=pltpu.CompilerParams(vmem_limit_bytes=2 << 20),
        )(hidden, *crossed, meta)
    ]
    step = 1
    while step < owners:
        if len(held) > 1:
            held = [jnp.concatenate(held, axis=0)]
        held.append(swap_devices(held[0], step, devices))
        offsets += [offset ^ step for offset in offsets]
        step *= 2
    up_near, meta = fetch(meta, w_up, first, held[0])
    others = [swap_cores(held[0])]
    if len(held) > 1:
        held[1], meta = lax.optimization_barrier((held[1], meta))
        others.append(swap_cores(held[1]))
    meta_other = swap_cores(meta)
    kept, sent = pl.pallas_call(
        functools.partial(expert_kernel, offsets),
        in_specs=[VMEM] * (2 * len(held) + 2) + [HBM] * 2,
        out_specs=[VMEM, VMEM],
        out_shape=[
            jax.ShapeDtypeStruct((devices, rows, half), jnp.float32),
            jax.ShapeDtypeStruct((devices, rows, half), jnp.bfloat16),
        ],
        scratch_shapes=[
            pltpu.VMEM((count, width), jnp.bfloat16),
            pltpu.VMEM((count, units), jnp.float32),
            pltpu.VMEM((count, units), jnp.bfloat16),
            pltpu.VMEM((max(1, (units - first) // block), width, block), jnp.bfloat16),
            pltpu.VMEM((width // piece, units, piece), jnp.bfloat16),
            pltpu.SemaphoreType.DMA((max(1, (units - first) // block),)),
            pltpu.SemaphoreType.DMA((width // piece,)),
        ],
        compiler_params=pltpu.CompilerParams(vmem_limit_bytes=32 << 20),
    )(*held, *others, gate_near, up_near, far(w_up), far(w_down))
    received = swap_cores(sent)
    summed = (kept + received.astype(jnp.float32)).astype(jnp.bfloat16)
    returned = lax.all_to_all(summed, "devs", split_axis=0, concat_axis=0, tiled=True)
    return pl.pallas_call(
        functools.partial(combine_kernel, experts),
        in_specs=[VMEM] * 4,
        out_specs=VMEM,
        out_shape=jax.ShapeDtypeStruct(query.shape, jnp.bfloat16),
        compiler_params=pltpu.CompilerParams(vmem_limit_bytes=16 << 20),
    )(returned, hidden, meta, meta_other)


def solution(mesh):
    in_specs = (
        P(None, ("groups", "devs"), "pair"),
        P(None, ("groups", "devs"), None, "pair"),
        P(None, ("groups", "devs"), None, "pair"),
        P(None, ("groups", "devs")),
        P(None, ("groups", "devs"), "pair"),
        P("pair", None),
        P(None, ("groups", "devs"), None),
        P(None, ("devs", "pair")),
        P(None, ("devs", "pair")),
        P(("devs", "pair"), None),
    )
    out_specs = P(None, ("groups", "devs"), "pair")
    return jax.shard_map(
        on_device, mesh=mesh, in_specs=in_specs, out_specs=out_specs, check_vma=False
    )
```

time: 53.7 us -> 46.6 us (0.87)
  blocking collectives: 15 us -> 0 us
  starting transfers between devices: 3.8 us -> 12.9 us
  local copies, waits for them, and re-layouts: 5.69 us -> 0 us
  Pallas kernels: 17 us -> 20.8 us
  waiting for transfers between devices: 10.9 us -> 11.8 us
    all_to_all x1 -> x0, blocking collectives: 15 us -> none  [on_device(): lax.all_to_all(outgoing, 'devs', split_axis=0, concat_axis=0, tiled=True)]
    ppermute x0 -> x4, starting transfers between devices: none -> 7.24 us  [swap_devices(): lax.ppermute(value, 'devs', [(d, d ^ offset) for d in range(devices)])]
    unnamed x14 -> x0, local copies, waits for them, and re-layouts: 5.69 us -> none
    pallas_call x2 -> x5, Pallas kernels: 16 us -> 19.9 us  [the longest x1 9.92 us: on_device(): pl.pallas_call(functools.partial(expert_kernel, offsets), in_specs=[VMEM]...]
    all_to_all x1, starting transfers between devices: 3.39 us -> 5.03 us  [on_device(): lax.all_to_all(summed, 'devs', split_axis=0, concat_axis=0, tiled=True)]
    ppermute x0 -> x4, waiting for transfers between devices: none -> 1.34 us  [swap_devices(): lax.ppermute(value, 'devs', [(d, d ^ offset) for d in range(devices)])]
    ppermute x3 -> x4, waiting for transfers between devices: 3.67 us -> 3.38 us  [swap_cores(): return lax.ppermute(value, 'pair', [(0, 1), (1, 0)])]
  transfers between devices with their start and end apart: 4 -> 9, of which waited for: 4 -> 6; matrix products, arithmetic and copies ran while one was open for 0% -> 0% of each run, Pallas kernels for 0% -> 16%
where the time goes in v2:
time: 46.6 us; the launch traced here: 46.3 us
  Pallas kernels  20.8 us (45%)
  starting transfers between devices  12.9 us (28%)
  waiting for transfers between devices  11.8 us (25%)
  other arithmetic  0.71 us (2%)
    pallas_call x1, Pallas kernels, on_device(): pl.pallas_call(functools.partial(expert_kernel, offsets), in_specs=[VMEM]...  9.92 us
    pallas_call x2, Pallas kernels, fetch(): pl.pallas_call(fetch_kernel, in_specs=[VMEM, VMEM, HBM], out_specs=[VMEM,...  7.38 us
    ppermute x4, starting transfers between devices, swap_devices(): lax.ppermute(value, 'devs', [(d, d ^ offset) for d in range(devices)])  7.24 us
    all_to_all x1, waiting for transfers between devices, on_device(): lax.all_to_all(summed, 'devs', split_axis=0, concat_axis=0, tiled=True)  7.11 us
    all_to_all x1, starting transfers between devices, on_device(): lax.all_to_all(summed, 'devs', split_axis=0, concat_axis=0, tiled=True)  5.03 us
    ppermute x4, waiting for transfers between devices, swap_cores(): return lax.ppermute(value, 'pair', [(0, 1), (1, 0)])  3.38 us
    pallas_call x1, Pallas kernels, on_device(): pl.pallas_call(attend_kernel, in_specs=[HBM] * 7, out_specs=[VMEM, VMEM],...  2.57 us
    ppermute x4, waiting for transfers between devices, swap_devices(): lax.ppermute(value, 'devs', [(d, d ^ offset) for d in range(devices)])  1.34 us
  transfers between devices with their start and end apart: 9, of which 6 were waited for; matrix products, arithmetic and copies ran while one was open for 0% of the time, Pallas kernels for 16%

profile of v2, /device:TPU:0, one launch (start us, length us, event | category | flops | bytes accessed | tf_op | source)
XLA Modules:
  0.0 46.3 jit_solution(4338015853226825617)
XLA Ops:
  0.0 2.6 %shard_map.100 = (bf16[8,1536]{1,0:T(8,128)(2,1)S(1)}, f32[8,128]{1,0:T(8,128)S(1)}) custom-call(bf16[2,4,1536]{2,1,0:T(4,128)(2,1)} %query_hbm.1, bf16[2,4,256,256]{3,2,1,0:T(8,128)(2,1)} %key_hbm.1, bf16[2,4,256,256]{3,2,1,0:T(8,128)(2,1)} %value_hbm.1, s32[2,4]{1,0:T(2,128)} %lengths_hbm.1, bf16[2,4,1536]{2,1,0:T(4,128)(2,1)} %residual_hbm.1, ...), custom_call_target="tpu_custom_call" | custom-call | tf_op jit(solution)/shard_map/pallas_call | solution.py:303
  2.6 3.1 %collective-permute-start = (bf16[8,1536]{1,0:T(8,128)(2,1)S(1)}, bf16[8,1536]{1,0:T(8,128)(2,1)S(1)}, u32[]{:S(2)}, u32[]{:S(2)}) collective-permute-start(bf16[8,1536]{1,0:T(8,128)(2,1)S(1)} %get-tuple-element.15.refs_0_.hidden_ref), channel_id=1, source_target_pairs={{0,4},{2,6},{4,0},{6,2},{8,12},{10,14},{12,8},{14,10},{1,5},{3,7},... | collective-permute-start | bytes 73736 | tf_op jit(solution)/shard_map/ppermute | solution.py:280
  5.7 2.6 %collective-permute-start.1 = (bf16[8,1536]{1,0:T(8,128)(2,1)S(1)}, bf16[8,1536]{1,0:T(8,128)(2,1)S(1)}, u32[]{:S(2)}, u32[]{:S(2)}) collective-permute-start(bf16[8,1536]{1,0:T(8,128)(2,1)S(1)} %get-tuple-element.15.refs_0_.hidden_ref), channel_id=1, source_target_pairs={{0,8},{2,10},{4,12},{6,14},{8,0},{10,2},{12,4},{14,6},{1,9},{3,11}... | collective-permute-start | bytes 73736 | tf_op jit(solution)/shard_map/ppermute | solution.py:280
  8.3 0.0 collective-permute-start.2
  8.3 4.6 %shard_map.101 = (bf16[3072,2048]{1,0:T(8,128)(2,1)S(1)}, f32[8,128]{1,0:T(8,128)S(1)}) custom-call(f32[8,128]{1,0:T(8,128)S(1)} %get-tuple-element.16.after_ref.meta_ref, f32[8,128]{1,0:T(8,128)S(1)} %get-tuple-element.16.after_ref.meta_ref, bf16[3072,2048]{1,0:T(8,128)(2,1)} %source_hbm.2), custom_call_target="tpu_custom_call" | custom-call | bytes 12582912 | tf_op jit(solution)/shard_map/pallas_call | solution.py:266
  12.9 0.0 collective-permute-done.refs_1_
  12.9 0.0 collective-permute-done.1.refs_2_
  12.9 1.0 %collective-permute-done.2.refs_3_ = bf16[8,1536]{1,0:T(8,128)(2,1)S(1)} collective-permute-done((bf16[8,1536]{1,0:T(8,128)(2,1)S(1)}, bf16[8,1536]{1,0:T(8,128)(2,1)S(1)}, u32[]{:S(2)}, u32[]{:S(2)}) %collective-permute-start.2) | collective-permute-done | bytes 24608 | tf_op jit(solution)/shard_map/ppermute | solution.py:280
  13.9 1.6 %collective-permute-start.3 = (bf16[4,8,1536]{2,1,0:T(8,128)(2,1)S(1)}, bf16[4,8,1536]{2,1,0:T(8,128)(2,1)S(1)}, u32[]{:S(2)}, u32[]{:S(2)}) collective-permute-start(bf16[4,8,1536]{2,1,0:T(8,128)(2,1)S(1)} %shard_map.102.after_ref.refs_0_), channel_id=1, source_target_pairs={{0,2},{2,0},{4,6},{6,4},{8,10},{10,8},{12,14},{14,12},{1,3},{3,1},... | collective-permute-start | bytes 294920 | tf_op jit(solution)/shard_map/ppermute | solution.py:280
  15.5 0.0 collective-permute-start.4
  15.5 2.8 %shard_map.103 = (bf16[3072,1024]{1,0:T(8,128)(2,1)S(1)}, f32[8,128]{1,0:T(8,128)S(1)}) custom-call(bf16[4,8,1536]{2,1,0:T(8,128)(2,1)S(1)} %shard_map.102.after_ref.refs_0_, f32[8,128]{1,0:T(8,128)S(1)} %get-tuple-element.17.refs_4_.meta_ref, bf16[3072,2048]{1,0:T(8,128)(2,1)} %refs_6_.1), custom_call_target="tpu_custom_call" | custom-call | bytes 6291456 | tf_op jit(solution)/shard_map/pallas_call | solution.py:266
  18.3 0.3 collective-permute-done.3.refs_1_
  18.6 0.3 collective-permute-start.5
  18.8 0.0 collective-permute-done.4.refs_2_
  18.8 1.0 %collective-permute-done.5.refs_3_ = bf16[4,8,1536]{2,1,0:T(8,128)(2,1)S(1)} collective-permute-done((bf16[4,8,1536]{2,1,0:T(8,128)(2,1)S(1)}, bf16[4,8,1536]{2,1,0:T(8,128)(2,1)S(1)}, u32[]{:S(2)}, u32[]{:S(2)}) %collective-permute-start.5) | collective-permute-done | bytes 98336 | tf_op jit(solution)/shard_map/ppermute | solution.py:284
  19.9 9.9 %shard_map.104 = (f32[8,8,1536]{2,1,0:T(8,128)S(1)}, bf16[8,8,1536]{2,1,0:T(8,128)(2,1)S(1)}) custom-call(bf16[4,8,1536]{2,1,0:T(8,128)(2,1)S(1)} %shard_map.102.after_ref.refs_0_, bf16[4,8,1536]{2,1,0:T(8,128)(2,1)S(1)} %collective-permute-done.3.refs_1_, bf16[4,8,1536]{2,1,0:T(8,128)(2,1)S(1)} %collective-permute-done.4.refs_2_, ...), custom_call_target="tpu_custom_call" | custom-call | tf_op jit(solution)/shard_map/pallas_call | solution.py:350
  29.8 0.3 collective-permute-start.6
  30.1 1.2 %collective-permute-done.6 = bf16[8,8,1536]{2,1,0:T(8,128)(2,1)S(1)} collective-permute-done((bf16[8,8,1536]{2,1,0:T(8,128)(2,1)S(1)}, bf16[8,8,1536]{2,1,0:T(8,128)(2,1)S(1)}, u32[]{:S(2)}, u32[]{:S(2)}) %collective-permute-start.6) | collective-permute-done | bytes 196640 | tf_op jit(solution)/shard_map/ppermute | solution.py:284
  31.3 0.7 %add_convert_fusion = bf16[8,8,1536]{2,1,0:T(8,128)(2,1)} fusion(f32[8,8,1536]{2,1,0:T(8,128)S(1)} %get-tuple-element.22, bf16[8,8,1536]{2,1,0:T(8,128)(2,1)S(1)} %collective-permute-done.6), kind=kLoop, calls=%fused_computation | loop fusion | flops 294912 | bytes 786432 | tf_op jit(solution)/shard_map/convert_element_type | solution.py:370
  32.0 5.0 %all-to-all-start = ((bf16[8,8,1536]{2,1,0:T(8,128)(2,1)}), bf16[8,8,1536]{2,1,0:T(8,128)(2,1)S(1)}, u32[]{:S(2)}, u32[]{:S(2)}) async-start(bf16[8,8,1536]{2,1,0:T(8,128)(2,1)} %add_convert_fusion), calls=%async_computation | async-start | bytes 393216 | tf_op jit(solution)/shard_map/all_to_all | solution.py:371
  37.1 0.0 collective-permute-start.7
  37.1 1.2 %collective-permute-done.7.meta_other_ref = f32[8,128]{1,0:T(8,128)S(1)} collective-permute-done((f32[8,128]{1,0:T(8,128)S(1)}, f32[8,128]{1,0:T(8,128)S(1)}, u32[]{:S(2)}, u32[]{:S(2)}) %collective-permute-start.7) | collective-permute-done | bytes 4128 | tf_op jit(solution)/shard_map/ppermute | solution.py:284
  38.2 7.1 %all-to-all-done.returned_ref = bf16[8,8,1536]{2,1,0:T(8,128)(2,1)S(1)} async-done(((bf16[8,8,1536]{2,1,0:T(8,128)(2,1)}), bf16[8,8,1536]{2,1,0:T(8,128)(2,1)S(1)}, u32[]{:S(2)}, u32[]{:S(2)}) %all-to-all-start) | async-done | bytes 196640 | tf_op jit(solution)/shard_map/all_to_all | solution.py:371
  45.3 0.9 %shard_map.105 = bf16[2,4,1536]{2,1,0:T(4,128)(2,1)} custom-call(bf16[8,8,1536]{2,1,0:T(8,128)(2,1)S(1)} %all-to-all-done.returned_ref, bf16[8,1536]{1,0:T(8,128)(2,1)S(1)} %get-tuple-element.15.refs_0_.hidden_ref, f32[8,128]{1,0:T(8,128)S(1)} %get-tuple-element.24.meta_ref, f32[8,128]{1,0:T(8,128)S(1)} %collective-permute-done.7.meta_other_ref), custom_call_target="tpu_custom_call" | custom-call | tf_op jit(solution)/shard_map/pallas_call | solution.py:372
  (1 shorter events, 0.0 us)
Async XLA Ops:
  2.6 10.3 %collective-permute-start = (bf16[8,1536]{1,0:T(8,128)(2,1)S(1)}, bf16[8,1536]{1,0:T(8,128)(2,1)S(1)}, u32[]{:S(2)}, u32[]{:S(2)}) collective-permute-start(bf16[8,1536]{1,0:T(8,128)(2,1)S(1)} %get-tuple-element.15.refs_0_.hidden_ref), channel_id=1, source_target_pairs={{0,4},{2,6},{4,0},{6,2},{8,12},{10,14},{12,8},{14,10},{1,5},{3,7},... | collective-permute-start | bytes 73736 | tf_op jit(solution)/shard_map/ppermute | solution.py:280
  5.7 7.2 %collective-permute-start.1 = (bf16[8,1536]{1,0:T(8,128)(2,1)S(1)}, bf16[8,1536]{1,0:T(8,128)(2,1)S(1)}, u32[]{:S(2)}, u32[]{:S(2)}) collective-permute-start(bf16[8,1536]{1,0:T(8,128)(2,1)S(1)} %get-tuple-element.15.refs_0_.hidden_ref), channel_id=1, source_target_pairs={{0,8},{2,10},{4,12},{6,14},{8,0},{10,2},{12,4},{14,6},{1,9},{3,11}... | collective-permute-start | bytes 73736 | tf_op jit(solution)/shard_map/ppermute | solution.py:280
  8.3 5.6 %collective-permute-start.2 = (bf16[8,1536]{1,0:T(8,128)(2,1)S(1)}, bf16[8,1536]{1,0:T(8,128)(2,1)S(1)}, u32[]{:S(2)}, u32[]{:S(2)}) collective-permute-start(bf16[8,1536]{1,0:T(8,128)(2,1)S(1)} %get-tuple-element.15.refs_0_.hidden_ref), channel_id=1, source_target_pairs={{0,12},{2,14},{4,8},{6,10},{8,4},{10,6},{12,0},{14,2},{1,13},{3,15... | collective-permute-start | bytes 73736 | tf_op jit(solution)/shard_map/ppermute | solution.py:280
  13.9 4.7 %collective-permute-start.3 = (bf16[4,8,1536]{2,1,0:T(8,128)(2,1)S(1)}, bf16[4,8,1536]{2,1,0:T(8,128)(2,1)S(1)}, u32[]{:S(2)}, u32[]{:S(2)}) collective-permute-start(bf16[4,8,1536]{2,1,0:T(8,128)(2,1)S(1)} %shard_map.102.after_ref.refs_0_), channel_id=1, source_target_pairs={{0,2},{2,0},{4,6},{6,4},{8,10},{10,8},{12,14},{14,12},{1,3},{3,1},... | collective-permute-start | bytes 294920 | tf_op jit(solution)/shard_map/ppermute | solution.py:280
  15.5 3.4 %collective-permute-start.4 = (bf16[4,8,1536]{2,1,0:T(8,128)(2,1)S(1)}, bf16[4,8,1536]{2,1,0:T(8,128)(2,1)S(1)}, u32[]{:S(2)}, u32[]{:S(2)}) collective-permute-start(bf16[4,8,1536]{2,1,0:T(8,128)(2,1)S(1)} %shard_map.102.after_ref.refs_0_), channel_id=1, source_target_pairs={{0,1},{1,0},{2,3},{3,2},{4,5},{5,4},{6,7},{7,6},{8,9},{9,8},{10,11... | collective-permute-start | bytes 294920 | tf_op jit(solution)/shard_map/ppermute | solution.py:284
  18.6 1.3 %collective-permute-start.5 = (bf16[4,8,1536]{2,1,0:T(8,128)(2,1)S(1)}, bf16[4,8,1536]{2,1,0:T(8,128)(2,1)S(1)}, u32[]{:S(2)}, u32[]{:S(2)}) collective-permute-start(bf16[4,8,1536]{2,1,0:T(8,128)(2,1)S(1)} %collective-permute-done.3.refs_1_), channel_id=1, source_target_pairs={{0,1},{1,0},{2,3},{3,2},{4,5},{5,4},{6,7},{7,6},{8,9},{9,8},{10,11... | collective-permute-start | bytes 294920 | tf_op jit(solution)/shard_map/ppermute | solution.py:284
  29.8 1.5 %collective-permute-start.6 = (bf16[8,8,1536]{2,1,0:T(8,128)(2,1)S(1)}, bf16[8,8,1536]{2,1,0:T(8,128)(2,1)S(1)}, u32[]{:S(2)}, u32[]{:S(2)}) collective-permute-start(bf16[8,8,1536]{2,1,0:T(8,128)(2,1)S(1)} %get-tuple-element.23), channel_id=1, source_target_pairs={{0,1},{1,0},{2,3},{3,2},{4,5},{5,4},{6,7},{7,6},{8,9},{9,8},{10,11... | collective-permute-start | bytes 589832 | tf_op jit(solution)/shard_map/ppermute | solution.py:284
  32.0 13.3 %all-to-all-start = ((bf16[8,8,1536]{2,1,0:T(8,128)(2,1)}), bf16[8,8,1536]{2,1,0:T(8,128)(2,1)S(1)}, u32[]{:S(2)}, u32[]{:S(2)}) async-start(bf16[8,8,1536]{2,1,0:T(8,128)(2,1)} %add_convert_fusion), calls=%async_computation | async-start | bytes 393216 | tf_op jit(solution)/shard_map/all_to_all | solution.py:371
  37.1 1.2 %collective-permute-start.7 = (f32[8,128]{1,0:T(8,128)S(1)}, f32[8,128]{1,0:T(8,128)S(1)}, u32[]{:S(2)}, u32[]{:S(2)}) collective-permute-start(f32[8,128]{1,0:T(8,128)S(1)} %get-tuple-element.24.meta_ref), channel_id=1, source_target_pairs={{0,1},{1,0},{2,3},{3,2},{4,5},{5,4},{6,7},{7,6},{8,9},{9,8},{10,11... | collective-permute-start | bytes 12296 | tf_op jit(solution)/shard_map/ppermute | solution.py:284

commit v3 on v2

--- a/solution.py
+++ b/solution.py
@@ -9,7 +9,6 @@
 from jax.sharding import PartitionSpec as P
 
 HD = 128
-AHEAD = 2
 LANES = 128
 
 
@@ -114,13 +113,25 @@
     hidden_ref[...] = hidden
 
 
-def fetch_kernel(after_ref, meta_ref, source_hbm, target_ref, meta_out_ref, arrival):
-    copy = pltpu.make_async_copy(
-        source_hbm.at[:, pl.ds(0, target_ref.shape[1])], target_ref, arrival
-    )
-    copy.start()
+def fetch_kernel(starts, after_ref, meta_ref, *refs):
+    count = len(starts)
+    sources, targets, meta_out_ref, arrival = (
+        refs[:count],
+        refs[count : 2 * count],
+        refs[2 * count],
+        refs[2 * count + 1],
+    )
+    copies = [
+        pltpu.make_async_copy(
+            source.at[pl.ds(start, target.shape[0])], target, arrival.at[i]
+        )
+        for i, (start, source, target) in enumerate(zip(starts, sources, targets))
+    ]
+    for copy in copies:
+        copy.start()
     meta_out_ref[...] = meta_ref[...]
-    copy.wait()
+    for copy in copies:
+        copy.wait()
 
 
 def stack_kernel(*refs):
@@ -128,100 +139,134 @@
         refs[-1][i] = ref[...]
 
 
-def expert_kernel(
-    offsets,
-    *refs,
-):
-    parts = (len(refs) - 13) // 2
-    own_refs, other_refs = refs[:parts], refs[parts : 2 * parts]
+def rows_of(refs):
+    half = refs[0].shape[-1]
+    tall = [ref[...].astype(jnp.float32).reshape(-1, half) for ref in refs]
+    return jnp.concatenate(tall, axis=0)
+
+
+def half_starts(half):
+    side = lax.axis_index("pair")
+    return (
+        pl.multiple_of(side * half, LANES),
+        pl.multiple_of((1 - side) * half, LANES),
+    )
+
+
+def gate_kernel(block, *refs):
+    *own_refs, gate_ref, down_hbm, gates_ref, down_ref, arrival = refs
+    half = own_refs[0].shape[-1]
+    units = gate_ref.shape[1]
+    own_start, _ = half_starts(half)
+    copy = pltpu.make_async_copy(down_hbm.at[pl.ds(0, block)], down_ref, arrival)
+    copy.start()
+    rows = rows_of(own_refs).astype(jnp.bfloat16)
+    for start in range(0, units, block):
+        part = slice(start, start + block)
+        gates_ref[:, part] = jnp.dot(
+            rows, gate_ref[pl.ds(own_start, half), part], preferred_element_type=jnp.float32
+        )
+    copy.wait()
+
+
+def store_rows(offsets, target, columns, product):
+    me = lax.axis_index("devs")
+    rows = target.shape[1]
+    for j, offset in enumerate(offsets):
+        target[lax.bitwise_xor(me, offset), :, columns] = product[
+            j * rows : (j + 1) * rows
+        ].astype(target.dtype)
+
+
+def down_dot(units_ref, down_refs, columns):
+    total, start = None, 0
+    for ref in down_refs:
+        stop = start + ref.shape[0]
+        product = jnp.dot(
+            units_ref[:, start:stop], ref[:, columns], preferred_element_type=jnp.float32
+        )
+        total = product if total is None else total + product
+        start = stop
+    return total
+
+
+def expert_kernel(block, piece, offsets, parts, *refs):
+    own_refs, refs = refs[:parts], refs[parts:]
+    other_refs, refs = refs[:parts], refs[parts:]
     (
+        up_early_ref,
+        up_late_ref,
         gate_ref,
-        first_up_ref,
-        up_hbm,
+        gates_ref,
+        down_early_ref,
+        meta_other_ref,
         down_hbm,
-        kept_ref,
         sent_ref,
-        normed,
-        gates,
-        units_bf,
-        up_ref,
-        down_ref,
-        up_arrival,
-        down_arrival,
-    ) = refs[2 * parts :]
-    count, width = normed.shape
+        units_ref,
+        down_late_ref,
+        rows_ref,
+        arrival,
+    ) = refs
+    width = rows_ref.shape[1]
     half = width // 2
     units = gate_ref.shape[1]
-    block = min(512, units)
-    first = first_up_ref.shape[1]
-    me = lax.axis_index("devs")
-    side = lax.axis_index("pair")
-    own_start = pl.multiple_of(side * half, LANES)
-    other_start = pl.multiple_of((1 - side) * half, LANES)
-
-    up_copies = []
-    for i, start in enumerate(range(first, units, block)):
-        up_copies.append(
+    early = up_early_ref.shape[0]
+    own_start, other_start = half_starts(half)
+    pending = []
+    for i, start in enumerate(range(block, units, block)):
+        pending.append(
             pltpu.make_async_copy(
-                up_hbm.at[:, pl.ds(start, block)], up_ref.at[i], up_arrival.at[i]
+                down_hbm.at[pl.ds(start, block)],
+                down_late_ref.at[pl.ds(start - block, block)],
+                arrival.at[i],
             )
         )
-    down_copies = []
-    slices = down_ref.shape[0]
-    piece = down_ref.shape[2]
-    for i in range(slices):
-        base = other_start if i < slices // 2 else own_start
-        start = pl.multiple_of(base + (i % (slices // 2)) * piece, LANES)
-        down_copies.append(
-            pltpu.make_async_copy(
-                down_hbm.at[:, pl.ds(start, piece)], down_ref.at[i], down_arrival.at[i]
-            )
-        )
-    copies = up_copies + down_copies
-    for copy in copies[:AHEAD]:
+    copies = list(pending)
+    for copy in copies:
         copy.start()
-
-    def wait(i):
-        copies[i].wait()
-        if i + AHEAD < len(copies):
-            copies[i + AHEAD].start()
-
-    def rows_of(refs):
-        tall = [ref[...].astype(jnp.float32).reshape(-1, half) for ref in refs]
-        return jnp.concatenate(tall, axis=0)
 
     own, other = rows_of(own_refs), rows_of(other_refs)
     squares = jnp.sum(own * own, axis=-1, keepdims=True) + jnp.sum(
         other * other, axis=-1, keepdims=True
     )
     inv_rms = lax.rsqrt(squares / width + 1e-05)
-    normed[:, pl.ds(own_start, half)] = (own * inv_rms).astype(jnp.bfloat16)
-    normed[:, pl.ds(other_start, half)] = (other * inv_rms).astype(jnp.bfloat16)
+    other = other.astype(jnp.bfloat16)
+    rows_ref[:, pl.ds(own_start, half)] = own.astype(jnp.bfloat16)
+    rows_ref[:, pl.ds(other_start, half)] = other
 
     for start in range(0, units, block):
         part = slice(start, start + block)
-        gate = jnp.dot(normed[...], gate_ref[:, part], preferred_element_type=jnp.float32)
-        gates[:, part] = jax.nn.silu(gate)
-    for start in range(0, units, block):
-        part = slice(start, start + block)
-        if start < first:
-            held = first_up_ref[:, part]
-        else:
-            i = (start - first) // block
-            wait(i)
-            held = up_ref[i]
-        up = jnp.dot(normed[...], held, preferred_element_type=jnp.float32)
-        units_bf[:, part] = (gates[:, part] * up).astype(jnp.bfloat16)
-    rows = count // len(offsets)
-    for i in range(slices):
-        wait(len(up_copies) + i)
-        product = jnp.dot(units_bf[...], down_ref[i], preferred_element_type=jnp.float32)
-        columns = slice(i % (slices // 2) * piece, (i % (slices // 2) + 1) * piece)
-        target = sent_ref if i < slices // 2 else kept_ref
-        for j, offset in enumerate(offsets):
-            target[lax.bitwise_xor(me, offset), :, columns] = product[
-                j * rows : (j + 1) * rows
-            ].astype(target.dtype)
+        gate = gates_ref[:, part] + jnp.dot(
+            other, gate_ref[pl.ds(other_start, half), part], preferred_element_type=jnp.float32
+        )
+        gate = jax.nn.silu(gate * inv_rms) * inv_rms
+        up = jnp.dot(
+            rows_ref[:, :early], up_early_ref[:, part], preferred_element_type=jnp.float32
+        ) + jnp.dot(
+            rows_ref[:, early:], up_late_ref[:, part], preferred_element_type=jnp.float32
+        )
+        units_ref[:, part] = (gate * up).astype(jnp.bfloat16)
+    for copy in copies:
+        copy.wait()
+    downs = [down_early_ref] + [down_late_ref] * (units > block)
+    for start in range(0, half, piece):
+        columns = pl.ds(pl.multiple_of(other_start + start, LANES), piece)
+        product = down_dot(units_ref, downs, columns)
+        store_rows(offsets, sent_ref, slice(start, start + piece), product)
+
+
+def keep_kernel(block, piece, offsets, units_ref, down_early_ref, down_late_ref, kept_ref):
+    half = kept_ref.shape[-1]
+    own_start, _ = half_starts(half)
+    downs = [down_early_ref] + [down_late_ref] * (units_ref.shape[1] > block)
+    for start in range(0, half, piece):
+        columns = pl.ds(pl.multiple_of(own_start + start, LANES), piece)
+        product = down_dot(units_ref, downs, columns)
+        store_rows(offsets, kept_ref, slice(start, start + piece), product)
+
+
+def add_kernel(kept_ref, received_ref, out_ref):
+    out_ref[...] = (kept_ref[...] + received_ref[...].astype(jnp.float32)).astype(jnp.bfloat16)
 
 
 def combine_kernel(
@@ -260,20 +305,23 @@
     return pltpu.with_memory_space_constraint(array, pltpu.HBM)
 
 
-def fetch(meta, weights, columns, after=None):
-    after = meta if after is None else after
-    near = jax.ShapeDtypeStruct((weights.shape[0], columns), weights.dtype)
-    return pl.pallas_call(
-        fetch_kernel,
-        in_specs=[VMEM, VMEM, HBM],
-        out_specs=[VMEM, VMEM],
-        out_shape=[near, jax.ShapeDtypeStruct(meta.shape, meta.dtype)],
-        scratch_shapes=[pltpu.SemaphoreType.DMA],
+def fetch(meta, after, *wanted):
+    near = [
+        jax.ShapeDtypeStruct((count, weights.shape[1]), weights.dtype)
+        for weights, _, count in wanted
+    ]
+    *loaded, meta = pl.pallas_call(
+        functools.partial(fetch_kernel, [start for _, start, _ in wanted]),
+        in_specs=[VMEM, VMEM] + [HBM] * len(wanted),
+        out_specs=[VMEM] * (len(wanted) + 1),
+        out_shape=near + [jax.ShapeDtypeStruct(meta.shape, meta.dtype)],
+        scratch_shapes=[pltpu.SemaphoreType.DMA((len(wanted),))],
         compiler_params=pltpu.CompilerParams(vmem_limit_bytes=1 << 20),
         cost_estimate=pl.CostEstimate(
-            flops=0, bytes_accessed=2 * near.size, transcendentals=0
+            flops=0, bytes_accessed=2 * sum(array.size for array in near), transcendentals=0
         ),
-    )(after, meta, far(weights))
+    )(after, meta, *[far(weights) for weights, _, _ in wanted])
+    return loaded, meta
 
 
 def swap_devices(value, offset, devices):
@@ -300,10 +348,16 @@
         jnp.transpose(router),
         jnp.transpose(routes, (0, 2, 1)),
     )
+    width, units = w_gate.shape
+    block = min(512, units)
+    early = width // 4
+    piece = min(512, half)
+    count = devices * rows
+    owners = devices // experts
     hidden, meta = pl.pallas_call(
         attend_kernel,
         in_specs=[HBM] * 7,
-        out_specs=[VMEM, VMEM],
+        out_specs=[VMEM] * 2,
         out_shape=[
             jax.ShapeDtypeStruct((rows, half), jnp.bfloat16),
             jax.ShapeDtypeStruct((rows, LANES), jnp.float32),
@@ -315,16 +369,11 @@
         + [pltpu.SemaphoreType.DMA((7,))],
         compiler_params=pltpu.CompilerParams(vmem_limit_bytes=16 << 20),
     )(*[far(array) for array in inputs])
-    width, units = w_gate.shape
-    block = min(512, units)
-    first = min(1024, units)
-    piece = min(512, half)
-    count = devices * rows
-    owners = devices // experts
 
     offsets = [k * owners for k in range(experts)]
     crossed = [swap_devices(hidden, offset, devices) for offset in offsets[1:]]
-    gate_near, meta = fetch(meta, w_gate, units)
+    gate_near = pltpu.with_memory_space_constraint(w_gate, pltpu.VMEM)
+    (up_early,), meta = fetch(meta, meta, (w_up, 0, early))
     held = [
         pl.pallas_call(
             stack_kernel,
@@ -341,33 +390,61 @@
         held.append(swap_devices(held[0], step, devices))
         offsets += [offset ^ step for offset in offsets]
         step *= 2
-    up_near, meta = fetch(meta, w_up, first, held[0])
+    (up_late,), meta = fetch(meta, held[0], (w_up, early, width - early))
     others = [swap_cores(held[0])]
     if len(held) > 1:
         held[1], meta = lax.optimization_barrier((held[1], meta))
         others.append(swap_cores(held[1]))
     meta_other = swap_cores(meta)
-    kept, sent = pl.pallas_call(
-        functools.partial(expert_kernel, offsets),
-        in_specs=[VMEM] * (2 * len(held) + 2) + [HBM] * 2,
+    parts = len(held)
+    gates, down_early = pl.pallas_call(
+        functools.partial(gate_kernel, block),
+        in_specs=[VMEM] * (parts + 1) + [HBM],
         out_specs=[VMEM, VMEM],
         out_shape=[
-            jax.ShapeDtypeStruct((devices, rows, half), jnp.float32),
+            jax.ShapeDtypeStruct((count, units), jnp.float32),
+            jax.ShapeDtypeStruct((block, width), jnp.bfloat16),
+        ],
+        scratch_shapes=[pltpu.SemaphoreType.DMA],
+        compiler_params=pltpu.CompilerParams(vmem_limit_bytes=min(48, count // 16) << 20),
+        cost_estimate=pl.CostEstimate(
+            flops=2 * count * half * units, bytes_accessed=2 * half * units, transcendentals=0
+        ),
+    )(*held, gate_near, far(w_down))
+    late = max(block, units - block)
+    sent, units_bf, down_late = pl.pallas_call(
+        functools.partial(expert_kernel, block, piece, offsets, parts),
+        in_specs=[VMEM] * (2 * parts + 6) + [HBM],
+        out_specs=[VMEM] * 3,
+        out_shape=[
             jax.ShapeDtypeStruct((devices, rows, half), jnp.bfloat16),
+            jax.ShapeDtypeStruct((count, units), jnp.bfloat16),
+            jax.ShapeDtypeStruct((late, width), jnp.bfloat16),
         ],
         scratch_shapes=[
             pltpu.VMEM((count, width), jnp.bfloat16),
-            pltpu.VMEM((count, units), jnp.float32),
-            pltpu.VMEM((count, units), jnp.bfloat16),
-            pltpu.VMEM((max(1, (units - first) // block), width, block), jnp.bfloat16),
-            pltpu.VMEM((width // piece, units, piece), jnp.bfloat16),
-            pltpu.SemaphoreType.DMA((max(1, (units - first) // block),)),
-            pltpu.SemaphoreType.DMA((width // piece,)),
+            pltpu.SemaphoreType.DMA((late // block,)),
         ],
-        compiler_params=pltpu.CompilerParams(vmem_limit_bytes=32 << 20),
-    )(*held, *others, gate_near, up_near, far(w_up), far(w_down))
+        compiler_params=pltpu.CompilerParams(vmem_limit_bytes=min(48, count // 8) << 20),
+    )(*held, *others, up_early, up_late, gate_near, gates, down_early, meta_other, far(w_down))
     received = swap_cores(sent)
-    summed = (kept + received.astype(jnp.float32)).astype(jnp.bfloat16)
+    kept = pl.pallas_call(
+        functools.partial(keep_kernel, block, piece, offsets),
+        in_specs=[VMEM] * 3,
+        out_specs=VMEM,
+        out_shape=jax.ShapeDtypeStruct((devices, rows, half), jnp.float32),
+        compiler_params=pltpu.CompilerParams(vmem_limit_bytes=min(48, count // 16) << 20),
+        cost_estimate=pl.CostEstimate(
+            flops=2 * count * half * units, bytes_accessed=2 * half * units, transcendentals=0
+        ),
+    )(units_bf, down_early, down_late)
+    summed = pl.pallas_call(
+        add_kernel,
+        in_specs=[VMEM] * 2,
+        out_specs=VMEM,
+        out_shape=jax.ShapeDtypeStruct((devices, rows, half), jnp.bfloat16),
+        compiler_params=pltpu.CompilerParams(vmem_limit_bytes=min(48, count // 16) << 20),
+    )(kept, received)
     returned = lax.all_to_all(summed, "devs", split_axis=0, concat_axis=0, tiled=True)
     return pl.pallas_call(
         functools.partial(combine_kernel, experts),

time: 46.6 us -> 42.6 us (0.914)
  blocking collectives: 0 us -> 12.4 us
  waiting for transfers between devices: 11.8 us -> 2.03 us
  starting transfers between devices: 12.9 us -> 8.46 us
  Pallas kernels: 20.8 us -> 19.3 us
  other arithmetic: 0.71 us -> 0.01 us
    all_to_all x0 -> x1, blocking collectives: none -> 12.4 us  [on_device(): lax.all_to_all(summed, 'devs', split_axis=0, concat_axis=0, tiled=True)]
    all_to_all x1 -> x0, waiting for transfers between devices: 7.11 us -> none  [on_device(): lax.all_to_all(summed, 'devs', split_axis=0, concat_axis=0, tiled=True)]
    all_to_all x1 -> x0, starting transfers between devices: 5.03 us -> none  [on_device(): lax.all_to_all(summed, 'devs', split_axis=0, concat_axis=0, tiled=True)]
    ppermute x4, waiting for transfers between devices: 3.38 us -> 0.01 us  [swap_cores(): return lax.ppermute(value, 'pair', [(0, 1), (1, 0)])]
    pallas_call x4 -> x7, Pallas kernels: 19.9 us -> 18.3 us  [the longest x1 6.87 us: on_device(): pl.pallas_call(functools.partial(expert_kernel, block, piece, offsets, pa...]
    convert_element_type x1 -> x0, other arithmetic: 0.71 us -> none  [on_device(): summed = (kept + received.astype(jnp.float32)).astype(jnp.bfloat16)]
    ppermute x4, waiting for transfers between devices: 1.34 us -> 2.02 us  [swap_devices(): lax.ppermute(value, 'devs', [(d, d ^ offset) for d in range(devices)])]
    ppermute x4, starting transfers between devices: 0.59 us -> 1.15 us  [swap_cores(): return lax.ppermute(value, 'pair', [(0, 1), (1, 0)])]
  transfers between devices with their start and end apart: 9 -> 8, of which waited for: 6 -> 1; matrix products, arithmetic and copies ran while one was open for 0% -> 0% of each run, Pallas kernels for 16% -> 21%
where the time goes in v3:
time: 42.6 us; the launch traced here: 42.3 us
  Pallas kernels  19.3 us (45%)
  blocking collectives  12.4 us (29%)
  starting transfers between devices  8.46 us (20%)
  waiting for transfers between devices  2.03 us (5%)
    all_to_all x1, blocking collectives, on_device(): lax.all_to_all(summed, 'devs', split_axis=0, concat_axis=0, tiled=True)  12.4 us
    ppermute x4, starting transfers between devices, swap_devices(): lax.ppermute(value, 'devs', [(d, d ^ offset) for d in range(devices)])  7.31 us
    pallas_call x1, Pallas kernels, on_device(): pl.pallas_call(functools.partial(expert_kernel, block, piece, offsets, pa...  6.87 us
    pallas_call x2, Pallas kernels, fetch(): pl.pallas_call(functools.partial(fetch_kernel, [start for _, start, _ in...  5.74 us
    pallas_call x1, Pallas kernels, on_device(): pl.pallas_call(attend_kernel, in_specs=[HBM] * 7, out_specs=[VMEM] * 2, o...  2.57 us
    ppermute x4, waiting for transfers between devices, swap_devices(): lax.ppermute(value, 'devs', [(d, d ^ offset) for d in range(devices)])  2.02 us
    pallas_call x1, Pallas kernels, on_device(): pl.pallas_call(functools.partial(gate_kernel, block), in_specs=[VMEM] * (...  1.9 us
    pallas_call x1, Pallas kernels, on_device(): pl.pallas_call(functools.partial(keep_kernel, block, piece, offsets), in_...  1.22 us
  transfers between devices with their start and end apart: 8, of which 1 were waited for; matrix products, arithmetic and copies ran while one was open for 0% of the time, Pallas kernels for 21%

profile of v3, /device:TPU:0, one launch (start us, length us, event | category | flops | bytes accessed | tf_op | source)
XLA Modules:
  0.0 42.3 jit_solution(15628294059307782122)
XLA Ops:
  0.0 2.6 %shard_map.100 = (bf16[8,1536]{1,0:T(8,128)(2,1)S(1)}, f32[8,128]{1,0:T(8,128)S(1)}) custom-call(bf16[2,4,1536]{2,1,0:T(4,128)(2,1)} %query_hbm.1, bf16[2,4,256,256]{3,2,1,0:T(8,128)(2,1)} %key_hbm.1, bf16[2,4,256,256]{3,2,1,0:T(8,128)(2,1)} %value_hbm.1, s32[2,4]{1,0:T(2,128)} %lengths_hbm.1, bf16[2,4,1536]{2,1,0:T(4,128)(2,1)} %residual_hbm.1, ...), custom_call_target="tpu_custom_call" | custom-call | tf_op jit(solution)/shard_map/pallas_call | solution.py:357
  2.6 5.1 %collective-permute-start.2 = (bf16[8,1536]{1,0:T(8,128)(2,1)S(1)}, bf16[8,1536]{1,0:T(8,128)(2,1)S(1)}, u32[]{:S(2)}, u32[]{:S(2)}) collective-permute-start(bf16[8,1536]{1,0:T(8,128)(2,1)S(1)} %get-tuple-element.18.refs_0_.hidden_ref), channel_id=1, source_target_pairs={{0,12},{2,14},{4,8},{6,10},{8,4},{10,6},{12,0},{14,2},{1,13},{3,15... | collective-permute-start | bytes 73736 | tf_op jit(solution)/shard_map/ppermute | solution.py:328
  7.7 0.0 collective-permute-start.1
  7.7 0.6 %collective-permute-start = (bf16[8,1536]{1,0:T(8,128)(2,1)S(1)}, bf16[8,1536]{1,0:T(8,128)(2,1)S(1)}, u32[]{:S(2)}, u32[]{:S(2)}) collective-permute-start(bf16[8,1536]{1,0:T(8,128)(2,1)S(1)} %get-tuple-element.18.refs_0_.hidden_ref), channel_id=1, source_target_pairs={{0,4},{2,6},{4,0},{6,2},{8,12},{10,14},{12,8},{14,10},{1,5},{3,7},... | collective-permute-start | bytes 73736 | tf_op jit(solution)/shard_map/ppermute | solution.py:328
  8.3 2.0 %shard_map.101 = (bf16[768,2048]{1,0:T(8,128)(2,1)S(1)}, f32[8,128]{1,0:T(8,128)S(1)}) custom-call(f32[8,128]{1,0:T(8,128)S(1)} %get-tuple-element.19.after_ref.meta_ref, f32[8,128]{1,0:T(8,128)S(1)} %get-tuple-element.19.after_ref.meta_ref, bf16[3072,2048]{1,0:T(8,128)(2,1)} %refs_0_.3), custom_call_target="tpu_custom_call" | custom-call | bytes 3145728 | tf_op jit(solution)/shard_map/pallas_call | solution.py:313
  10.4 0.0 collective-permute-done.2.refs_3_
  10.4 2.0 %collective-permute-done.1.refs_2_ = bf16[8,1536]{1,0:T(8,128)(2,1)S(1)} collective-permute-done((bf16[8,1536]{1,0:T(8,128)(2,1)S(1)}, bf16[8,1536]{1,0:T(8,128)(2,1)S(1)}, u32[]{:S(2)}, u32[]{:S(2)}) %collective-permute-start.1) | collective-permute-done | bytes 24608 | tf_op jit(solution)/shard_map/ppermute | solution.py:328
  12.4 0.0 collective-permute-done.refs_1_
  12.4 0.0 slice-start.2
  12.5 1.6 %collective-permute-start.3 = (bf16[4,8,1536]{2,1,0:T(8,128)(2,1)S(1)}, bf16[4,8,1536]{2,1,0:T(8,128)(2,1)S(1)}, u32[]{:S(2)}, u32[]{:S(2)}) collective-permute-start(bf16[4,8,1536]{2,1,0:T(8,128)(2,1)S(1)} %shard_map.102.after_ref.refs_0_), channel_id=1, source_target_pairs={{0,2},{2,0},{4,6},{6,4},{8,10},{10,8},{12,14},{14,12},{1,3},{3,1},... | collective-permute-start | bytes 294920 | tf_op jit(solution)/shard_map/ppermute | solution.py:328
  14.0 0.0 collective-permute-start.4
  14.0 3.7 %shard_map.103 = (bf16[2304,2048]{1,0:T(8,128)(2,1)S(1)}, f32[8,128]{1,0:T(8,128)S(1)}) custom-call(bf16[4,8,1536]{2,1,0:T(8,128)(2,1)S(1)} %shard_map.102.after_ref.refs_0_, f32[8,128]{1,0:T(8,128)S(1)} %get-tuple-element.20.refs_4_.meta_ref, bf16[3072,2048]{1,0:T(8,128)(2,1)} %refs_0_.3), custom_call_target="tpu_custom_call" | custom-call | bytes 9437184 | tf_op jit(solution)/shard_map/pallas_call | solution.py:313
  17.7 0.0 collective-permute-done.3.refs_1_
  17.7 0.6 %collective-permute-start.5 = (bf16[4,8,1536]{2,1,0:T(8,128)(2,1)S(1)}, bf16[4,8,1536]{2,1,0:T(8,128)(2,1)S(1)}, u32[]{:S(2)}, u32[]{:S(2)}) collective-permute-start(bf16[4,8,1536]{2,1,0:T(8,128)(2,1)S(1)} %collective-permute-done.3.refs_1_), channel_id=1, source_target_pairs={{0,1},{1,0},{2,3},{3,2},{4,5},{5,4},{6,7},{7,6},{8,9},{9,8},{10,11... | collective-permute-start | bytes 294920 | tf_op jit(solution)/shard_map/ppermute | solution.py:332
  18.3 0.1 collective-permute-start.6
  18.4 1.9 %shard_map.104 = (f32[64,2048]{1,0:T(8,128)S(1)}, bf16[512,3072]{1,0:T(8,128)(2,1)S(1)}) custom-call(bf16[4,8,1536]{2,1,0:T(8,128)(2,1)S(1)} %shard_map.102.after_ref.refs_0_, bf16[4,8,1536]{2,1,0:T(8,128)(2,1)S(1)} %collective-permute-done.3.refs_1_, bf16[3072,2048]{1,0:T(8,128)(2,1)S(1)} %bitcast.3, bf16[2048,3072]{1,0:T(8,128)(2,1)} %refs_10_.1), custom_call_target="tpu_custom_call" | custom-call | flops 402653184 | bytes 6291456 | tf_op jit(solution)/shard_map/pallas_call | solution.py:400
  20.3 0.0 collective-permute-done.4.refs_2_
  20.3 0.0 collective-permute-done.6.refs_9_.meta_other_ref
  20.3 6.9 %shard_map.105 = (bf16[8,8,1536]{2,1,0:T(8,128)(2,1)S(1)}, bf16[64,2048]{1,0:T(8,128)(2,1)S(1)}, bf16[1536,3072]{1,0:T(8,128)(2,1)S(1)}) custom-call(bf16[4,8,1536]{2,1,0:T(8,128)(2,1)S(1)} %shard_map.102.after_ref.refs_0_, bf16[4,8,1536]{2,1,0:T(8,128)(2,1)S(1)} %collective-permute-done.3.refs_1_, bf16[4,8,1536]{2,1,0:T(8,128)(2,1)S(1)} %collective-permute-done.4.refs_2_, ...), custom_call_target="tpu_custom_call" | custom-call | tf_op jit(solution)/shard_map/pallas_call | solution.py:415
  27.2 0.5 %collective-permute-start.7 = (bf16[8,8,1536]{2,1,0:T(8,128)(2,1)S(1)}, bf16[8,8,1536]{2,1,0:T(8,128)(2,1)S(1)}, u32[]{:S(2)}, u32[]{:S(2)}) collective-permute-start(bf16[8,8,1536]{2,1,0:T(8,128)(2,1)S(1)} %get-tuple-element.30), channel_id=1, source_target_pairs={{0,1},{1,0},{2,3},{3,2},{4,5},{5,4},{6,7},{7,6},{8,9},{9,8},{10,11... | collective-permute-start | bytes 589832 | tf_op jit(solution)/shard_map/ppermute | solution.py:332
  27.7 1.2 %shard_map.106.kept_ref = f32[8,8,1536]{2,1,0:T(8,128)S(1)} custom-call(bf16[64,2048]{1,0:T(8,128)(2,1)S(1)} %get-tuple-element.28.units_ref, bf16[512,3072]{1,0:T(8,128)(2,1)S(1)} %get-tuple-element.26.refs_8_.down_early_ref, bf16[1536,3072]{1,0:T(8,128)(2,1)S(1)} %get-tuple-element.29.down_late_ref), custom_call_target="tpu_custom_call" | custom-call | flops 402653184 | bytes 6291456 | tf_op jit(solution)/shard_map/pallas_call | solution.py:431
  28.9 0.0 collective-permute-done.7.received_ref
  29.0 12.4 %all_to_all.5.returned_ref = bf16[8,8,1536]{2,1,0:T(8,128)(2,1)S(1)} all-to-all(bf16[8,8,1536]{2,1,0:T(8,128)(2,1)S(1)} %shard_map.107), channel_id=1, replica_groups=mesh['groups'=2,'devs'=8,'pair'=2] {'devs'}, dimensions={0} | all-to-all | bytes 393216 | tf_op jit(solution)/shard_map/all_to_all | solution.py:448
  41.4 0.9 %shard_map.108 = bf16[2,4,1536]{2,1,0:T(4,128)(2,1)} custom-call(bf16[8,8,1536]{2,1,0:T(8,128)(2,1)S(1)} %all_to_all.5.returned_ref, bf16[8,1536]{1,0:T(8,128)(2,1)S(1)} %get-tuple-element.18.refs_0_.hidden_ref, f32[8,128]{1,0:T(8,128)S(1)} %get-tuple-element.27.meta_ref, f32[8,128]{1,0:T(8,128)S(1)} %collective-permute-done.6.refs_9_.meta_other_ref), custom_call_target="tpu_custom_call" | custom-call | tf_op jit(solution)/shard_map/pallas_call | solution.py:449
  (9 shorter events, 0.1 us)
Async XLA Ops:
  2.6 7.8 %collective-permute-start.2 = (bf16[8,1536]{1,0:T(8,128)(2,1)S(1)}, bf16[8,1536]{1,0:T(8,128)(2,1)S(1)}, u32[]{:S(2)}, u32[]{:S(2)}) collective-permute-start(bf16[8,1536]{1,0:T(8,128)(2,1)S(1)} %get-tuple-element.18.refs_0_.hidden_ref), channel_id=1, source_target_pairs={{0,12},{2,14},{4,8},{6,10},{8,4},{10,6},{12,0},{14,2},{1,13},{3,15... | collective-permute-start | bytes 73736 | tf_op jit(solution)/shard_map/ppermute | solution.py:328
  7.7 4.7 %collective-permute-start.1 = (bf16[8,1536]{1,0:T(8,128)(2,1)S(1)}, bf16[8,1536]{1,0:T(8,128)(2,1)S(1)}, u32[]{:S(2)}, u32[]{:S(2)}) collective-permute-start(bf16[8,1536]{1,0:T(8,128)(2,1)S(1)} %get-tuple-element.18.refs_0_.hidden_ref), channel_id=1, source_target_pairs={{0,8},{2,10},{4,12},{6,14},{8,0},{10,2},{12,4},{14,6},{1,9},{3,11}... | collective-permute-start | bytes 73736 | tf_op jit(solution)/shard_map/ppermute | solution.py:328
  7.7 4.7 %collective-permute-start = (bf16[8,1536]{1,0:T(8,128)(2,1)S(1)}, bf16[8,1536]{1,0:T(8,128)(2,1)S(1)}, u32[]{:S(2)}, u32[]{:S(2)}) collective-permute-start(bf16[8,1536]{1,0:T(8,128)(2,1)S(1)} %get-tuple-element.18.refs_0_.hidden_ref), channel_id=1, source_target_pairs={{0,4},{2,6},{4,0},{6,2},{8,12},{10,14},{12,8},{14,10},{1,5},{3,7},... | collective-permute-start | bytes 73736 | tf_op jit(solution)/shard_map/ppermute | solution.py:328
  8.3 10.0 %slice-start = ((s8[12582912]{0:T(1024)(128)(4,1)}), s8[4194304]{0:T(1024)(128)(4,1)S(1)}, s32[]{:S(2)}) async-start(s8[12582912]{0:T(1024)(128)(4,1)} %bitcast.2), calls=%async_computation.1 | async-start | bytes 8388608
  8.3 10.0 %slice-start.1 = ((s8[12582912]{0:T(1024)(128)(4,1)}), s8[4194304]{0:T(1024)(128)(4,1)S(1)}, s32[]{:S(2)}) async-start(s8[12582912]{0:T(1024)(128)(4,1)} %bitcast.2), calls=%async_computation.2 | async-start | bytes 8388608
  12.4 5.9 %slice-start.2 = ((s8[12582912]{0:T(1024)(128)(4,1)}), s8[4194304]{0:T(1024)(128)(4,1)S(1)}, s32[]{:S(2)}) async-start(s8[12582912]{0:T(1024)(128)(4,1)} %bitcast.2), calls=%async_computation.3 | async-start | bytes 8388608
  12.5 5.3 %collective-permute-start.3 = (bf16[4,8,1536]{2,1,0:T(8,128)(2,1)S(1)}, bf16[4,8,1536]{2,1,0:T(8,128)(2,1)S(1)}, u32[]{:S(2)}, u32[]{:S(2)}) collective-permute-start(bf16[4,8,1536]{2,1,0:T(8,128)(2,1)S(1)} %shard_map.102.after_ref.refs_0_), channel_id=1, source_target_pairs={{0,2},{2,0},{4,6},{6,4},{8,10},{10,8},{12,14},{14,12},{1,3},{3,1},... | collective-permute-start | bytes 294920 | tf_op jit(solution)/shard_map/ppermute | solution.py:328
  14.0 6.3 %collective-permute-start.4 = (bf16[4,8,1536]{2,1,0:T(8,128)(2,1)S(1)}, bf16[4,8,1536]{2,1,0:T(8,128)(2,1)S(1)}, u32[]{:S(2)}, u32[]{:S(2)}) collective-permute-start(bf16[4,8,1536]{2,1,0:T(8,128)(2,1)S(1)} %shard_map.102.after_ref.refs_0_), channel_id=1, source_target_pairs={{0,1},{1,0},{2,3},{3,2},{4,5},{5,4},{6,7},{7,6},{8,9},{9,8},{10,11... | collective-permute-start | bytes 294920 | tf_op jit(solution)/shard_map/ppermute | solution.py:332
  17.7 2.6 %collective-permute-start.5 = (bf16[4,8,1536]{2,1,0:T(8,128)(2,1)S(1)}, bf16[4,8,1536]{2,1,0:T(8,128)(2,1)S(1)}, u32[]{:S(2)}, u32[]{:S(2)}) collective-permute-start(bf16[4,8,1536]{2,1,0:T(8,128)(2,1)S(1)} %collective-permute-done.3.refs_1_), channel_id=1, source_target_pairs={{0,1},{1,0},{2,3},{3,2},{4,5},{5,4},{6,7},{7,6},{8,9},{9,8},{10,11... | collective-permute-start | bytes 294920 | tf_op jit(solution)/shard_map/ppermute | solution.py:332
  18.3 2.0 %collective-permute-start.6 = (f32[8,128]{1,0:T(8,128)S(1)}, f32[8,128]{1,0:T(8,128)S(1)}, u32[]{:S(2)}, u32[]{:S(2)}) collective-permute-start(f32[8,128]{1,0:T(8,128)S(1)} %get-tuple-element.27.meta_ref), channel_id=1, source_target_pairs={{0,1},{1,0},{2,3},{3,2},{4,5},{5,4},{6,7},{7,6},{8,9},{9,8},{10,11... | collective-permute-start | bytes 12296 | tf_op jit(solution)/shard_map/ppermute | solution.py:332
  27.2 1.7 %collective-permute-start.7 = (bf16[8,8,1536]{2,1,0:T(8,128)(2,1)S(1)}, bf16[8,8,1536]{2,1,0:T(8,128)(2,1)S(1)}, u32[]{:S(2)}, u32[]{:S(2)}) collective-permute-start(bf16[8,8,1536]{2,1,0:T(8,128)(2,1)S(1)} %get-tuple-element.30), channel_id=1, source_target_pairs={{0,1},{1,0},{2,3},{3,2},{4,5},{5,4},{6,7},{7,6},{8,9},{9,8},{10,11... | collective-permute-start | bytes 589832 | tf_op jit(solution)/shard_map/ppermute | solution.py:332

commit v4 on v3

--- a/solution.py
+++ b/solution.py
@@ -154,19 +154,16 @@
 
 
 def gate_kernel(block, *refs):
-    *own_refs, gate_ref, down_hbm, gates_ref, down_ref, arrival = refs
+    *own_refs, gate_ref, gates_ref = refs
     half = own_refs[0].shape[-1]
     units = gate_ref.shape[1]
     own_start, _ = half_starts(half)
-    copy = pltpu.make_async_copy(down_hbm.at[pl.ds(0, block)], down_ref, arrival)
-    copy.start()
     rows = rows_of(own_refs).astype(jnp.bfloat16)
     for start in range(0, units, block):
         part = slice(start, start + block)
         gates_ref[:, part] = jnp.dot(
             rows, gate_ref[pl.ds(own_start, half), part], preferred_element_type=jnp.float32
         )
-    copy.wait()
 
 
 def store_rows(offsets, target, columns, product):
@@ -178,52 +175,23 @@
         ].astype(target.dtype)
 
 
-def down_dot(units_ref, down_refs, columns):
-    total, start = None, 0
-    for ref in down_refs:
-        stop = start + ref.shape[0]
-        product = jnp.dot(
-            units_ref[:, start:stop], ref[:, columns], preferred_element_type=jnp.float32
-        )
-        total = product if total is None else total + product
-        start = stop
-    return total
-
-
 def expert_kernel(block, piece, offsets, parts, *refs):
     own_refs, refs = refs[:parts], refs[parts:]
     other_refs, refs = refs[:parts], refs[parts:]
     (
-        up_early_ref,
-        up_late_ref,
+        up_ref,
         gate_ref,
         gates_ref,
-        down_early_ref,
+        down_ref,
         meta_other_ref,
-        down_hbm,
         sent_ref,
         units_ref,
-        down_late_ref,
         rows_ref,
-        arrival,
     ) = refs
     width = rows_ref.shape[1]
     half = width // 2
     units = gate_ref.shape[1]
-    early = up_early_ref.shape[0]
     own_start, other_start = half_starts(half)
-    pending = []
-    for i, start in enumerate(range(block, units, block)):
-        pending.append(
-            pltpu.make_async_copy(
-                down_hbm.at[pl.ds(start, block)],
-                down_late_ref.at[pl.ds(start - block, block)],
-                arrival.at[i],
-            )
-        )
-    copies = list(pending)
-    for copy in copies:
-        copy.start()
 
     own, other = rows_of(own_refs), rows_of(other_refs)
     squares = jnp.sum(own * own, axis=-1, keepdims=True) + jnp.sum(
@@ -240,28 +208,24 @@
             other, gate_ref[pl.ds(other_start, half), part], preferred_element_type=jnp.float32
         )
         gate = jax.nn.silu(gate * inv_rms) * inv_rms
-        up = jnp.dot(
-            rows_ref[:, :early], up_early_ref[:, part], preferred_element_type=jnp.float32
-        ) + jnp.dot(
-            rows_ref[:, early:], up_late_ref[:, part], preferred_element_type=jnp.float32
-        )
+        up = jnp.dot(rows_ref[...], up_ref[:, part], preferred_element_type=jnp.float32)
         units_ref[:, part] = (gate * up).astype(jnp.bfloat16)
-    for copy in copies:
-        copy.wait()
-    downs = [down_early_ref] + [down_late_ref] * (units > block)
     for start in range(0, half, piece):
         columns = pl.ds(pl.multiple_of(other_start + start, LANES), piece)
-        product = down_dot(units_ref, downs, columns)
+        product = jnp.dot(
+            units_ref[...], down_ref[:, columns], preferred_element_type=jnp.float32
+        )
         store_rows(offsets, sent_ref, slice(start, start + piece), product)
 
 
-def keep_kernel(block, piece, offsets, units_ref, down_early_ref, down_late_ref, kept_ref):
+def keep_kernel(piece, offsets, units_ref, down_ref, kept_ref):
     half = kept_ref.shape[-1]
     own_start, _ = half_starts(half)
-    downs = [down_early_ref] + [down_late_ref] * (units_ref.shape[1] > block)
     for start in range(0, half, piece):
         columns = pl.ds(pl.multiple_of(own_start + start, LANES), piece)
-        product = down_dot(units_ref, downs, columns)
+        product = jnp.dot(
+            units_ref[...], down_ref[:, columns], preferred_element_type=jnp.float32
+        )
         store_rows(offsets, kept_ref, slice(start, start + piece), product)
 
 
@@ -305,6 +269,10 @@
     return pltpu.with_memory_space_constraint(array, pltpu.HBM)
 
 
+def near(array):
+    return pltpu.with_memory_space_constraint(array, pltpu.VMEM)
+
+
 def fetch(meta, after, *wanted):
     near = [
         jax.ShapeDtypeStruct((count, weights.shape[1]), weights.dtype)
@@ -350,7 +318,6 @@
     )
     width, units = w_gate.shape
     block = min(512, units)
-    early = width // 4
     piece = min(512, half)
     count = devices * rows
     owners = devices // experts
@@ -372,8 +339,7 @@
 
     offsets = [k * owners for k in range(experts)]
     crossed = [swap_devices(hidden, offset, devices) for offset in offsets[1:]]
-    gate_near = pltpu.with_memory_space_constraint(w_gate, pltpu.VMEM)
-    (up_early,), meta = fetch(meta, meta, (w_up, 0, early))
+    (up_near,), meta = fetch(meta, meta, (w_up, 0, width))
     held = [
         pl.pallas_call(
             stack_kernel,
@@ -390,54 +356,44 @@
         held.append(swap_devices(held[0], step, devices))
         offsets += [offset ^ step for offset in offsets]
         step *= 2
-    (up_late,), meta = fetch(meta, held[0], (w_up, early, width - early))
     others = [swap_cores(held[0])]
     if len(held) > 1:
-        held[1], meta = lax.optimization_barrier((held[1], meta))
         others.append(swap_cores(held[1]))
     meta_other = swap_cores(meta)
     parts = len(held)
-    gates, down_early = pl.pallas_call(
+    w_gate, w_up, w_down = near(w_gate), up_near, near(w_down)
+    gates = pl.pallas_call(
         functools.partial(gate_kernel, block),
-        in_specs=[VMEM] * (parts + 1) + [HBM],
-        out_specs=[VMEM, VMEM],
-        out_shape=[
-            jax.ShapeDtypeStruct((count, units), jnp.float32),
-            jax.ShapeDtypeStruct((block, width), jnp.bfloat16),
-        ],
-        scratch_shapes=[pltpu.SemaphoreType.DMA],
+        in_specs=[VMEM] * (parts + 1),
+        out_specs=VMEM,
+        out_shape=jax.ShapeDtypeStruct((count, units), jnp.float32),
         compiler_params=pltpu.CompilerParams(vmem_limit_bytes=min(48, count // 16) << 20),
         cost_estimate=pl.CostEstimate(
             flops=2 * count * half * units, bytes_accessed=2 * half * units, transcendentals=0
         ),
-    )(*held, gate_near, far(w_down))
-    late = max(block, units - block)
-    sent, units_bf, down_late = pl.pallas_call(
+    )(*held, w_gate)
+    sent, units_bf = pl.pallas_call(
         functools.partial(expert_kernel, block, piece, offsets, parts),
-        in_specs=[VMEM] * (2 * parts + 6) + [HBM],
-        out_specs=[VMEM] * 3,
+        in_specs=[VMEM] * (2 * parts + 5),
+        out_specs=[VMEM] * 2,
         out_shape=[
             jax.ShapeDtypeStruct((devices, rows, half), jnp.bfloat16),
             jax.ShapeDtypeStruct((count, units), jnp.bfloat16),
-            jax.ShapeDtypeStruct((late, width), jnp.bfloat16),
         ],
-        scratch_shapes=[
-            pltpu.VMEM((count, width), jnp.bfloat16),
-            pltpu.SemaphoreType.DMA((late // block,)),
-        ],
+        scratch_shapes=[pltpu.VMEM((count, width), jnp.bfloat16)],
         compiler_params=pltpu.CompilerParams(vmem_limit_bytes=min(48, count // 8) << 20),
-    )(*held, *others, up_early, up_late, gate_near, gates, down_early, meta_other, far(w_down))
+    )(*held, *others, w_up, w_gate, gates, w_down, meta_other)
     received = swap_cores(sent)
     kept = pl.pallas_call(
-        functools.partial(keep_kernel, block, piece, offsets),
-        in_specs=[VMEM] * 3,
+        functools.partial(keep_kernel, piece, offsets),
+        in_specs=[VMEM] * 2,
         out_specs=VMEM,
         out_shape=jax.ShapeDtypeStruct((devices, rows, half), jnp.float32),
         compiler_params=pltpu.CompilerParams(vmem_limit_bytes=min(48, count // 16) << 20),
         cost_estimate=pl.CostEstimate(
             flops=2 * count * half * units, bytes_accessed=2 * half * units, transcendentals=0
         ),
-    )(units_bf, down_early, down_late)
+    )(units_bf, w_down)
     summed = pl.pallas_call(
         add_kernel,
         in_specs=[VMEM] * 2,

time: 42.6 us -> 41.2 us (0.967)
  Pallas kernels: 19.3 us -> 15.5 us
  blocking collectives: 12.4 us -> 14.2 us
  waiting for transfers between devices: 2.03 us -> 3.19 us
    pallas_call x1, Pallas kernels: 6.87 us -> 4.59 us  [on_device(): pl.pallas_call(functools.partial(expert_kernel, block, piece, offsets, pa...]
    all_to_all x1, blocking collectives: 12.4 us -> 14.2 us  [on_device(): lax.all_to_all(summed, 'devs', split_axis=0, concat_axis=0, tiled=True)]
    pallas_call x2 -> x1, Pallas kernels: 5.74 us -> 4.73 us  [fetch(): pl.pallas_call(functools.partial(fetch_kernel, [start for _, start, _ in...]
    ppermute x4, waiting for transfers between devices: 2.02 us -> 2.99 us  [swap_devices(): lax.ppermute(value, 'devs', [(d, d ^ offset) for d in range(devices)])]
    pallas_call x1, Pallas kernels: 1.9 us -> 1.23 us  [on_device(): pl.pallas_call(functools.partial(gate_kernel, block), in_specs=[VMEM] * (...]
    ppermute x4, starting transfers between devices: 1.15 us -> 0.58 us  [swap_cores(): return lax.ppermute(value, 'pair', [(0, 1), (1, 0)])]
  transfers between devices with their start and end apart: 8 -> 8, of which waited for: 1 -> 2; matrix products, arithmetic and copies ran while one was open for 0% -> 0% of each run, Pallas kernels for 21% -> 18%
where the time goes in v4:
time: 41.2 us; the launch traced here: 41 us
  Pallas kernels  15.5 us (38%)
  blocking collectives  14.2 us (34%)
  starting transfers between devices  8.04 us (20%)
  waiting for transfers between devices  3.19 us (8%)
    all_to_all x1, blocking collectives, on_device(): lax.all_to_all(summed, 'devs', split_axis=0, concat_axis=0, tiled=True)  14.2 us
    ppermute x4, starting transfers between devices, swap_devices(): lax.ppermute(value, 'devs', [(d, d ^ offset) for d in range(devices)])  7.46 us
    pallas_call x1, Pallas kernels, fetch(): pl.pallas_call(functools.partial(fetch_kernel, [start for _, start, _ in...  4.73 us
    pallas_call x1, Pallas kernels, on_device(): pl.pallas_call(functools.partial(expert_kernel, block, piece, offsets, pa...  4.59 us
    ppermute x4, waiting for transfers between devices, swap_devices(): lax.ppermute(value, 'devs', [(d, d ^ offset) for d in range(devices)])  2.99 us
    pallas_call x1, Pallas kernels, on_device(): pl.pallas_call(attend_kernel, in_specs=[HBM] * 7, out_specs=[VMEM] * 2, o...  2.72 us
    pallas_call x1, Pallas kernels, on_device(): pl.pallas_call(functools.partial(keep_kernel, piece, offsets), in_specs=[...  1.23 us
    pallas_call x1, Pallas kernels, on_device(): pl.pallas_call(functools.partial(gate_kernel, block), in_specs=[VMEM] * (...  1.23 us
  transfers between devices with their start and end apart: 8, of which 2 were waited for; matrix products, arithmetic and copies ran while one was open for 0% of the time, Pallas kernels for 18%

profile of v4, /device:TPU:0, one launch (start us, length us, event | category | flops | bytes accessed | tf_op | source)
XLA Modules:
  0.0 41.0 jit_solution(11925262453272340520)
XLA Ops:
  0.0 2.7 %shard_map.100 = (bf16[8,1536]{1,0:T(8,128)(2,1)S(1)}, f32[8,128]{1,0:T(8,128)S(1)}) custom-call(bf16[2,4,1536]{2,1,0:T(4,128)(2,1)} %query_hbm.1, bf16[2,4,256,256]{3,2,1,0:T(8,128)(2,1)} %key_hbm.1, bf16[2,4,256,256]{3,2,1,0:T(8,128)(2,1)} %value_hbm.1, s32[2,4]{1,0:T(2,128)} %lengths_hbm.1, bf16[2,4,1536]{2,1,0:T(4,128)(2,1)} %residual_hbm.1, ...), custom_call_target="tpu_custom_call" | custom-call | tf_op jit(solution)/shard_map/pallas_call | solution.py:324
  2.7 5.1 %collective-permute-start.2 = (bf16[8,1536]{1,0:T(8,128)(2,1)S(1)}, bf16[8,1536]{1,0:T(8,128)(2,1)S(1)}, u32[]{:S(2)}, u32[]{:S(2)}) collective-permute-start(bf16[8,1536]{1,0:T(8,128)(2,1)S(1)} %get-tuple-element.11.refs_0_.hidden_ref), channel_id=1, source_target_pairs={{0,12},{2,14},{4,8},{6,10},{8,4},{10,6},{12,0},{14,2},{1,13},{3,15... | collective-permute-start | bytes 73736 | tf_op jit(solution)/shard_map/ppermute | solution.py:296
  7.8 0.0 collective-permute-start.1
  7.9 0.6 %collective-permute-start = (bf16[8,1536]{1,0:T(8,128)(2,1)S(1)}, bf16[8,1536]{1,0:T(8,128)(2,1)S(1)}, u32[]{:S(2)}, u32[]{:S(2)}) collective-permute-start(bf16[8,1536]{1,0:T(8,128)(2,1)S(1)} %get-tuple-element.11.refs_0_.hidden_ref), channel_id=1, source_target_pairs={{0,4},{2,6},{4,0},{6,2},{8,12},{10,14},{12,8},{14,10},{1,5},{3,7},... | collective-permute-start | bytes 73736 | tf_op jit(solution)/shard_map/ppermute | solution.py:296
  8.5 4.7 %shard_map.101 = (bf16[3072,2048]{1,0:T(8,128)(2,1)S(1)}, f32[8,128]{1,0:T(8,128)S(1)}) custom-call(f32[8,128]{1,0:T(8,128)S(1)} %get-tuple-element.12.after_ref.meta_ref, f32[8,128]{1,0:T(8,128)S(1)} %get-tuple-element.12.after_ref.meta_ref, bf16[3072,2048]{1,0:T(8,128)(2,1)} %refs_0_.1), custom_call_target="tpu_custom_call" | custom-call | bytes 12582912 | tf_op jit(solution)/shard_map/pallas_call | solution.py:281
  13.2 0.0 collective-permute-done.2.refs_3_
  13.2 0.0 collective-permute-done.1.refs_2_
  13.3 0.0 collective-permute-done.refs_1_
  13.3 1.7 %collective-permute-start.3 = (bf16[4,8,1536]{2,1,0:T(8,128)(2,1)S(1)}, bf16[4,8,1536]{2,1,0:T(8,128)(2,1)S(1)}, u32[]{:S(2)}, u32[]{:S(2)}) collective-permute-start(bf16[4,8,1536]{2,1,0:T(8,128)(2,1)S(1)} %shard_map.102.refs_0_), channel_id=1, source_target_pairs={{0,2},{2,0},{4,6},{6,4},{8,10},{10,8},{12,14},{14,12},{1,3},{3,1},... | collective-permute-start | bytes 294920 | tf_op jit(solution)/shard_map/ppermute | solution.py:296
  15.0 0.0 collective-permute-start.4
  15.0 3.0 %collective-permute-done.3.refs_1_ = bf16[4,8,1536]{2,1,0:T(8,128)(2,1)S(1)} collective-permute-done((bf16[4,8,1536]{2,1,0:T(8,128)(2,1)S(1)}, bf16[4,8,1536]{2,1,0:T(8,128)(2,1)S(1)}, u32[]{:S(2)}, u32[]{:S(2)}) %collective-permute-start.3) | collective-permute-done | bytes 98336 | tf_op jit(solution)/shard_map/ppermute | solution.py:296
  18.0 0.0 collective-permute-start.5
  18.0 0.5 %collective-permute-start.6 = (f32[8,128]{1,0:T(8,128)S(1)}, f32[8,128]{1,0:T(8,128)S(1)}, u32[]{:S(2)}, u32[]{:S(2)}) collective-permute-start(f32[8,128]{1,0:T(8,128)S(1)} %get-tuple-element.13.refs_4_.meta_ref), channel_id=1, source_target_pairs={{0,1},{1,0},{2,3},{3,2},{4,5},{5,4},{6,7},{7,6},{8,9},{9,8},{10,11... | collective-permute-start | bytes 12296 | tf_op jit(solution)/shard_map/ppermute | solution.py:300
  18.5 0.0 copy-done
  18.5 1.2 %shard_map.103.refs_6_ = f32[64,2048]{1,0:T(8,128)S(1)} custom-call(bf16[4,8,1536]{2,1,0:T(8,128)(2,1)S(1)} %shard_map.102.refs_0_, bf16[4,8,1536]{2,1,0:T(8,128)(2,1)S(1)} %collective-permute-done.3.refs_1_, bf16[3072,2048]{1,0:T(8,128)(2,1)S(1)} %copy-done), custom_call_target="tpu_custom_call" | custom-call | flops 402653184 | bytes 6291456 | tf_op jit(solution)/shard_map/pallas_call | solution.py:365
  19.7 0.0 collective-permute-done.6.refs_8_.meta_other_ref
  19.7 0.0 collective-permute-done.4.refs_2_
  19.7 0.0 collective-permute-done.5.refs_3_
  19.8 4.6 %shard_map.104 = (bf16[8,8,1536]{2,1,0:T(8,128)(2,1)S(1)}, bf16[64,2048]{1,0:T(8,128)(2,1)S(1)}) custom-call(bf16[4,8,1536]{2,1,0:T(8,128)(2,1)S(1)} %shard_map.102.refs_0_, bf16[4,8,1536]{2,1,0:T(8,128)(2,1)S(1)} %collective-permute-done.3.refs_1_, bf16[4,8,1536]{2,1,0:T(8,128)(2,1)S(1)} %collective-permute-done.4.refs_2_, ...), custom_call_target="tpu_custom_call" | custom-call | tf_op jit(solution)/shard_map/pallas_call | solution.py:375
  24.4 0.1 collective-permute-start.7
  24.4 1.2 %shard_map.105.kept_ref = f32[8,8,1536]{2,1,0:T(8,128)S(1)} custom-call(bf16[64,2048]{1,0:T(8,128)(2,1)S(1)} %get-tuple-element.15.units_ref, bf16[2048,3072]{1,0:T(8,128)(2,1)S(1)} %copy-done.1), custom_call_target="tpu_custom_call" | custom-call | flops 402653184 | bytes 6291456 | tf_op jit(solution)/shard_map/pallas_call | solution.py:387
  25.7 0.2 collective-permute-done.7.received_ref
  25.9 14.2 %all_to_all.5.returned_ref = bf16[8,8,1536]{2,1,0:T(8,128)(2,1)S(1)} all-to-all(bf16[8,8,1536]{2,1,0:T(8,128)(2,1)S(1)} %shard_map.106), channel_id=1, replica_groups=mesh['groups'=2,'devs'=8,'pair'=2] {'devs'}, dimensions={0} | all-to-all | bytes 393216 | tf_op jit(solution)/shard_map/all_to_all | solution.py:404
  40.1 0.9 %shard_map.107 = bf16[2,4,1536]{2,1,0:T(4,128)(2,1)} custom-call(bf16[8,8,1536]{2,1,0:T(8,128)(2,1)S(1)} %all_to_all.5.returned_ref, bf16[8,1536]{1,0:T(8,128)(2,1)S(1)} %get-tuple-element.11.refs_0_.hidden_ref, f32[8,128]{1,0:T(8,128)S(1)} %get-tuple-element.13.refs_4_.meta_ref, f32[8,128]{1,0:T(8,128)S(1)} %collective-permute-done.6.refs_8_.meta_other_ref), custom_call_target="tpu_custom_call" | custom-call | tf_op jit(solution)/shard_map/pallas_call | solution.py:405
  (5 shorter events, 0.1 us)
Async XLA Ops:
  0.0 18.5 %copy-start = (bf16[3072,2048]{1,0:T(8,128)(2,1)S(1)}, bf16[3072,2048]{1,0:T(8,128)(2,1)}, u32[]{:S(2)}) copy-start(bf16[3072,2048]{1,0:T(8,128)(2,1)} %refs_5_.1) | copy-start | bytes 37748740
  2.7 10.5 %collective-permute-start.2 = (bf16[8,1536]{1,0:T(8,128)(2,1)S(1)}, bf16[8,1536]{1,0:T(8,128)(2,1)S(1)}, u32[]{:S(2)}, u32[]{:S(2)}) collective-permute-start(bf16[8,1536]{1,0:T(8,128)(2,1)S(1)} %get-tuple-element.11.refs_0_.hidden_ref), channel_id=1, source_target_pairs={{0,12},{2,14},{4,8},{6,10},{8,4},{10,6},{12,0},{14,2},{1,13},{3,15... | collective-permute-start | bytes 73736 | tf_op jit(solution)/shard_map/ppermute | solution.py:296
  7.8 5.4 %collective-permute-start.1 = (bf16[8,1536]{1,0:T(8,128)(2,1)S(1)}, bf16[8,1536]{1,0:T(8,128)(2,1)S(1)}, u32[]{:S(2)}, u32[]{:S(2)}) collective-permute-start(bf16[8,1536]{1,0:T(8,128)(2,1)S(1)} %get-tuple-element.11.refs_0_.hidden_ref), channel_id=1, source_target_pairs={{0,8},{2,10},{4,12},{6,14},{8,0},{10,2},{12,4},{14,6},{1,9},{3,11}... | collective-permute-start | bytes 73736 | tf_op jit(solution)/shard_map/ppermute | solution.py:296
  7.9 5.4 %collective-permute-start = (bf16[8,1536]{1,0:T(8,128)(2,1)S(1)}, bf16[8,1536]{1,0:T(8,128)(2,1)S(1)}, u32[]{:S(2)}, u32[]{:S(2)}) collective-permute-start(bf16[8,1536]{1,0:T(8,128)(2,1)S(1)} %get-tuple-element.11.refs_0_.hidden_ref), channel_id=1, source_target_pairs={{0,4},{2,6},{4,0},{6,2},{8,12},{10,14},{12,8},{14,10},{1,5},{3,7},... | collective-permute-start | bytes 73736 | tf_op jit(solution)/shard_map/ppermute | solution.py:296
  8.5 11.3 %copy-start.1 = (bf16[2048,3072]{1,0:T(8,128)(2,1)S(1)}, bf16[2048,3072]{1,0:T(8,128)(2,1)}, u32[]{:S(2)}) copy-start(bf16[2048,3072]{1,0:T(8,128)(2,1)} %down_ref.1) | copy-start | bytes 37748740
  13.3 4.7 %collective-permute-start.3 = (bf16[4,8,1536]{2,1,0:T(8,128)(2,1)S(1)}, bf16[4,8,1536]{2,1,0:T(8,128)(2,1)S(1)}, u32[]{:S(2)}, u32[]{:S(2)}) collective-permute-start(bf16[4,8,1536]{2,1,0:T(8,128)(2,1)S(1)} %shard_map.102.refs_0_), channel_id=1, source_target_pairs={{0,2},{2,0},{4,6},{6,4},{8,10},{10,8},{12,14},{14,12},{1,3},{3,1},... | collective-permute-start | bytes 294920 | tf_op jit(solution)/shard_map/ppermute | solution.py:296
  15.0 4.7 %collective-permute-start.4 = (bf16[4,8,1536]{2,1,0:T(8,128)(2,1)S(1)}, bf16[4,8,1536]{2,1,0:T(8,128)(2,1)S(1)}, u32[]{:S(2)}, u32[]{:S(2)}) collective-permute-start(bf16[4,8,1536]{2,1,0:T(8,128)(2,1)S(1)} %shard_map.102.refs_0_), channel_id=1, source_target_pairs={{0,1},{1,0},{2,3},{3,2},{4,5},{5,4},{6,7},{7,6},{8,9},{9,8},{10,11... | collective-permute-start | bytes 294920 | tf_op jit(solution)/shard_map/ppermute | solution.py:300
  18.0 1.8 %collective-permute-start.5 = (bf16[4,8,1536]{2,1,0:T(8,128)(2,1)S(1)}, bf16[4,8,1536]{2,1,0:T(8,128)(2,1)S(1)}, u32[]{:S(2)}, u32[]{:S(2)}) collective-permute-start(bf16[4,8,1536]{2,1,0:T(8,128)(2,1)S(1)} %collective-permute-done.3.refs_1_), channel_id=1, source_target_pairs={{0,1},{1,0},{2,3},{3,2},{4,5},{5,4},{6,7},{7,6},{8,9},{9,8},{10,11... | collective-permute-start | bytes 294920 | tf_op jit(solution)/shard_map/ppermute | solution.py:300
  18.0 1.7 %collective-permute-start.6 = (f32[8,128]{1,0:T(8,128)S(1)}, f32[8,128]{1,0:T(8,128)S(1)}, u32[]{:S(2)}, u32[]{:S(2)}) collective-permute-start(f32[8,128]{1,0:T(8,128)S(1)} %get-tuple-element.13.refs_4_.meta_ref), channel_id=1, source_target_pairs={{0,1},{1,0},{2,3},{3,2},{4,5},{5,4},{6,7},{7,6},{8,9},{9,8},{10,11... | collective-permute-start | bytes 12296 | tf_op jit(solution)/shard_map/ppermute | solution.py:300
  24.4 1.5 %collective-permute-start.7 = (bf16[8,8,1536]{2,1,0:T(8,128)(2,1)S(1)}, bf16[8,8,1536]{2,1,0:T(8,128)(2,1)S(1)}, u32[]{:S(2)}, u32[]{:S(2)}) collective-permute-start(bf16[8,8,1536]{2,1,0:T(8,128)(2,1)S(1)} %get-tuple-element.16), channel_id=1, source_target_pairs={{0,1},{1,0},{2,3},{3,2},{4,5},{5,4},{6,7},{7,6},{8,9},{9,8},{10,11... | collective-permute-start | bytes 589832 | tf_op jit(solution)/shard_map/ppermute | solution.py:300

commit v5 on v4

--- a/solution.py
+++ b/solution.py
@@ -135,7 +135,7 @@
 
 
 def stack_kernel(*refs):
-    for i, ref in enumerate(refs[:-2]):
+    for i, ref in enumerate(refs[:-3]):
         refs[-1][i] = ref[...]
 
 
@@ -175,16 +175,14 @@
         ].astype(target.dtype)
 
 
-def expert_kernel(block, piece, offsets, parts, *refs):
+def expert_kernel(block, parts, *refs):
     own_refs, refs = refs[:parts], refs[parts:]
     other_refs, refs = refs[:parts], refs[parts:]
     (
         up_ref,
         gate_ref,
         gates_ref,
-        down_ref,
         meta_other_ref,
-        sent_ref,
         units_ref,
         rows_ref,
     ) = refs
@@ -210,23 +208,17 @@
         gate = jax.nn.silu(gate * inv_rms) * inv_rms
         up = jnp.dot(rows_ref[...], up_ref[:, part], preferred_element_type=jnp.float32)
         units_ref[:, part] = (gate * up).astype(jnp.bfloat16)
+
+
+def down_kernel(piece, offsets, own, units_ref, down_ref, out_ref):
+    half = out_ref.shape[-1]
+    base = half_starts(half)[0 if own else 1]
     for start in range(0, half, piece):
-        columns = pl.ds(pl.multiple_of(other_start + start, LANES), piece)
+        columns = pl.ds(pl.multiple_of(base + start, LANES), piece)
         product = jnp.dot(
             units_ref[...], down_ref[:, columns], preferred_element_type=jnp.float32
         )
-        store_rows(offsets, sent_ref, slice(start, start + piece), product)
-
-
-def keep_kernel(piece, offsets, units_ref, down_ref, kept_ref):
-    half = kept_ref.shape[-1]
-    own_start, _ = half_starts(half)
-    for start in range(0, half, piece):
-        columns = pl.ds(pl.multiple_of(own_start + start, LANES), piece)
-        product = jnp.dot(
-            units_ref[...], down_ref[:, columns], preferred_element_type=jnp.float32
-        )
-        store_rows(offsets, kept_ref, slice(start, start + piece), product)
+        store_rows(offsets, out_ref, slice(start, start + piece), product)
 
 
 def add_kernel(kept_ref, received_ref, out_ref):
@@ -334,20 +326,21 @@
             for array in inputs
         ]
         + [pltpu.SemaphoreType.DMA((7,))],
-        compiler_params=pltpu.CompilerParams(vmem_limit_bytes=16 << 20),
+        compiler_params=pltpu.CompilerParams(vmem_limit_bytes=6 << 20),
     )(*[far(array) for array in inputs])
 
     offsets = [k * owners for k in range(experts)]
     crossed = [swap_devices(hidden, offset, devices) for offset in offsets[1:]]
-    (up_near,), meta = fetch(meta, meta, (w_up, 0, width))
+    _, meta = fetch(meta, meta, (w_up, 0, 16))
+    w_gate, w_up, w_down = near(w_gate), near(w_up), near(w_down)
     held = [
         pl.pallas_call(
             stack_kernel,
-            in_specs=[VMEM] * (experts + 1),
+            in_specs=[VMEM] * (experts + 2),
             out_specs=VMEM,
             out_shape=jax.ShapeDtypeStruct((experts, rows, half), jnp.bfloat16),
             compiler_params=pltpu.CompilerParams(vmem_limit_bytes=2 << 20),
-        )(hidden, *crossed, meta)
+        )(hidden, *crossed, meta, w_gate)
     ]
     step = 1
     while step < owners:
@@ -361,7 +354,6 @@
         others.append(swap_cores(held[1]))
     meta_other = swap_cores(meta)
     parts = len(held)
-    w_gate, w_up, w_down = near(w_gate), up_near, near(w_down)
     gates = pl.pallas_call(
         functools.partial(gate_kernel, block),
         in_specs=[VMEM] * (parts + 1),
@@ -372,28 +364,31 @@
             flops=2 * count * half * units, bytes_accessed=2 * half * units, transcendentals=0
         ),
     )(*held, w_gate)
-    sent, units_bf = pl.pallas_call(
-        functools.partial(expert_kernel, block, piece, offsets, parts),
-        in_specs=[VMEM] * (2 * parts + 5),
-        out_specs=[VMEM] * 2,
-        out_shape=[
-            jax.ShapeDtypeStruct((devices, rows, half), jnp.bfloat16),
-            jax.ShapeDtypeStruct((count, units), jnp.bfloat16),
-        ],
+    units_bf = pl.pallas_call(
+        functools.partial(expert_kernel, block, parts),
+        in_specs=[VMEM] * (2 * parts + 4),
+        out_specs=VMEM,
+        out_shape=jax.ShapeDtypeStruct((count, units), jnp.bfloat16),
         scratch_shapes=[pltpu.VMEM((count, width), jnp.bfloat16)],
         compiler_params=pltpu.CompilerParams(vmem_limit_bytes=min(48, count // 8) << 20),
-    )(*held, *others, w_up, w_gate, gates, w_down, meta_other)
-    received = swap_cores(sent)
-    kept = pl.pallas_call(
-        functools.partial(keep_kernel, piece, offsets),
-        in_specs=[VMEM] * 2,
-        out_specs=VMEM,
-        out_shape=jax.ShapeDtypeStruct((devices, rows, half), jnp.float32),
-        compiler_params=pltpu.CompilerParams(vmem_limit_bytes=min(48, count // 16) << 20),
-        cost_estimate=pl.CostEstimate(
-            flops=2 * count * half * units, bytes_accessed=2 * half * units, transcendentals=0
-        ),
-    )(units_bf, w_down)
+    )(*held, *others, w_up, w_gate, gates, meta_other)
+
+    def project(own, dtype):
+        return pl.pallas_call(
+            functools.partial(down_kernel, piece, offsets, own),
+            in_specs=[VMEM] * 2,
+            out_specs=VMEM,
+            out_shape=jax.ShapeDtypeStruct((devices, rows, half), dtype),
+            compiler_params=pltpu.CompilerParams(vmem_limit_bytes=min(48, count // 16) << 20),
+            cost_estimate=pl.CostEstimate(
+                flops=2 * count * half * units,
+                bytes_accessed=2 * half * units,
+                transcendentals=0,
+            ),
+        )(units_bf, w_down)
+
+    received = swap_cores(project(False, jnp.bfloat16))
+    kept = project(True, jnp.float32)
     summed = pl.pallas_call(
         add_kernel,
         in_specs=[VMEM] * 2,
@@ -407,7 +402,7 @@
         in_specs=[VMEM] * 4,
         out_specs=VMEM,
         out_shape=jax.ShapeDtypeStruct(query.shape, jnp.bfloat16),
-        compiler_params=pltpu.CompilerParams(vmem_limit_bytes=16 << 20),
+        compiler_params=pltpu.CompilerParams(vmem_limit_bytes=6 << 20),
     )(returned, hidden, meta, meta_other)
 
 

time: 41.2 us -> 39 us (0.947)
  Pallas kernels: 15.5 us -> 12.3 us
  waiting for transfers between devices: 3.19 us -> 5.92 us
  blocking collectives: 14.2 us -> 12.4 us
    pallas_call x1, Pallas kernels: 4.73 us -> 1.47 us  [fetch(): pl.pallas_call(functools.partial(fetch_kernel, [start for _, start, _ in...]
    ppermute x4, waiting for transfers between devices: 2.99 us -> 5.72 us  [swap_devices(): lax.ppermute(value, 'devs', [(d, d ^ offset) for d in range(devices)])]
    all_to_all x1, blocking collectives: 14.2 us -> 12.4 us  [on_device(): lax.all_to_all(summed, 'devs', split_axis=0, concat_axis=0, tiled=True)]
    pallas_call x3 -> x4, Pallas kernels: 5.83 us -> 5.94 us  [the longest x1 3.48 us: on_device(): pl.pallas_call(functools.partial(expert_kernel, block, parts), in_specs=[...]
  transfers between devices with their start and end apart: 8 -> 8, of which waited for: 2 -> 3; matrix products, arithmetic and copies ran while one was open for 0% -> 0% of each run, Pallas kernels for 18% -> 10%
where the time goes in v5:
time: 39 us; the launch traced here: 38.8 us
  blocking collectives  12.4 us (32%)
  Pallas kernels  12.3 us (32%)
  starting transfers between devices  7.9 us (20%)
  waiting for transfers between devices  5.92 us (15%)
    all_to_all x1, blocking collectives, on_device(): lax.all_to_all(summed, 'devs', split_axis=0, concat_axis=0, tiled=True)  12.4 us
    ppermute x4, starting transfers between devices, swap_devices(): lax.ppermute(value, 'devs', [(d, d ^ offset) for d in range(devices)])  7.31 us
    ppermute x4, waiting for transfers between devices, swap_devices(): lax.ppermute(value, 'devs', [(d, d ^ offset) for d in range(devices)])  5.72 us
    pallas_call x1, Pallas kernels, on_device(): pl.pallas_call(functools.partial(expert_kernel, block, parts), in_specs=[...  3.48 us
    pallas_call x1, Pallas kernels, on_device(): pl.pallas_call(attend_kernel, in_specs=[HBM] * 7, out_specs=[VMEM] * 2, o...  2.72 us
    pallas_call x2, Pallas kernels, project(): pl.pallas_call(functools.partial(down_kernel, piece, offsets, own), in_sp...  2.45 us
    pallas_call x1, Pallas kernels, fetch(): pl.pallas_call(functools.partial(fetch_kernel, [start for _, start, _ in...  1.47 us
    pallas_call x1, Pallas kernels, on_device(): pl.pallas_call(functools.partial(gate_kernel, block), in_specs=[VMEM] * (...  1.22 us
  transfers between devices with their start and end apart: 8, of which 3 were waited for; matrix products, arithmetic and copies ran while one was open for 0% of the time, Pallas kernels for 10%

profile of v5, /device:TPU:0, one launch (start us, length us, event | category | flops | bytes accessed | tf_op | source)
XLA Modules:
  0.0 38.8 jit_solution(13710897525808252733)
XLA Ops:
  0.0 2.7 %shard_map.100 = (bf16[8,1536]{1,0:T(8,128)(2,1)S(1)}, f32[8,128]{1,0:T(8,128)S(1)}) custom-call(bf16[2,4,1536]{2,1,0:T(4,128)(2,1)} %query_hbm.1, bf16[2,4,256,256]{3,2,1,0:T(8,128)(2,1)} %key_hbm.1, bf16[2,4,256,256]{3,2,1,0:T(8,128)(2,1)} %value_hbm.1, s32[2,4]{1,0:T(2,128)} %lengths_hbm.1, bf16[2,4,1536]{2,1,0:T(4,128)(2,1)} %residual_hbm.1, ...), custom_call_target="tpu_custom_call" | custom-call | tf_op jit(solution)/shard_map/pallas_call | solution.py:316
  2.7 5.1 %collective-permute-start.2 = (bf16[8,1536]{1,0:T(8,128)(2,1)S(1)}, bf16[8,1536]{1,0:T(8,128)(2,1)S(1)}, u32[]{:S(2)}, u32[]{:S(2)}) collective-permute-start(bf16[8,1536]{1,0:T(8,128)(2,1)S(1)} %get-tuple-element.8.refs_0_.hidden_ref), channel_id=1, source_target_pairs={{0,12},{2,14},{4,8},{6,10},{8,4},{10,6},{12,0},{14,2},{1,13},{3,15... | collective-permute-start | bytes 73736 | tf_op jit(solution)/shard_map/ppermute | solution.py:288
  7.9 0.6 %collective-permute-start = (bf16[8,1536]{1,0:T(8,128)(2,1)S(1)}, bf16[8,1536]{1,0:T(8,128)(2,1)S(1)}, u32[]{:S(2)}, u32[]{:S(2)}) collective-permute-start(bf16[8,1536]{1,0:T(8,128)(2,1)S(1)} %get-tuple-element.8.refs_0_.hidden_ref), channel_id=1, source_target_pairs={{0,4},{2,6},{4,0},{6,2},{8,12},{10,14},{12,8},{14,10},{1,5},{3,7},... | collective-permute-start | bytes 73736 | tf_op jit(solution)/shard_map/ppermute | solution.py:288
  8.5 1.5 %shard_map.101 = (bf16[16,2048]{1,0:T(8,128)(2,1)}, f32[8,128]{1,0:T(8,128)S(1)}) custom-call(f32[8,128]{1,0:T(8,128)S(1)} %get-tuple-element.9.after_ref.meta_ref, f32[8,128]{1,0:T(8,128)S(1)} %get-tuple-element.9.after_ref.meta_ref, bf16[3072,2048]{1,0:T(8,128)(2,1)} %refs_4_.1), custom_call_target="tpu_custom_call" | custom-call | bytes 65536 | tf_op jit(solution)/shard_map/pallas_call | solution.py:273
  10.0 0.0 collective-permute-done.2.refs_3_
  10.0 2.6 %collective-permute-done.1.refs_2_ = bf16[8,1536]{1,0:T(8,128)(2,1)S(1)} collective-permute-done((bf16[8,1536]{1,0:T(8,128)(2,1)S(1)}, bf16[8,1536]{1,0:T(8,128)(2,1)S(1)}, u32[]{:S(2)}, u32[]{:S(2)}) %collective-permute-start.1) | collective-permute-done | bytes 24608 | tf_op jit(solution)/shard_map/ppermute | solution.py:288
  12.6 0.0 slice-start.4
  12.6 0.0 slice-start.5
  12.6 1.6 %collective-permute-start.3 = (bf16[4,8,1536]{2,1,0:T(8,128)(2,1)S(1)}, bf16[4,8,1536]{2,1,0:T(8,128)(2,1)S(1)}, u32[]{:S(2)}, u32[]{:S(2)}) collective-permute-start(bf16[4,8,1536]{2,1,0:T(8,128)(2,1)S(1)} %shard_map.102.refs_0_), channel_id=1, source_target_pairs={{0,2},{2,0},{4,6},{6,4},{8,10},{10,8},{12,14},{14,12},{1,3},{3,1},... | collective-permute-start | bytes 294920 | tf_op jit(solution)/shard_map/ppermute | solution.py:288
  14.2 3.1 %collective-permute-done.3.refs_1_ = bf16[4,8,1536]{2,1,0:T(8,128)(2,1)S(1)} collective-permute-done((bf16[4,8,1536]{2,1,0:T(8,128)(2,1)S(1)}, bf16[4,8,1536]{2,1,0:T(8,128)(2,1)S(1)}, u32[]{:S(2)}, u32[]{:S(2)}) %collective-permute-start.3) | collective-permute-done | bytes 98336 | tf_op jit(solution)/shard_map/ppermute | solution.py:288
  17.3 0.0 collective-permute-start.5
  17.3 0.5 %collective-permute-start.6 = (f32[8,128]{1,0:T(8,128)S(1)}, f32[8,128]{1,0:T(8,128)S(1)}, u32[]{:S(2)}, u32[]{:S(2)}) collective-permute-start(f32[8,128]{1,0:T(8,128)S(1)} %get-tuple-element.10.refs_4_.meta_ref), channel_id=1, source_target_pairs={{0,1},{1,0},{2,3},{3,2},{4,5},{5,4},{6,7},{7,6},{8,9},{9,8},{10,11... | collective-permute-start | bytes 12296 | tf_op jit(solution)/shard_map/ppermute | solution.py:292
  17.8 1.2 %shard_map.103.refs_6_ = f32[64,2048]{1,0:T(8,128)S(1)} custom-call(bf16[4,8,1536]{2,1,0:T(8,128)(2,1)S(1)} %shard_map.102.refs_0_, bf16[4,8,1536]{2,1,0:T(8,128)(2,1)S(1)} %collective-permute-done.3.refs_1_, bf16[3072,2048]{1,0:T(8,128)(2,1)S(1)} %copy-done), custom_call_target="tpu_custom_call" | custom-call | flops 402653184 | bytes 6291456 | tf_op jit(solution)/shard_map/pallas_call | solution.py:357
  19.1 0.0 slice-start.2
  19.1 0.0 collective-permute-done.6.refs_7_.meta_other_ref
  19.1 0.0 collective-permute-done.4.refs_2_
  19.1 3.5 %shard_map.104.units_ref = bf16[64,2048]{1,0:T(8,128)(2,1)S(1)} custom-call(bf16[4,8,1536]{2,1,0:T(8,128)(2,1)S(1)} %shard_map.102.refs_0_, bf16[4,8,1536]{2,1,0:T(8,128)(2,1)S(1)} %collective-permute-done.3.refs_1_, bf16[4,8,1536]{2,1,0:T(8,128)(2,1)S(1)} %collective-permute-done.4.refs_2_, bf16[4,8,1536]{2,1,0:T(8,128)(2,1)S(1)} %collective-permute-done.5.refs_3_, ...), custom_call_target="tpu_custom_call" | custom-call | tf_op jit(solution)/shard_map/pallas_call | solution.py:367
  22.7 0.0 slice-done.2
  22.7 1.2 %shard_map.106 = bf16[8,8,1536]{2,1,0:T(8,128)(2,1)S(1)} custom-call(bf16[64,2048]{1,0:T(8,128)(2,1)S(1)} %shard_map.104.units_ref, bf16[2048,3072]{1,0:T(8,128)(2,1)S(1)} %bitcast.3), custom_call_target="tpu_custom_call" | custom-call | flops 402653184 | bytes 6291456 | tf_op jit(solution)/shard_map/pallas_call | solution.py:377
  23.9 0.1 collective-permute-start.7
  24.0 1.2 %shard_map.105.kept_ref = f32[8,8,1536]{2,1,0:T(8,128)S(1)} custom-call(bf16[64,2048]{1,0:T(8,128)(2,1)S(1)} %shard_map.104.units_ref, bf16[2048,3072]{1,0:T(8,128)(2,1)S(1)} %bitcast.3), custom_call_target="tpu_custom_call" | custom-call | flops 402653184 | bytes 6291456 | tf_op jit(solution)/shard_map/pallas_call | solution.py:377
  25.2 0.2 collective-permute-done.7.received_ref
  25.5 12.4 %all_to_all.5.returned_ref = bf16[8,8,1536]{2,1,0:T(8,128)(2,1)S(1)} all-to-all(bf16[8,8,1536]{2,1,0:T(8,128)(2,1)S(1)} %shard_map.107), channel_id=1, replica_groups=mesh['groups'=2,'devs'=8,'pair'=2] {'devs'}, dimensions={0} | all-to-all | bytes 393216 | tf_op jit(solution)/shard_map/all_to_all | solution.py:399
  37.9 0.9 %shard_map.108 = bf16[2,4,1536]{2,1,0:T(4,128)(2,1)} custom-call(bf16[8,8,1536]{2,1,0:T(8,128)(2,1)S(1)} %all_to_all.5.returned_ref, bf16[8,1536]{1,0:T(8,128)(2,1)S(1)} %get-tuple-element.8.refs_0_.hidden_ref, f32[8,128]{1,0:T(8,128)S(1)} %get-tuple-element.10.refs_4_.meta_ref, f32[8,128]{1,0:T(8,128)S(1)} %collective-permute-done.6.refs_7_.meta_other_ref), custom_call_target="tpu_custom_call" | custom-call | tf_op jit(solution)/shard_map/pallas_call | solution.py:400
  (18 shorter events, 0.1 us)
Async XLA Ops:
  0.0 12.6 %copy-start = (bf16[3072,2048]{1,0:T(8,128)(2,1)S(1)}, bf16[3072,2048]{1,0:T(8,128)(2,1)}, u32[]{:S(2)}) copy-start(bf16[3072,2048]{1,0:T(8,128)(2,1)} %refs_5_.3) | copy-start | bytes 37748740
  2.7 7.2 %collective-permute-start.2 = (bf16[8,1536]{1,0:T(8,128)(2,1)S(1)}, bf16[8,1536]{1,0:T(8,128)(2,1)S(1)}, u32[]{:S(2)}, u32[]{:S(2)}) collective-permute-start(bf16[8,1536]{1,0:T(8,128)(2,1)S(1)} %get-tuple-element.8.refs_0_.hidden_ref), channel_id=1, source_target_pairs={{0,12},{2,14},{4,8},{6,10},{8,4},{10,6},{12,0},{14,2},{1,13},{3,15... | collective-permute-start | bytes 73736 | tf_op jit(solution)/shard_map/ppermute | solution.py:288
  7.8 4.7 %collective-permute-start.1 = (bf16[8,1536]{1,0:T(8,128)(2,1)S(1)}, bf16[8,1536]{1,0:T(8,128)(2,1)S(1)}, u32[]{:S(2)}, u32[]{:S(2)}) collective-permute-start(bf16[8,1536]{1,0:T(8,128)(2,1)S(1)} %get-tuple-element.8.refs_0_.hidden_ref), channel_id=1, source_target_pairs={{0,8},{2,10},{4,12},{6,14},{8,0},{10,2},{12,4},{14,6},{1,9},{3,11}... | collective-permute-start | bytes 73736 | tf_op jit(solution)/shard_map/ppermute | solution.py:288
  7.9 4.7 %collective-permute-start = (bf16[8,1536]{1,0:T(8,128)(2,1)S(1)}, bf16[8,1536]{1,0:T(8,128)(2,1)S(1)}, u32[]{:S(2)}, u32[]{:S(2)}) collective-permute-start(bf16[8,1536]{1,0:T(8,128)(2,1)S(1)} %get-tuple-element.8.refs_0_.hidden_ref), channel_id=1, source_target_pairs={{0,4},{2,6},{4,0},{6,2},{8,12},{10,14},{12,8},{14,10},{1,5},{3,7},... | collective-permute-start | bytes 73736 | tf_op jit(solution)/shard_map/ppermute | solution.py:288
  12.6 6.5 %slice-start.3 = ((s8[12582912]{0:T(1024)(128)(4,1)}), s8[4194304]{0:T(1024)(128)(4,1)S(1)}, s32[]{:S(2)}) async-start(s8[12582912]{0:T(1024)(128)(4,1)} %bitcast.4), calls=%async_computation.4 | async-start | bytes 8388608
  12.6 6.5 %slice-start.4 = ((s8[12582912]{0:T(1024)(128)(4,1)}), s8[4194304]{0:T(1024)(128)(4,1)S(1)}, s32[]{:S(2)}) async-start(s8[12582912]{0:T(1024)(128)(4,1)} %bitcast.4), calls=%async_computation.5 | async-start | bytes 8388608
  12.6 6.5 %slice-start.5 = ((s8[12582912]{0:T(1024)(128)(4,1)}), s8[4194304]{0:T(1024)(128)(4,1)S(1)}, s32[]{:S(2)}) async-start(s8[12582912]{0:T(1024)(128)(4,1)} %bitcast.4), calls=%async_computation.6 | async-start | bytes 8388608
  12.6 4.7 %collective-permute-start.3 = (bf16[4,8,1536]{2,1,0:T(8,128)(2,1)S(1)}, bf16[4,8,1536]{2,1,0:T(8,128)(2,1)S(1)}, u32[]{:S(2)}, u32[]{:S(2)}) collective-permute-start(bf16[4,8,1536]{2,1,0:T(8,128)(2,1)S(1)} %shard_map.102.refs_0_), channel_id=1, source_target_pairs={{0,2},{2,0},{4,6},{6,4},{8,10},{10,8},{12,14},{14,12},{1,3},{3,1},... | collective-permute-start | bytes 294920 | tf_op jit(solution)/shard_map/ppermute | solution.py:288
  14.2 4.9 %collective-permute-start.4 = (bf16[4,8,1536]{2,1,0:T(8,128)(2,1)S(1)}, bf16[4,8,1536]{2,1,0:T(8,128)(2,1)S(1)}, u32[]{:S(2)}, u32[]{:S(2)}) collective-permute-start(bf16[4,8,1536]{2,1,0:T(8,128)(2,1)S(1)} %shard_map.102.refs_0_), channel_id=1, source_target_pairs={{0,1},{1,0},{2,3},{3,2},{4,5},{5,4},{6,7},{7,6},{8,9},{9,8},{10,11... | collective-permute-start | bytes 294920 | tf_op jit(solution)/shard_map/ppermute | solution.py:292
  17.3 1.8 %collective-permute-start.5 = (bf16[4,8,1536]{2,1,0:T(8,128)(2,1)S(1)}, bf16[4,8,1536]{2,1,0:T(8,128)(2,1)S(1)}, u32[]{:S(2)}, u32[]{:S(2)}) collective-permute-start(bf16[4,8,1536]{2,1,0:T(8,128)(2,1)S(1)} %collective-permute-done.3.refs_1_), channel_id=1, source_target_pairs={{0,1},{1,0},{2,3},{3,2},{4,5},{5,4},{6,7},{7,6},{8,9},{9,8},{10,11... | collective-permute-start | bytes 294920 | tf_op jit(solution)/shard_map/ppermute | solution.py:292
  17.3 1.8 %collective-permute-start.6 = (f32[8,128]{1,0:T(8,128)S(1)}, f32[8,128]{1,0:T(8,128)S(1)}, u32[]{:S(2)}, u32[]{:S(2)}) collective-permute-start(f32[8,128]{1,0:T(8,128)S(1)} %get-tuple-element.10.refs_4_.meta_ref), channel_id=1, source_target_pairs={{0,1},{1,0},{2,3},{3,2},{4,5},{5,4},{6,7},{7,6},{8,9},{9,8},{10,11... | collective-permute-start | bytes 12296 | tf_op jit(solution)/shard_map/ppermute | solution.py:292
  17.8 4.8 %slice-start = ((s8[12582912]{0:T(1024)(128)(4,1)}), s8[4194304]{0:T(1024)(128)(4,1)S(1)}, s32[]{:S(2)}) async-start(s8[12582912]{0:T(1024)(128)(4,1)} %bitcast.2), calls=%async_computation.1 | async-start | bytes 8388608
  17.8 4.8 %slice-start.1 = ((s8[12582912]{0:T(1024)(128)(4,1)}), s8[4194304]{0:T(1024)(128)(4,1)S(1)}, s32[]{:S(2)}) async-start(s8[12582912]{0:T(1024)(128)(4,1)} %bitcast.2), calls=%async_computation.2 | async-start | bytes 8388608
  19.1 3.6 %slice-start.2 = ((s8[12582912]{0:T(1024)(128)(4,1)}), s8[4194304]{0:T(1024)(128)(4,1)S(1)}, s32[]{:S(2)}) async-start(s8[12582912]{0:T(1024)(128)(4,1)} %bitcast.2), calls=%async_computation.3 | async-start | bytes 8388608
  23.9 1.5 %collective-permute-start.7 = (bf16[8,8,1536]{2,1,0:T(8,128)(2,1)S(1)}, bf16[8,8,1536]{2,1,0:T(8,128)(2,1)S(1)}, u32[]{:S(2)}, u32[]{:S(2)}) collective-permute-start(bf16[8,8,1536]{2,1,0:T(8,128)(2,1)S(1)} %shard_map.106), channel_id=1, source_target_pairs={{0,1},{1,0},{2,3},{3,2},{4,5},{5,4},{6,7},{7,6},{8,9},{9,8},{10,11... | collective-permute-start | bytes 589832 | tf_op jit(solution)/shard_map/ppermute | solution.py:292

commit v6 on v5

--- a/solution.py
+++ b/solution.py
@@ -63,7 +63,7 @@
     for r in range(rows):
         limit = jnp.where(row_of == r, lengths_ref[r // per_batch, r % per_batch], limit)
     live = position < limit
-    pieces = []
+    pieces, all_scores = [], []
     for k in range(kv_local):
         heads = jnp.concatenate(
             [queries[:, (k * group + j) * HD : (k * group + j + 1) * HD] for j in range(group)],
@@ -77,14 +77,16 @@
                 heads, keys, (((1,), (1,)), ((), ())), preferred_element_type=jnp.float32
             )
             scores = jnp.where(row_of == r, part, scores)
+        all_scores.append(scores)
+    for copy in copies[len(early) :]:
+        copy.wait()
+    for k, scores in enumerate(all_scores):
+        columns = slice(k * HD, (k + 1) * HD)
         scores = jnp.where(live, scores * (1.0 / math.sqrt(HD)), -jnp.inf)
         peak = jnp.max(scores, axis=-1, keepdims=True)
         weights = jnp.where(live, jnp.exp(scores - peak), 0.0)
         total = jnp.sum(weights, axis=-1, keepdims=True)
         weights_bf = weights.astype(jnp.bfloat16)
-        if k == 0:
-            for copy in copies[len(early) :]:
-                copy.wait()
         mixed = jnp.zeros((tall, HD), jnp.float32)
         for r in range(rows):
             values = value_ref[r // per_batch, r % per_batch, :, columns]
@@ -175,15 +177,17 @@
         ].astype(target.dtype)
 
 
-def expert_kernel(block, parts, *refs):
+def expert_kernel(block, experts, parts, *refs):
     own_refs, refs = refs[:parts], refs[parts:]
     other_refs, refs = refs[:parts], refs[parts:]
     (
         up_ref,
         gate_ref,
         gates_ref,
+        meta_ref,
         meta_other_ref,
         units_ref,
+        weights_ref,
         rows_ref,
     ) = refs
     width = rows_ref.shape[1]
@@ -208,6 +212,17 @@
         gate = jax.nn.silu(gate * inv_rms) * inv_rms
         up = jnp.dot(rows_ref[...], up_ref[:, part], preferred_element_type=jnp.float32)
         units_ref[:, part] = (gate * up).astype(jnp.bfloat16)
+
+    meta = meta_ref[...] + meta_other_ref[...]
+    logits = meta * lax.rsqrt(meta[:, experts : experts + 1] / width + 1e-05)
+    chosen = meta_ref[:, experts + 1 : experts + 3].astype(jnp.int32)
+    first, second = chosen[:, 0:1], chosen[:, 1:2]
+    lane = lax.broadcasted_iota(jnp.int32, meta.shape, 1)
+    logit_first = jnp.sum(jnp.where(lane == first, logits, 0.0), axis=-1, keepdims=True)
+    logit_second = jnp.sum(jnp.where(lane == second, logits, 0.0), axis=-1, keepdims=True)
+    weights_ref[...] = jnp.where(
+        lane == first, jax.nn.sigmoid(logit_first - logit_second), 0.0
+    ) + jnp.where(lane == second, jax.nn.sigmoid(logit_second - logit_first), 0.0)
 
 
 def down_kernel(piece, offsets, own, units_ref, down_ref, out_ref):
@@ -225,30 +240,16 @@
     out_ref[...] = (kept_ref[...] + received_ref[...].astype(jnp.float32)).astype(jnp.bfloat16)
 
 
-def combine_kernel(
-    experts, returned_ref, hidden_ref, meta_ref, meta_other_ref, out_ref
-):
-    devices, rows, half = returned_ref.shape
+def combine_kernel(experts, returned_ref, hidden_ref, weights_ref, out_ref):
+    devices = returned_ref.shape[0]
     batches, per_batch, _ = out_ref.shape
     owners = devices // experts
-    meta = meta_ref[...] + meta_other_ref[...]
-    squares = meta[:, experts : experts + 1]
-    inv_rms = lax.rsqrt(squares / (2 * half) + 1e-05)
-    logits = meta * inv_rms
-    chosen = meta_ref[:, experts + 1 : experts + 3].astype(jnp.int32)
-    lane = lax.broadcasted_iota(jnp.int32, (rows, LANES), 1)
-    first, second = chosen[:, 0:1], chosen[:, 1:2]
-    logit_first = jnp.sum(jnp.where(lane == first, logits, 0.0), axis=-1, keepdims=True)
-    logit_second = jnp.sum(jnp.where(lane == second, logits, 0.0), axis=-1, keepdims=True)
-    gate_first = jax.nn.sigmoid(logit_first - logit_second)
-    gate_second = jax.nn.sigmoid(logit_second - logit_first)
     result = hidden_ref[...].astype(jnp.float32)
     for e in range(experts):
         expert_out = returned_ref[e * owners].astype(jnp.float32)
         for o in range(1, owners):
             expert_out += returned_ref[e * owners + o].astype(jnp.float32)
-        weight = jnp.where(first == e, gate_first, 0.0) + jnp.where(second == e, gate_second, 0.0)
-        result += weight * expert_out
+        result += weights_ref[:, e : e + 1] * expert_out
     for b in range(batches):
         out_ref[b] = result[b * per_batch : (b + 1) * per_batch].astype(jnp.bfloat16)
 
@@ -350,9 +351,10 @@
         offsets += [offset ^ step for offset in offsets]
         step *= 2
     others = [swap_cores(held[0])]
+    meta_other = swap_cores(meta)
     if len(held) > 1:
+        held[1], meta_other = lax.optimization_barrier((held[1], meta_other))
         others.append(swap_cores(held[1]))
-    meta_other = swap_cores(meta)
     parts = len(held)
     gates = pl.pallas_call(
         functools.partial(gate_kernel, block),
@@ -364,14 +366,17 @@
             flops=2 * count * half * units, bytes_accessed=2 * half * units, transcendentals=0
         ),
     )(*held, w_gate)
-    units_bf = pl.pallas_call(
-        functools.partial(expert_kernel, block, parts),
-        in_specs=[VMEM] * (2 * parts + 4),
-        out_specs=VMEM,
-        out_shape=jax.ShapeDtypeStruct((count, units), jnp.bfloat16),
+    units_bf, weights = pl.pallas_call(
+        functools.partial(expert_kernel, block, experts, parts),
+        in_specs=[VMEM] * (2 * parts + 5),
+        out_specs=[VMEM] * 2,
+        out_shape=[
+            jax.ShapeDtypeStruct((count, units), jnp.bfloat16),
+            jax.ShapeDtypeStruct(meta.shape, jnp.float32),
+        ],
         scratch_shapes=[pltpu.VMEM((count, width), jnp.bfloat16)],
         compiler_params=pltpu.CompilerParams(vmem_limit_bytes=min(48, count // 8) << 20),
-    )(*held, *others, w_up, w_gate, gates, meta_other)
+    )(*held, *others, w_up, w_gate, gates, meta, meta_other)
 
     def project(own, dtype):
         return pl.pallas_call(
@@ -399,11 +404,11 @@
     returned = lax.all_to_all(summed, "devs", split_axis=0, concat_axis=0, tiled=True)
     return pl.pallas_call(
         functools.partial(combine_kernel, experts),
-        in_specs=[VMEM] * 4,
+        in_specs=[VMEM] * 3,
         out_specs=VMEM,
         out_shape=jax.ShapeDtypeStruct(query.shape, jnp.bfloat16),
         compiler_params=pltpu.CompilerParams(vmem_limit_bytes=6 << 20),
-    )(returned, hidden, meta, meta_other)
+    )(returned, hidden, weights)
 
 
 def solution(mesh):

time: 39 us -> 38.2 us (0.979)
  waiting for transfers between devices: 5.92 us -> 5.27 us
  Pallas kernels: 12.3 us -> 11.8 us
  starting transfers between devices: 7.9 us -> 8.4 us
    ppermute x4, waiting for transfers between devices: 5.72 us -> 4.57 us  [swap_devices(): lax.ppermute(value, 'devs', [(d, d ^ offset) for d in range(devices)])]
    ppermute x4, waiting for transfers between devices: 0.2 us -> 0.71 us  [swap_cores(): return lax.ppermute(value, 'pair', [(0, 1), (1, 0)])]
    ppermute x4, starting transfers between devices: 0.58 us -> 1.09 us  [swap_cores(): return lax.ppermute(value, 'pair', [(0, 1), (1, 0)])]
where the time goes in v6:
time: 38.2 us; the launch traced here: 38 us
  blocking collectives  12.3 us (32%)
  Pallas kernels  11.8 us (31%)
  starting transfers between devices  8.4 us (22%)
  waiting for transfers between devices  5.27 us (14%)
    all_to_all x1, blocking collectives, on_device(): lax.all_to_all(summed, 'devs', split_axis=0, concat_axis=0, tiled=True)  12.3 us
    ppermute x4, starting transfers between devices, swap_devices(): lax.ppermute(value, 'devs', [(d, d ^ offset) for d in range(devices)])  7.31 us
    ppermute x4, waiting for transfers between devices, swap_devices(): lax.ppermute(value, 'devs', [(d, d ^ offset) for d in range(devices)])  4.57 us
    pallas_call x1, Pallas kernels, on_device(): pl.pallas_call(functools.partial(expert_kernel, block, experts, parts), i...  3.51 us
    pallas_call x2, Pallas kernels, project(): pl.pallas_call(functools.partial(down_kernel, piece, offsets, own), in_sp...  2.44 us
    pallas_call x1, Pallas kernels, on_device(): pl.pallas_call(attend_kernel, in_specs=[HBM] * 7, out_specs=[VMEM] * 2, o...  2.43 us
    pallas_call x1, Pallas kernels, fetch(): pl.pallas_call(functools.partial(fetch_kernel, [start for _, start, _ in...  1.46 us
    pallas_call x1, Pallas kernels, on_device(): pl.pallas_call(functools.partial(gate_kernel, block), in_specs=[VMEM] * (...  1.22 us
  transfers between devices with their start and end apart: 8, of which 3 were waited for; matrix products, arithmetic and copies ran while one was open for 0% of the time, Pallas kernels for 10%

profile of v6, /device:TPU:0, one launch (start us, length us, event | category | flops | bytes accessed | tf_op | source)
XLA Modules:
  0.0 38.0 jit_solution(13353583644558199608)
XLA Ops:
  0.0 2.4 %shard_map.100 = (bf16[8,1536]{1,0:T(8,128)(2,1)S(1)}, f32[8,128]{1,0:T(8,128)S(1)}) custom-call(bf16[2,4,1536]{2,1,0:T(4,128)(2,1)} %query_hbm.1, bf16[2,4,256,256]{3,2,1,0:T(8,128)(2,1)} %key_hbm.1, bf16[2,4,256,256]{3,2,1,0:T(8,128)(2,1)} %value_hbm.1, s32[2,4]{1,0:T(2,128)} %lengths_hbm.1, bf16[2,4,1536]{2,1,0:T(4,128)(2,1)} %residual_hbm.1, ...), custom_call_target="tpu_custom_call" | custom-call | tf_op jit(solution)/shard_map/pallas_call | solution.py:317
  2.4 5.1 %collective-permute-start.2 = (bf16[8,1536]{1,0:T(8,128)(2,1)S(1)}, bf16[8,1536]{1,0:T(8,128)(2,1)S(1)}, u32[]{:S(2)}, u32[]{:S(2)}) collective-permute-start(bf16[8,1536]{1,0:T(8,128)(2,1)S(1)} %get-tuple-element.12.refs_0_.hidden_ref), channel_id=1, source_target_pairs={{0,12},{2,14},{4,8},{6,10},{8,4},{10,6},{12,0},{14,2},{1,13},{3,15... | collective-permute-start | bytes 73736 | tf_op jit(solution)/shard_map/ppermute | solution.py:289
  7.6 0.6 %collective-permute-start = (bf16[8,1536]{1,0:T(8,128)(2,1)S(1)}, bf16[8,1536]{1,0:T(8,128)(2,1)S(1)}, u32[]{:S(2)}, u32[]{:S(2)}) collective-permute-start(bf16[8,1536]{1,0:T(8,128)(2,1)S(1)} %get-tuple-element.12.refs_0_.hidden_ref), channel_id=1, source_target_pairs={{0,4},{2,6},{4,0},{6,2},{8,12},{10,14},{12,8},{14,10},{1,5},{3,7},... | collective-permute-start | bytes 73736 | tf_op jit(solution)/shard_map/ppermute | solution.py:289
  8.2 1.5 %shard_map.101 = (bf16[16,2048]{1,0:T(8,128)(2,1)}, f32[8,128]{1,0:T(8,128)S(1)}) custom-call(f32[8,128]{1,0:T(8,128)S(1)} %get-tuple-element.13.after_ref.meta_ref, f32[8,128]{1,0:T(8,128)S(1)} %get-tuple-element.13.after_ref.meta_ref, bf16[3072,2048]{1,0:T(8,128)(2,1)} %refs_4_.1), custom_call_target="tpu_custom_call" | custom-call | bytes 65536 | tf_op jit(solution)/shard_map/pallas_call | solution.py:274
  9.7 0.0 collective-permute-done.2.refs_3_
  9.7 2.6 %collective-permute-done.1.refs_2_ = bf16[8,1536]{1,0:T(8,128)(2,1)S(1)} collective-permute-done((bf16[8,1536]{1,0:T(8,128)(2,1)S(1)}, bf16[8,1536]{1,0:T(8,128)(2,1)S(1)}, u32[]{:S(2)}, u32[]{:S(2)}) %collective-permute-start.1) | collective-permute-done | bytes 24608 | tf_op jit(solution)/shard_map/ppermute | solution.py:289
  12.3 0.0 collective-permute-done.refs_1_
  12.3 0.0 slice-start.1
  12.3 0.0 slice-start.2
  12.3 1.6 %collective-permute-start.3 = (bf16[4,8,1536]{2,1,0:T(8,128)(2,1)S(1)}, bf16[4,8,1536]{2,1,0:T(8,128)(2,1)S(1)}, u32[]{:S(2)}, u32[]{:S(2)}) collective-permute-start(bf16[4,8,1536]{2,1,0:T(8,128)(2,1)S(1)} %shard_map.102.refs_0_), channel_id=1, source_target_pairs={{0,2},{2,0},{4,6},{6,4},{8,10},{10,8},{12,14},{14,12},{1,3},{3,1},... | collective-permute-start | bytes 294920 | tf_op jit(solution)/shard_map/ppermute | solution.py:289
  13.9 0.0 collective-permute-start.4
  13.9 0.5 %collective-permute-start.5 = (bf16[4,8,1536]{2,1,0:T(8,128)(2,1)S(1)}, bf16[4,8,1536]{2,1,0:T(8,128)(2,1)S(1)}, u32[]{:S(2)}, u32[]{:S(2)}) collective-permute-start(bf16[4,8,1536]{2,1,0:T(8,128)(2,1)S(1)} %shard_map.102.refs_0_), channel_id=1, source_target_pairs={{0,1},{1,0},{2,3},{3,2},{4,5},{5,4},{6,7},{7,6},{8,9},{9,8},{10,11... | collective-permute-start | bytes 294920 | tf_op jit(solution)/shard_map/ppermute | solution.py:293
  14.4 0.7 %collective-permute-done.4.refs_8_ = f32[8,128]{1,0:T(8,128)S(1)} collective-permute-done((f32[8,128]{1,0:T(8,128)S(1)}, f32[8,128]{1,0:T(8,128)S(1)}, u32[]{:S(2)}, u32[]{:S(2)}) %collective-permute-start.4) | collective-permute-done | bytes 4128 | tf_op jit(solution)/shard_map/ppermute | solution.py:293
  15.1 2.0 %collective-permute-done.3.refs_1_ = bf16[4,8,1536]{2,1,0:T(8,128)(2,1)S(1)} collective-permute-done((bf16[4,8,1536]{2,1,0:T(8,128)(2,1)S(1)}, bf16[4,8,1536]{2,1,0:T(8,128)(2,1)S(1)}, u32[]{:S(2)}, u32[]{:S(2)}) %collective-permute-start.3) | collective-permute-done | bytes 98336 | tf_op jit(solution)/shard_map/ppermute | solution.py:289
  17.0 1.2 %shard_map.103.refs_6_ = f32[64,2048]{1,0:T(8,128)S(1)} custom-call(bf16[4,8,1536]{2,1,0:T(8,128)(2,1)S(1)} %shard_map.102.refs_0_, bf16[4,8,1536]{2,1,0:T(8,128)(2,1)S(1)} %collective-permute-done.3.refs_1_, bf16[3072,2048]{1,0:T(8,128)(2,1)S(1)} %copy-done), custom_call_target="tpu_custom_call" | custom-call | flops 402653184 | bytes 6291456 | tf_op jit(solution)/shard_map/pallas_call | solution.py:359
  18.3 0.0 slice-start.5
  18.3 0.0 collective-permute-done.6.refs_3_
  18.3 3.5 %shard_map.104 = (bf16[64,2048]{1,0:T(8,128)(2,1)S(1)}, f32[8,128]{1,0:T(8,128)S(1)}) custom-call(bf16[4,8,1536]{2,1,0:T(8,128)(2,1)S(1)} %shard_map.102.refs_0_, bf16[4,8,1536]{2,1,0:T(8,128)(2,1)S(1)} %collective-permute-done.3.refs_1_, bf16[4,8,1536]{2,1,0:T(8,128)(2,1)S(1)} %collective-permute-done.5.refs_2_, ...), custom_call_target="tpu_custom_call" | custom-call | tf_op jit(solution)/shard_map/pallas_call | solution.py:369
  21.9 0.0 slice-done.5
  21.9 1.2 %shard_map.106 = bf16[8,8,1536]{2,1,0:T(8,128)(2,1)S(1)} custom-call(bf16[64,2048]{1,0:T(8,128)(2,1)S(1)} %get-tuple-element.17.units_ref, bf16[2048,3072]{1,0:T(8,128)(2,1)S(1)} %bitcast.5), custom_call_target="tpu_custom_call" | custom-call | flops 402653184 | bytes 6291456 | tf_op jit(solution)/shard_map/pallas_call | solution.py:382
  23.1 0.6 %collective-permute-start.7 = (bf16[8,8,1536]{2,1,0:T(8,128)(2,1)S(1)}, bf16[8,8,1536]{2,1,0:T(8,128)(2,1)S(1)}, u32[]{:S(2)}, u32[]{:S(2)}) collective-permute-start(bf16[8,8,1536]{2,1,0:T(8,128)(2,1)S(1)} %shard_map.106), channel_id=1, source_target_pairs={{0,1},{1,0},{2,3},{3,2},{4,5},{5,4},{6,7},{7,6},{8,9},{9,8},{10,11... | collective-permute-start | bytes 589832 | tf_op jit(solution)/shard_map/ppermute | solution.py:293
  23.7 1.2 %shard_map.105.kept_ref = f32[8,8,1536]{2,1,0:T(8,128)S(1)} custom-call(bf16[64,2048]{1,0:T(8,128)(2,1)S(1)} %get-tuple-element.17.units_ref, bf16[2048,3072]{1,0:T(8,128)(2,1)S(1)} %bitcast.5), custom_call_target="tpu_custom_call" | custom-call | flops 402653184 | bytes 6291456 | tf_op jit(solution)/shard_map/pallas_call | solution.py:382
  25.0 12.3 %all_to_all.5.returned_ref = bf16[8,8,1536]{2,1,0:T(8,128)(2,1)S(1)} all-to-all(bf16[8,8,1536]{2,1,0:T(8,128)(2,1)S(1)} %shard_map.107), channel_id=1, replica_groups=mesh['groups'=2,'devs'=8,'pair'=2] {'devs'}, dimensions={0} | all-to-all | bytes 393216 | tf_op jit(solution)/shard_map/all_to_all | solution.py:404
  37.3 0.7 %shard_map.108 = bf16[2,4,1536]{2,1,0:T(4,128)(2,1)} custom-call(bf16[8,8,1536]{2,1,0:T(8,128)(2,1)S(1)} %all_to_all.5.returned_ref, bf16[8,1536]{1,0:T(8,128)(2,1)S(1)} %get-tuple-element.12.refs_0_.hidden_ref, f32[8,128]{1,0:T(8,128)S(1)} %get-tuple-element.18.weights_ref), custom_call_target="tpu_custom_call" | custom-call | tf_op jit(solution)/shard_map/pallas_call | solution.py:405
  (18 shorter events, 0.1 us)
Async XLA Ops:
  0.0 12.3 %copy-start = (bf16[3072,2048]{1,0:T(8,128)(2,1)S(1)}, bf16[3072,2048]{1,0:T(8,128)(2,1)}, u32[]{:S(2)}) copy-start(bf16[3072,2048]{1,0:T(8,128)(2,1)} %refs_5_.3) | copy-start | bytes 37748740
  2.4 7.2 %collective-permute-start.2 = (bf16[8,1536]{1,0:T(8,128)(2,1)S(1)}, bf16[8,1536]{1,0:T(8,128)(2,1)S(1)}, u32[]{:S(2)}, u32[]{:S(2)}) collective-permute-start(bf16[8,1536]{1,0:T(8,128)(2,1)S(1)} %get-tuple-element.12.refs_0_.hidden_ref), channel_id=1, source_target_pairs={{0,12},{2,14},{4,8},{6,10},{8,4},{10,6},{12,0},{14,2},{1,13},{3,15... | collective-permute-start | bytes 73736 | tf_op jit(solution)/shard_map/ppermute | solution.py:289
  7.6 4.7 %collective-permute-start.1 = (bf16[8,1536]{1,0:T(8,128)(2,1)S(1)}, bf16[8,1536]{1,0:T(8,128)(2,1)S(1)}, u32[]{:S(2)}, u32[]{:S(2)}) collective-permute-start(bf16[8,1536]{1,0:T(8,128)(2,1)S(1)} %get-tuple-element.12.refs_0_.hidden_ref), channel_id=1, source_target_pairs={{0,8},{2,10},{4,12},{6,14},{8,0},{10,2},{12,4},{14,6},{1,9},{3,11}... | collective-permute-start | bytes 73736 | tf_op jit(solution)/shard_map/ppermute | solution.py:289
  7.6 4.7 %collective-permute-start = (bf16[8,1536]{1,0:T(8,128)(2,1)S(1)}, bf16[8,1536]{1,0:T(8,128)(2,1)S(1)}, u32[]{:S(2)}, u32[]{:S(2)}) collective-permute-start(bf16[8,1536]{1,0:T(8,128)(2,1)S(1)} %get-tuple-element.12.refs_0_.hidden_ref), channel_id=1, source_target_pairs={{0,4},{2,6},{4,0},{6,2},{8,12},{10,14},{12,8},{14,10},{1,5},{3,7},... | collective-permute-start | bytes 73736 | tf_op jit(solution)/shard_map/ppermute | solution.py:289
  12.3 6.0 %slice-start = ((s8[12582912]{0:T(1024)(128)(4,1)}), s8[4194304]{0:T(1024)(128)(4,1)S(1)}, s32[]{:S(2)}) async-start(s8[12582912]{0:T(1024)(128)(4,1)} %bitcast.2), calls=%async_computation.1 | async-start | bytes 8388608
  12.3 6.0 %slice-start.1 = ((s8[12582912]{0:T(1024)(128)(4,1)}), s8[4194304]{0:T(1024)(128)(4,1)S(1)}, s32[]{:S(2)}) async-start(s8[12582912]{0:T(1024)(128)(4,1)} %bitcast.2), calls=%async_computation.2 | async-start | bytes 8388608
  12.3 6.0 %slice-start.2 = ((s8[12582912]{0:T(1024)(128)(4,1)}), s8[4194304]{0:T(1024)(128)(4,1)S(1)}, s32[]{:S(2)}) async-start(s8[12582912]{0:T(1024)(128)(4,1)} %bitcast.2), calls=%async_computation.3 | async-start | bytes 8388608
  12.3 4.7 %collective-permute-start.3 = (bf16[4,8,1536]{2,1,0:T(8,128)(2,1)S(1)}, bf16[4,8,1536]{2,1,0:T(8,128)(2,1)S(1)}, u32[]{:S(2)}, u32[]{:S(2)}) collective-permute-start(bf16[4,8,1536]{2,1,0:T(8,128)(2,1)S(1)} %shard_map.102.refs_0_), channel_id=1, source_target_pairs={{0,2},{2,0},{4,6},{6,4},{8,10},{10,8},{12,14},{14,12},{1,3},{3,1},... | collective-permute-start | bytes 294920 | tf_op jit(solution)/shard_map/ppermute | solution.py:289
  13.9 1.2 %collective-permute-start.4 = (f32[8,128]{1,0:T(8,128)S(1)}, f32[8,128]{1,0:T(8,128)S(1)}, u32[]{:S(2)}, u32[]{:S(2)}) collective-permute-start(f32[8,128]{1,0:T(8,128)S(1)} %get-tuple-element.14.refs_4_.refs_7_), channel_id=1, source_target_pairs={{0,1},{1,0},{2,3},{3,2},{4,5},{5,4},{6,7},{7,6},{8,9},{9,8},{10,11... | collective-permute-start | bytes 12296 | tf_op jit(solution)/shard_map/ppermute | solution.py:293
  13.9 4.4 %collective-permute-start.5 = (bf16[4,8,1536]{2,1,0:T(8,128)(2,1)S(1)}, bf16[4,8,1536]{2,1,0:T(8,128)(2,1)S(1)}, u32[]{:S(2)}, u32[]{:S(2)}) collective-permute-start(bf16[4,8,1536]{2,1,0:T(8,128)(2,1)S(1)} %shard_map.102.refs_0_), channel_id=1, source_target_pairs={{0,1},{1,0},{2,3},{3,2},{4,5},{5,4},{6,7},{7,6},{8,9},{9,8},{10,11... | collective-permute-start | bytes 294920 | tf_op jit(solution)/shard_map/ppermute | solution.py:293
  17.0 1.3 %collective-permute-start.6 = (bf16[4,8,1536]{2,1,0:T(8,128)(2,1)S(1)}, bf16[4,8,1536]{2,1,0:T(8,128)(2,1)S(1)}, u32[]{:S(2)}, u32[]{:S(2)}) collective-permute-start(bf16[4,8,1536]{2,1,0:T(8,128)(2,1)S(1)} %collective-permute-done.3.refs_1_), channel_id=1, source_target_pairs={{0,1},{1,0},{2,3},{3,2},{4,5},{5,4},{6,7},{7,6},{8,9},{9,8},{10,11... | collective-permute-start | bytes 294920 | tf_op jit(solution)/shard_map/ppermute | solution.py:293
  17.0 4.8 %slice-start.3 = ((s8[12582912]{0:T(1024)(128)(4,1)}), s8[4194304]{0:T(1024)(128)(4,1)S(1)}, s32[]{:S(2)}) async-start(s8[12582912]{0:T(1024)(128)(4,1)} %bitcast.4), calls=%async_computation.4 | async-start | bytes 8388608
  17.0 4.8 %slice-start.4 = ((s8[12582912]{0:T(1024)(128)(4,1)}), s8[4194304]{0:T(1024)(128)(4,1)S(1)}, s32[]{:S(2)}) async-start(s8[12582912]{0:T(1024)(128)(4,1)} %bitcast.4), calls=%async_computation.5 | async-start | bytes 8388608
  18.3 3.7 %slice-start.5 = ((s8[12582912]{0:T(1024)(128)(4,1)}), s8[4194304]{0:T(1024)(128)(4,1)S(1)}, s32[]{:S(2)}) async-start(s8[12582912]{0:T(1024)(128)(4,1)} %bitcast.4), calls=%async_computation.6 | async-start | bytes 8388608
  23.1 1.8 %collective-permute-start.7 = (bf16[8,8,1536]{2,1,0:T(8,128)(2,1)S(1)}, bf16[8,8,1536]{2,1,0:T(8,128)(2,1)S(1)}, u32[]{:S(2)}, u32[]{:S(2)}) collective-permute-start(bf16[8,8,1536]{2,1,0:T(8,128)(2,1)S(1)} %shard_map.106), channel_id=1, source_target_pairs={{0,1},{1,0},{2,3},{3,2},{4,5},{5,4},{6,7},{7,6},{8,9},{9,8},{10,11... | collective-permute-start | bytes 589832 | tf_op jit(solution)/shard_map/ppermute | solution.py:293

commit v7 on v6

--- a/solution.py
+++ b/solution.py
@@ -20,6 +20,7 @@
     residual_hbm,
     router_hbm,
     routes_hbm,
+    up_hbm,
     hidden_ref,
     meta_ref,
     query_ref,
@@ -29,6 +30,7 @@
     residual_ref,
     router_ref,
     routes_ref,
+    up_ref,
     arrival,
 ):
     batches, per_batch, width = query_ref.shape
@@ -42,6 +44,7 @@
         (residual_hbm, residual_ref),
         (router_hbm, router_ref),
         (routes_hbm, routes_ref),
+        (up_hbm.at[pl.ds(0, up_ref.shape[0])], up_ref),
     ]
     copies = [
         pltpu.make_async_copy(source, target, arrival.at[i])
@@ -115,30 +118,15 @@
     hidden_ref[...] = hidden
 
 
-def fetch_kernel(starts, after_ref, meta_ref, *refs):
-    count = len(starts)
-    sources, targets, meta_out_ref, arrival = (
-        refs[:count],
-        refs[count : 2 * count],
-        refs[2 * count],
-        refs[2 * count + 1],
-    )
-    copies = [
-        pltpu.make_async_copy(
-            source.at[pl.ds(start, target.shape[0])], target, arrival.at[i]
-        )
-        for i, (start, source, target) in enumerate(zip(starts, sources, targets))
-    ]
-    for copy in copies:
-        copy.start()
-    meta_out_ref[...] = meta_ref[...]
-    for copy in copies:
-        copy.wait()
-
-
-def stack_kernel(*refs):
-    for i, ref in enumerate(refs[:-3]):
-        refs[-1][i] = ref[...]
+def stack_kernel(count, *refs):
+    out_ref, start = refs[-1], 0
+    for ref in refs[:count]:
+        if ref.ndim == 2:
+            out_ref[start] = ref[...]
+            start += 1
+        else:
+            out_ref[start : start + ref.shape[0]] = ref[...]
+            start += ref.shape[0]
 
 
 def rows_of(refs):
@@ -262,27 +250,20 @@
     return pltpu.with_memory_space_constraint(array, pltpu.HBM)
 
 
+def stack(values, extras=()):
+    rows, half = values[0].shape[-2:]
+    blocks = sum(value.size for value in values) // (rows * half)
+    return pl.pallas_call(
+        functools.partial(stack_kernel, len(values)),
+        in_specs=[VMEM] * (len(values) + len(extras)),
+        out_specs=VMEM,
+        out_shape=jax.ShapeDtypeStruct((blocks, rows, half), values[0].dtype),
+        compiler_params=pltpu.CompilerParams(vmem_limit_bytes=2 << 20),
+    )(*values, *extras)
+
+
 def near(array):
     return pltpu.with_memory_space_constraint(array, pltpu.VMEM)
-
-
-def fetch(meta, after, *wanted):
-    near = [
-        jax.ShapeDtypeStruct((count, weights.shape[1]), weights.dtype)
-        for weights, _, count in wanted
-    ]
-    *loaded, meta = pl.pallas_call(
-        functools.partial(fetch_kernel, [start for _, start, _ in wanted]),
-        in_specs=[VMEM, VMEM] + [HBM] * len(wanted),
-        out_specs=[VMEM] * (len(wanted) + 1),
-        out_shape=near + [jax.ShapeDtypeStruct(meta.shape, meta.dtype)],
-        scratch_shapes=[pltpu.SemaphoreType.DMA((len(wanted),))],
-        compiler_params=pltpu.CompilerParams(vmem_limit_bytes=1 << 20),
-        cost_estimate=pl.CostEstimate(
-            flops=0, bytes_accessed=2 * sum(array.size for array in near), transcendentals=0
-        ),
-    )(after, meta, *[far(weights) for weights, _, _ in wanted])
-    return loaded, meta
 
 
 def swap_devices(value, offset, devices):
@@ -316,7 +297,7 @@
     owners = devices // experts
     hidden, meta = pl.pallas_call(
         attend_kernel,
-        in_specs=[HBM] * 7,
+        in_specs=[HBM] * 8,
         out_specs=[VMEM] * 2,
         out_shape=[
             jax.ShapeDtypeStruct((rows, half), jnp.bfloat16),
@@ -326,35 +307,30 @@
             (pltpu.SMEM if array.dtype == jnp.int32 else pltpu.VMEM)(array.shape, array.dtype)
             for array in inputs
         ]
-        + [pltpu.SemaphoreType.DMA((7,))],
+        + [pltpu.VMEM((16, units), w_up.dtype), pltpu.SemaphoreType.DMA((8,))],
         compiler_params=pltpu.CompilerParams(vmem_limit_bytes=6 << 20),
-    )(*[far(array) for array in inputs])
-
-    offsets = [k * owners for k in range(experts)]
-    crossed = [swap_devices(hidden, offset, devices) for offset in offsets[1:]]
-    _, meta = fetch(meta, meta, (w_up, 0, 16))
-    w_gate, w_up, w_down = near(w_gate), near(w_up), near(w_down)
-    held = [
-        pl.pallas_call(
-            stack_kernel,
-            in_specs=[VMEM] * (experts + 2),
-            out_specs=VMEM,
-            out_shape=jax.ShapeDtypeStruct((experts, rows, half), jnp.bfloat16),
-            compiler_params=pltpu.CompilerParams(vmem_limit_bytes=2 << 20),
-        )(hidden, *crossed, meta, w_gate)
-    ]
-    step = 1
+    )(*[far(array) for array in inputs], far(w_up))
+
+    offsets, near_rows, step = [0], hidden, 1
     while step < owners:
-        if len(held) > 1:
-            held = [jnp.concatenate(held, axis=0)]
-        held.append(swap_devices(held[0], step, devices))
+        arrived = swap_devices(near_rows, step, devices)
+        extras = ()
+        if step == 1:
+            w_gate, w_up, w_down = near(w_gate), near(w_up), near(w_down)
+            extras = (meta, w_gate)
+        near_rows = stack((near_rows, arrived), extras)
         offsets += [offset ^ step for offset in offsets]
         step *= 2
-    others = [swap_cores(held[0])]
+    crossed = stack(
+        [swap_devices(near_rows, k * owners, devices) for k in range(1, experts)],
+        (w_up,),
+    )
+    offsets = [k * owners ^ offset for k in range(experts) for offset in offsets]
+    others = [swap_cores(near_rows)]
     meta_other = swap_cores(meta)
-    if len(held) > 1:
-        held[1], meta_other = lax.optimization_barrier((held[1], meta_other))
-        others.append(swap_cores(held[1]))
+    crossed, meta_other, others[0] = lax.optimization_barrier((crossed, meta_other, others[0]))
+    others.append(swap_cores(crossed))
+    held = [near_rows, crossed]
     parts = len(held)
     gates = pl.pallas_call(
         functools.partial(gate_kernel, block),

time: 38.2 us -> 37.8 us (0.990)
  Pallas kernels: 11.8 us -> 10.4 us
  starting transfers between devices: 8.4 us -> 8.97 us
  waiting for transfers between devices: 5.27 us -> 5.74 us
    pallas_call x3, Pallas kernels: 3.91 us -> 2.46 us  [the longest x1 2.45 us: on_device(): pl.pallas_call(attend_kernel, in_specs=[HBM] * 8, out_specs=[VMEM] * 2, o...]
    ppermute x4, waiting for transfers between devices: 4.57 us -> 5.64 us  [swap_devices(): lax.ppermute(value, 'devs', [(d, d ^ offset) for d in range(devices)])]
    ppermute x4, waiting for transfers between devices: 0.71 us -> 0.09 us  [swap_cores(): return lax.ppermute(value, 'pair', [(0, 1), (1, 0)])]
    ppermute x4, starting transfers between devices: 7.31 us -> 7.85 us  [swap_devices(): lax.ppermute(value, 'devs', [(d, d ^ offset) for d in range(devices)])]
  transfers between devices with their start and end apart: 8 -> 8, of which waited for: 3 -> 4; matrix products, arithmetic and copies ran while one was open for 0% -> 0% of each run, Pallas kernels for 10% -> 7%
where the time goes in v7:
time: 37.8 us; the launch traced here: 37.6 us
  blocking collectives  12.3 us (33%)
  Pallas kernels  10.4 us (28%)
  starting transfers between devices  8.97 us (24%)
  waiting for transfers between devices  5.74 us (15%)
    all_to_all x1, blocking collectives, on_device(): lax.all_to_all(summed, 'devs', split_axis=0, concat_axis=0, tiled=True)  12.3 us
    ppermute x4, starting transfers between devices, swap_devices(): lax.ppermute(value, 'devs', [(d, d ^ offset) for d in range(devices)])  7.85 us
    ppermute x4, waiting for transfers between devices, swap_devices(): lax.ppermute(value, 'devs', [(d, d ^ offset) for d in range(devices)])  5.64 us
    pallas_call x1, Pallas kernels, on_device(): pl.pallas_call(functools.partial(expert_kernel, block, experts, parts), i...  3.5 us
    pallas_call x2, Pallas kernels, project(): pl.pallas_call(functools.partial(down_kernel, piece, offsets, own), in_sp...  2.45 us
    pallas_call x1, Pallas kernels, on_device(): pl.pallas_call(attend_kernel, in_specs=[HBM] * 8, out_specs=[VMEM] * 2, o...  2.45 us
    pallas_call x1, Pallas kernels, on_device(): pl.pallas_call(functools.partial(gate_kernel, block), in_specs=[VMEM] * (...  1.23 us
    ppermute x4, starting transfers between devices, swap_cores(): return lax.ppermute(value, 'pair', [(0, 1), (1, 0)])  1.13 us
  transfers between devices with their start and end apart: 8, of which 4 were waited for; matrix products, arithmetic and copies ran while one was open for 0% of the time, Pallas kernels for 7%

profile of v7, /device:TPU:0, one launch (start us, length us, event | category | flops | bytes accessed | tf_op | source)
XLA Modules:
  0.0 37.6 jit_solution(15342790712298061435)
XLA Ops:
  0.0 2.4 %shard_map.100 = (bf16[8,1536]{1,0:T(8,128)(2,1)S(1)}, f32[8,128]{1,0:T(8,128)S(1)}) custom-call(bf16[2,4,1536]{2,1,0:T(4,128)(2,1)} %query_hbm.1, bf16[2,4,256,256]{3,2,1,0:T(8,128)(2,1)} %key_hbm.1, bf16[2,4,256,256]{3,2,1,0:T(8,128)(2,1)} %value_hbm.1, s32[2,4]{1,0:T(2,128)} %lengths_hbm.1, bf16[2,4,1536]{2,1,0:T(4,128)(2,1)} %residual_hbm.1, ...), custom_call_target="tpu_custom_call" | custom-call | tf_op jit(solution)/shard_map/pallas_call | solution.py:298
  2.5 3.0 %collective-permute-start = (bf16[8,1536]{1,0:T(8,128)(2,1)S(1)}, bf16[8,1536]{1,0:T(8,128)(2,1)S(1)}, u32[]{:S(2)}, u32[]{:S(2)}) collective-permute-start(bf16[8,1536]{1,0:T(8,128)(2,1)S(1)} %get-tuple-element.12.refs_0_.hidden_ref), channel_id=1, source_target_pairs={{0,2},{2,0},{4,6},{6,4},{8,10},{10,8},{12,14},{14,12},{1,3},{3,1},... | collective-permute-start | bytes 73736 | tf_op jit(solution)/shard_map/ppermute | solution.py:270
  5.5 1.8 %collective-permute-done.refs_1_ = bf16[8,1536]{1,0:T(8,128)(2,1)S(1)} collective-permute-done((bf16[8,1536]{1,0:T(8,128)(2,1)S(1)}, bf16[8,1536]{1,0:T(8,128)(2,1)S(1)}, u32[]{:S(2)}, u32[]{:S(2)}) %collective-permute-start) | collective-permute-done | bytes 24608 | tf_op jit(solution)/shard_map/ppermute | solution.py:270
  7.3 4.2 %collective-permute-start.3 = (bf16[2,8,1536]{2,1,0:T(8,128)(2,1)S(1)}, bf16[2,8,1536]{2,1,0:T(8,128)(2,1)S(1)}, u32[]{:S(2)}, u32[]{:S(2)}) collective-permute-start(bf16[2,8,1536]{2,1,0:T(8,128)(2,1)S(1)} %shard_map.101.refs_0_), channel_id=1, source_target_pairs={{0,12},{2,14},{4,8},{6,10},{8,4},{10,6},{12,0},{14,2},{1,13},{3,15... | collective-permute-start | bytes 147464 | tf_op jit(solution)/shard_map/ppermute | solution.py:270
  11.5 0.6 %collective-permute-start.1 = (bf16[2,8,1536]{2,1,0:T(8,128)(2,1)S(1)}, bf16[2,8,1536]{2,1,0:T(8,128)(2,1)S(1)}, u32[]{:S(2)}, u32[]{:S(2)}) collective-permute-start(bf16[2,8,1536]{2,1,0:T(8,128)(2,1)S(1)} %shard_map.101.refs_0_), channel_id=1, source_target_pairs={{0,4},{2,6},{4,0},{6,2},{8,12},{10,14},{12,8},{14,10},{1,5},{3,7},... | collective-permute-start | bytes 147464 | tf_op jit(solution)/shard_map/ppermute | solution.py:270
  12.1 0.0 collective-permute-start.5
  12.1 0.5 %collective-permute-start.4 = (f32[8,128]{1,0:T(8,128)S(1)}, f32[8,128]{1,0:T(8,128)S(1)}, u32[]{:S(2)}, u32[]{:S(2)}) collective-permute-start(f32[8,128]{1,0:T(8,128)S(1)} %get-tuple-element.13.refs_2_.refs_7_), channel_id=1, source_target_pairs={{0,1},{1,0},{2,3},{3,2},{4,5},{5,4},{6,7},{7,6},{8,9},{9,8},{10,11... | collective-permute-start | bytes 12296 | tf_op jit(solution)/shard_map/ppermute | solution.py:274
  12.6 1.0 %collective-permute-done.3.refs_2_ = bf16[2,8,1536]{2,1,0:T(8,128)(2,1)S(1)} collective-permute-done((bf16[2,8,1536]{2,1,0:T(8,128)(2,1)S(1)}, bf16[2,8,1536]{2,1,0:T(8,128)(2,1)S(1)}, u32[]{:S(2)}, u32[]{:S(2)}) %collective-permute-start.3) | collective-permute-done | bytes 49184 | tf_op jit(solution)/shard_map/ppermute | solution.py:270
  13.6 2.9 %collective-permute-done.2.refs_1_ = bf16[2,8,1536]{2,1,0:T(8,128)(2,1)S(1)} collective-permute-done((bf16[2,8,1536]{2,1,0:T(8,128)(2,1)S(1)}, bf16[2,8,1536]{2,1,0:T(8,128)(2,1)S(1)}, u32[]{:S(2)}, u32[]{:S(2)}) %collective-permute-start.2) | collective-permute-done | bytes 49184 | tf_op jit(solution)/shard_map/ppermute | solution.py:270
  16.5 0.0 collective-permute-done.1.refs_0_
  16.5 0.0 collective-permute-done.4.refs_8_
  16.5 0.1 collective-permute-start.6
  16.6 0.0 slice-start.3
  16.6 0.0 slice-start.4
  16.6 1.2 %shard_map.103.refs_6_ = f32[64,2048]{1,0:T(8,128)S(1)} custom-call(bf16[2,8,1536]{2,1,0:T(8,128)(2,1)S(1)} %shard_map.101.refs_0_, bf16[6,8,1536]{2,1,0:T(8,128)(2,1)S(1)} %shard_map.102.refs_1_, bf16[3072,2048]{1,0:T(8,128)(2,1)S(1)} %copy-done), custom_call_target="tpu_custom_call" | custom-call | flops 402653184 | bytes 6291456 | tf_op jit(solution)/shard_map/pallas_call | solution.py:335
  17.9 0.0 slice-start.5
  17.9 0.1 collective-permute-done.6.refs_3_
  18.0 3.5 %shard_map.104 = (bf16[64,2048]{1,0:T(8,128)(2,1)S(1)}, f32[8,128]{1,0:T(8,128)S(1)}) custom-call(bf16[2,8,1536]{2,1,0:T(8,128)(2,1)S(1)} %shard_map.101.refs_0_, bf16[6,8,1536]{2,1,0:T(8,128)(2,1)S(1)} %shard_map.102.refs_1_, bf16[2,8,1536]{2,1,0:T(8,128)(2,1)S(1)} %collective-permute-done.5.refs_2_, ...), custom_call_target="tpu_custom_call" | custom-call | tf_op jit(solution)/shard_map/pallas_call | solution.py:345
  21.5 0.0 slice-done.5
  21.5 1.2 %shard_map.106 = bf16[8,8,1536]{2,1,0:T(8,128)(2,1)S(1)} custom-call(bf16[64,2048]{1,0:T(8,128)(2,1)S(1)} %get-tuple-element.17.units_ref, bf16[2048,3072]{1,0:T(8,128)(2,1)S(1)} %bitcast.5), custom_call_target="tpu_custom_call" | custom-call | flops 402653184 | bytes 6291456 | tf_op jit(solution)/shard_map/pallas_call | solution.py:358
  22.8 0.5 %collective-permute-start.7 = (bf16[8,8,1536]{2,1,0:T(8,128)(2,1)S(1)}, bf16[8,8,1536]{2,1,0:T(8,128)(2,1)S(1)}, u32[]{:S(2)}, u32[]{:S(2)}) collective-permute-start(bf16[8,8,1536]{2,1,0:T(8,128)(2,1)S(1)} %shard_map.106), channel_id=1, source_target_pairs={{0,1},{1,0},{2,3},{3,2},{4,5},{5,4},{6,7},{7,6},{8,9},{9,8},{10,11... | collective-permute-start | bytes 589832 | tf_op jit(solution)/shard_map/ppermute | solution.py:274
  23.3 1.2 %shard_map.105.kept_ref = f32[8,8,1536]{2,1,0:T(8,128)S(1)} custom-call(bf16[64,2048]{1,0:T(8,128)(2,1)S(1)} %get-tuple-element.17.units_ref, bf16[2048,3072]{1,0:T(8,128)(2,1)S(1)} %bitcast.5), custom_call_target="tpu_custom_call" | custom-call | flops 402653184 | bytes 6291456 | tf_op jit(solution)/shard_map/pallas_call | solution.py:358
  24.6 12.3 %all_to_all.5.returned_ref = bf16[8,8,1536]{2,1,0:T(8,128)(2,1)S(1)} all-to-all(bf16[8,8,1536]{2,1,0:T(8,128)(2,1)S(1)} %shard_map.107), channel_id=1, replica_groups=mesh['groups'=2,'devs'=8,'pair'=2] {'devs'}, dimensions={0} | all-to-all | bytes 393216 | tf_op jit(solution)/shard_map/all_to_all | solution.py:380
  36.9 0.7 %shard_map.108 = bf16[2,4,1536]{2,1,0:T(4,128)(2,1)} custom-call(bf16[8,8,1536]{2,1,0:T(8,128)(2,1)S(1)} %all_to_all.5.returned_ref, bf16[8,1536]{1,0:T(8,128)(2,1)S(1)} %get-tuple-element.12.refs_0_.hidden_ref, f32[8,128]{1,0:T(8,128)S(1)} %get-tuple-element.18.weights_ref), custom_call_target="tpu_custom_call" | custom-call | tf_op jit(solution)/shard_map/pallas_call | solution.py:381
  (18 shorter events, 0.1 us)
Async XLA Ops:
  0.0 7.3 %copy-start = (bf16[3072,2048]{1,0:T(8,128)(2,1)S(1)}, bf16[3072,2048]{1,0:T(8,128)(2,1)}, u32[]{:S(2)}) copy-start(bf16[3072,2048]{1,0:T(8,128)(2,1)} %refs_5_.1) | copy-start | bytes 37748740
  0.0 16.5 %slice-start = ((s8[12582912]{0:T(1024)(128)(4,1)}), s8[4194304]{0:T(1024)(128)(4,1)S(1)}, s32[]{:S(2)}) async-start(s8[12582912]{0:T(1024)(128)(4,1)} %bitcast.2), calls=%async_computation.1 | async-start | bytes 8388608
  0.0 16.5 %slice-start.1 = ((s8[12582912]{0:T(1024)(128)(4,1)}), s8[4194304]{0:T(1024)(128)(4,1)S(1)}, s32[]{:S(2)}) async-start(s8[12582912]{0:T(1024)(128)(4,1)} %bitcast.2), calls=%async_computation.2 | async-start | bytes 8388608
  2.5 4.8 %collective-permute-start = (bf16[8,1536]{1,0:T(8,128)(2,1)S(1)}, bf16[8,1536]{1,0:T(8,128)(2,1)S(1)}, u32[]{:S(2)}, u32[]{:S(2)}) collective-permute-start(bf16[8,1536]{1,0:T(8,128)(2,1)S(1)} %get-tuple-element.12.refs_0_.hidden_ref), channel_id=1, source_target_pairs={{0,2},{2,0},{4,6},{6,4},{8,10},{10,8},{12,14},{14,12},{1,3},{3,1},... | collective-permute-start | bytes 73736 | tf_op jit(solution)/shard_map/ppermute | solution.py:270
  7.3 9.2 %slice-start.2 = ((s8[12582912]{0:T(1024)(128)(4,1)}), s8[4194304]{0:T(1024)(128)(4,1)S(1)}, s32[]{:S(2)}) async-start(s8[12582912]{0:T(1024)(128)(4,1)} %bitcast.2), calls=%async_computation.3 | async-start | bytes 8388608
  7.3 6.3 %collective-permute-start.3 = (bf16[2,8,1536]{2,1,0:T(8,128)(2,1)S(1)}, bf16[2,8,1536]{2,1,0:T(8,128)(2,1)S(1)}, u32[]{:S(2)}, u32[]{:S(2)}) collective-permute-start(bf16[2,8,1536]{2,1,0:T(8,128)(2,1)S(1)} %shard_map.101.refs_0_), channel_id=1, source_target_pairs={{0,12},{2,14},{4,8},{6,10},{8,4},{10,6},{12,0},{14,2},{1,13},{3,15... | collective-permute-start | bytes 147464 | tf_op jit(solution)/shard_map/ppermute | solution.py:270
  11.5 5.0 %collective-permute-start.2 = (bf16[2,8,1536]{2,1,0:T(8,128)(2,1)S(1)}, bf16[2,8,1536]{2,1,0:T(8,128)(2,1)S(1)}, u32[]{:S(2)}, u32[]{:S(2)}) collective-permute-start(bf16[2,8,1536]{2,1,0:T(8,128)(2,1)S(1)} %shard_map.101.refs_0_), channel_id=1, source_target_pairs={{0,8},{2,10},{4,12},{6,14},{8,0},{10,2},{12,4},{14,6},{1,9},{3,11}... | collective-permute-start | bytes 147464 | tf_op jit(solution)/shard_map/ppermute | solution.py:270
  11.5 5.0 %collective-permute-start.1 = (bf16[2,8,1536]{2,1,0:T(8,128)(2,1)S(1)}, bf16[2,8,1536]{2,1,0:T(8,128)(2,1)S(1)}, u32[]{:S(2)}, u32[]{:S(2)}) collective-permute-start(bf16[2,8,1536]{2,1,0:T(8,128)(2,1)S(1)} %shard_map.101.refs_0_), channel_id=1, source_target_pairs={{0,4},{2,6},{4,0},{6,2},{8,12},{10,14},{12,8},{14,10},{1,5},{3,7},... | collective-permute-start | bytes 147464 | tf_op jit(solution)/shard_map/ppermute | solution.py:270
  12.1 4.4 %collective-permute-start.5 = (bf16[2,8,1536]{2,1,0:T(8,128)(2,1)S(1)}, bf16[2,8,1536]{2,1,0:T(8,128)(2,1)S(1)}, u32[]{:S(2)}, u32[]{:S(2)}) collective-permute-start(bf16[2,8,1536]{2,1,0:T(8,128)(2,1)S(1)} %shard_map.101.refs_0_), channel_id=1, source_target_pairs={{0,1},{1,0},{2,3},{3,2},{4,5},{5,4},{6,7},{7,6},{8,9},{9,8},{10,11... | collective-permute-start | bytes 147464 | tf_op jit(solution)/shard_map/ppermute | solution.py:274
  12.1 4.4 %collective-permute-start.4 = (f32[8,128]{1,0:T(8,128)S(1)}, f32[8,128]{1,0:T(8,128)S(1)}, u32[]{:S(2)}, u32[]{:S(2)}) collective-permute-start(f32[8,128]{1,0:T(8,128)S(1)} %get-tuple-element.13.refs_2_.refs_7_), channel_id=1, source_target_pairs={{0,1},{1,0},{2,3},{3,2},{4,5},{5,4},{6,7},{7,6},{8,9},{9,8},{10,11... | collective-permute-start | bytes 12296 | tf_op jit(solution)/shard_map/ppermute | solution.py:274
  16.5 1.4 %collective-permute-start.6 = (bf16[6,8,1536]{2,1,0:T(8,128)(2,1)S(1)}, bf16[6,8,1536]{2,1,0:T(8,128)(2,1)S(1)}, u32[]{:S(2)}, u32[]{:S(2)}) collective-permute-start(bf16[6,8,1536]{2,1,0:T(8,128)(2,1)S(1)} %shard_map.102.refs_1_), channel_id=1, source_target_pairs={{0,1},{1,0},{2,3},{3,2},{4,5},{5,4},{6,7},{7,6},{8,9},{9,8},{10,11... | collective-permute-start | bytes 442376 | tf_op jit(solution)/shard_map/ppermute | solution.py:274
  16.6 4.9 %slice-start.3 = ((s8[12582912]{0:T(1024)(128)(4,1)}), s8[4194304]{0:T(1024)(128)(4,1)S(1)}, s32[]{:S(2)}) async-start(s8[12582912]{0:T(1024)(128)(4,1)} %bitcast.4), calls=%async_computation.4 | async-start | bytes 8388608
  16.6 4.9 %slice-start.4 = ((s8[12582912]{0:T(1024)(128)(4,1)}), s8[4194304]{0:T(1024)(128)(4,1)S(1)}, s32[]{:S(2)}) async-start(s8[12582912]{0:T(1024)(128)(4,1)} %bitcast.4), calls=%async_computation.5 | async-start | bytes 8388608
  17.9 3.6 %slice-start.5 = ((s8[12582912]{0:T(1024)(128)(4,1)}), s8[4194304]{0:T(1024)(128)(4,1)S(1)}, s32[]{:S(2)}) async-start(s8[12582912]{0:T(1024)(128)(4,1)} %bitcast.4), calls=%async_computation.6 | async-start | bytes 8388608
  22.8 1.8 %collective-permute-start.7 = (bf16[8,8,1536]{2,1,0:T(8,128)(2,1)S(1)}, bf16[8,8,1536]{2,1,0:T(8,128)(2,1)S(1)}, u32[]{:S(2)}, u32[]{:S(2)}) collective-permute-start(bf16[8,8,1536]{2,1,0:T(8,128)(2,1)S(1)} %shard_map.106), channel_id=1, source_target_pairs={{0,1},{1,0},{2,3},{3,2},{4,5},{5,4},{6,7},{7,6},{8,9},{9,8},{10,11... | collective-permute-start | bytes 589832 | tf_op jit(solution)/shard_map/ppermute | solution.py:274

commit v8 on v7

--- a/solution.py
+++ b/solution.py
@@ -156,13 +156,10 @@
         )
 
 
-def store_rows(offsets, target, columns, product):
-    me = lax.axis_index("devs")
-    rows = target.shape[1]
-    for j, offset in enumerate(offsets):
-        target[lax.bitwise_xor(me, offset), :, columns] = product[
-            j * rows : (j + 1) * rows
-        ].astype(target.dtype)
+def store_rows(target, columns, product):
+    blocks, rows, _ = target.shape
+    for j in range(blocks):
+        target[j, :, columns] = product[j * rows : (j + 1) * rows].astype(target.dtype)
 
 
 def expert_kernel(block, experts, parts, *refs):
@@ -213,7 +210,7 @@
     ) + jnp.where(lane == second, jax.nn.sigmoid(logit_second - logit_first), 0.0)
 
 
-def down_kernel(piece, offsets, own, units_ref, down_ref, out_ref):
+def down_kernel(piece, own, units_ref, down_ref, out_ref):
     half = out_ref.shape[-1]
     base = half_starts(half)[0 if own else 1]
     for start in range(0, half, piece):
@@ -221,23 +218,44 @@
         product = jnp.dot(
             units_ref[...], down_ref[:, columns], preferred_element_type=jnp.float32
         )
-        store_rows(offsets, out_ref, slice(start, start + piece), product)
-
-
-def add_kernel(kept_ref, received_ref, out_ref):
-    out_ref[...] = (kept_ref[...] + received_ref[...].astype(jnp.float32)).astype(jnp.bfloat16)
-
-
-def combine_kernel(experts, returned_ref, hidden_ref, weights_ref, out_ref):
-    devices = returned_ref.shape[0]
+        store_rows(out_ref, slice(start, start + piece), product)
+
+
+def add_kernel(kept_ref, received_ref, near_ref, *far_refs):
+    total = kept_ref[...] + received_ref[...].astype(jnp.float32)
+    size = near_ref.shape[0]
+    near_ref[...] = total[:size]
+    for i, ref in enumerate(far_refs):
+        start = size + i * ref.shape[0]
+        ref[...] = total[start : start + ref.shape[0]].astype(jnp.bfloat16)
+
+
+def mix_kernel(owners, weights_ref, *refs):
+    *expert_refs, kept_ref, sent_ref = refs
+    home = lax.axis_index("devs") // owners
+    lane = lax.broadcasted_iota(jnp.int32, weights_ref.shape[1:], 1)
+    for block in range(owners):
+        weights = weights_ref[block]
+        total = None
+        for k, ref in enumerate(expert_refs):
+            mine = lane == lax.bitwise_xor(home, k)
+            weight = jnp.sum(jnp.where(mine, weights, 0.0), axis=-1, keepdims=True)
+            product = weight * ref[block].astype(jnp.float32)
+            total = product if total is None else total + product
+        kept = kept_ref.shape[0]
+        if block < kept:
+            kept_ref[block] = total
+        else:
+            sent_ref[block - kept] = total.astype(jnp.bfloat16)
+
+
+def finish_kernel(hidden_ref, kept_ref, received_ref, out_ref):
     batches, per_batch, _ = out_ref.shape
-    owners = devices // experts
-    result = hidden_ref[...].astype(jnp.float32)
-    for e in range(experts):
-        expert_out = returned_ref[e * owners].astype(jnp.float32)
-        for o in range(1, owners):
-            expert_out += returned_ref[e * owners + o].astype(jnp.float32)
-        result += weights_ref[:, e : e + 1] * expert_out
+    result = (
+        hidden_ref[...].astype(jnp.float32)
+        + kept_ref[0]
+        + received_ref[0].astype(jnp.float32)
+    )
     for b in range(batches):
         out_ref[b] = result[b * per_batch : (b + 1) * per_batch].astype(jnp.bfloat16)
 
@@ -260,6 +278,19 @@
         out_shape=jax.ShapeDtypeStruct((blocks, rows, half), values[0].dtype),
         compiler_params=pltpu.CompilerParams(vmem_limit_bytes=2 << 20),
     )(*values, *extras)
+
+
+def add(kept, received, count):
+    blocks, rows, half = kept.shape
+    size = blocks // (count + 1)
+    return pl.pallas_call(
+        add_kernel,
+        in_specs=[VMEM] * 2,
+        out_specs=[VMEM] * (count + 1),
+        out_shape=[jax.ShapeDtypeStruct((size, rows, half), jnp.float32)]
+        + [jax.ShapeDtypeStruct((size, rows, half), jnp.bfloat16)] * count,
+        compiler_params=pltpu.CompilerParams(vmem_limit_bytes=min(48, max(4, blocks // 2)) << 20),
+    )(kept, received)
 
 
 def near(array):
@@ -356,7 +387,7 @@
 
     def project(own, dtype):
         return pl.pallas_call(
-            functools.partial(down_kernel, piece, offsets, own),
+            functools.partial(down_kernel, piece, own),
             in_specs=[VMEM] * 2,
             out_specs=VMEM,
             out_shape=jax.ShapeDtypeStruct((devices, rows, half), dtype),
@@ -370,21 +401,37 @@
 
     received = swap_cores(project(False, jnp.bfloat16))
     kept = project(True, jnp.float32)
-    summed = pl.pallas_call(
-        add_kernel,
-        in_specs=[VMEM] * 2,
-        out_specs=VMEM,
-        out_shape=jax.ShapeDtypeStruct((devices, rows, half), jnp.bfloat16),
-        compiler_params=pltpu.CompilerParams(vmem_limit_bytes=min(48, count // 16) << 20),
-    )(kept, received)
-    returned = lax.all_to_all(summed, "devs", split_axis=0, concat_axis=0, tiled=True)
+    kept, *sent = add(kept, received, experts - 1)
+    returned = [
+        swap_devices(value, k * owners, devices) for k, value in enumerate(sent, 1)
+    ]
+    weights_all, reach = weights, 1
+    while reach < owners:
+        weights_all = stack((weights_all, swap_devices(weights_all, reach, devices)))
+        reach *= 2
+    step = owners // 2
+    kept, sent = pl.pallas_call(
+        functools.partial(mix_kernel, owners),
+        in_specs=[VMEM] * (experts + 1),
+        out_specs=[VMEM] * 2,
+        out_shape=[
+            jax.ShapeDtypeStruct((step, rows, half), jnp.float32),
+            jax.ShapeDtypeStruct((step, rows, half), jnp.bfloat16),
+        ],
+        compiler_params=pltpu.CompilerParams(vmem_limit_bytes=min(48, max(4, owners)) << 20),
+    )(weights_all, kept, *returned)
+    received = swap_devices(sent, step, devices)
+    while step > 1:
+        step //= 2
+        kept, sent = add(kept, received, 1)
+        received = swap_devices(sent, step, devices)
     return pl.pallas_call(
-        functools.partial(combine_kernel, experts),
+        finish_kernel,
         in_specs=[VMEM] * 3,
         out_specs=VMEM,
         out_shape=jax.ShapeDtypeStruct(query.shape, jnp.bfloat16),
-        compiler_params=pltpu.CompilerParams(vmem_limit_bytes=6 << 20),
-    )(returned, hidden, weights)
+        compiler_params=pltpu.CompilerParams(vmem_limit_bytes=4 << 20),
+    )(hidden, kept, received)
 
 
 def solution(mesh):

time: 37.8 us -> 37.5 us (level)
  blocking collectives: 12.3 us -> 0 us
  starting transfers between devices: 8.97 us -> 16.5 us
  waiting for transfers between devices: 5.74 us -> 10.2 us
    all_to_all x1 -> x0, blocking collectives: 12.3 us -> none  [on_device(): lax.all_to_all(summed, 'devs', split_axis=0, concat_axis=0, tiled=True)]
    ppermute x4 -> x9, starting transfers between devices: 7.85 us -> 15.3 us  [swap_devices(): lax.ppermute(value, 'devs', [(d, d ^ offset) for d in range(devices)])]
    ppermute x4 -> x9, waiting for transfers between devices: 5.64 us -> 10.1 us  [swap_devices(): lax.ppermute(value, 'devs', [(d, d ^ offset) for d in range(devices)])]
    pallas_call x4 -> x5, Pallas kernels: 3.18 us -> 3.24 us  [the longest x2 2.45 us: project(): pl.pallas_call(functools.partial(down_kernel, piece, own), in_specs=[VMEM...]
  transfers between devices with their start and end apart: 8 -> 13, of which waited for: 4 -> 6; matrix products, arithmetic and copies ran while one was open for 0% -> 0% of each run, Pallas kernels for 7% -> 7%
where the time goes in v8:
time: 37.5 us; the launch traced here: 37.3 us
  starting transfers between devices  16.5 us (44%)
  Pallas kernels  10.4 us (28%)
  waiting for transfers between devices  10.2 us (27%)
    ppermute x9, starting transfers between devices, swap_devices(): lax.ppermute(value, 'devs', [(d, d ^ offset) for d in range(devices)])  15.3 us
    ppermute x9, waiting for transfers between devices, swap_devices(): lax.ppermute(value, 'devs', [(d, d ^ offset) for d in range(devices)])  10.1 us
    pallas_call x1, Pallas kernels, on_device(): pl.pallas_call(functools.partial(expert_kernel, block, experts, parts), i...  3.5 us
    pallas_call x2, Pallas kernels, project(): pl.pallas_call(functools.partial(down_kernel, piece, own), in_specs=[VMEM...  2.45 us
    pallas_call x1, Pallas kernels, on_device(): pl.pallas_call(attend_kernel, in_specs=[HBM] * 8, out_specs=[VMEM] * 2, o...  2.45 us
    pallas_call x1, Pallas kernels, on_device(): pl.pallas_call(functools.partial(gate_kernel, block), in_specs=[VMEM] * (...  1.23 us
    ppermute x4, starting transfers between devices, swap_cores(): return lax.ppermute(value, 'pair', [(0, 1), (1, 0)])  1.13 us
  transfers between devices with their start and end apart: 13, of which 6 were waited for; matrix products, arithmetic and copies ran while one was open for 0% of the time, Pallas kernels for 7%

profile of v8, /device:TPU:0, one launch (start us, length us, event | category | flops | bytes accessed | tf_op | source)
XLA Modules:
  0.0 37.3 jit_solution(243814254508185496)
XLA Ops:
  0.0 2.4 %shard_map.100 = (bf16[8,1536]{1,0:T(8,128)(2,1)S(1)}, f32[8,128]{1,0:T(8,128)S(1)}) custom-call(bf16[2,4,1536]{2,1,0:T(4,128)(2,1)} %query_hbm.1, bf16[2,4,256,256]{3,2,1,0:T(8,128)(2,1)} %key_hbm.1, bf16[2,4,256,256]{3,2,1,0:T(8,128)(2,1)} %value_hbm.1, s32[2,4]{1,0:T(2,128)} %lengths_hbm.1, bf16[2,4,1536]{2,1,0:T(4,128)(2,1)} %residual_hbm.1, ...), custom_call_target="tpu_custom_call" | custom-call | tf_op jit(solution)/shard_map/pallas_call | solution.py:329
  2.5 3.0 %collective-permute-start = (bf16[8,1536]{1,0:T(8,128)(2,1)S(1)}, bf16[8,1536]{1,0:T(8,128)(2,1)S(1)}, u32[]{:S(2)}, u32[]{:S(2)}) collective-permute-start(bf16[8,1536]{1,0:T(8,128)(2,1)S(1)} %get-tuple-element.18.refs_0_.hidden_ref), channel_id=1, source_target_pairs={{0,2},{2,0},{4,6},{6,4},{8,10},{10,8},{12,14},{14,12},{1,3},{3,1},... | collective-permute-start | bytes 73736 | tf_op jit(solution)/shard_map/ppermute | solution.py:301
  5.5 1.8 %collective-permute-done.refs_1_ = bf16[8,1536]{1,0:T(8,128)(2,1)S(1)} collective-permute-done((bf16[8,1536]{1,0:T(8,128)(2,1)S(1)}, bf16[8,1536]{1,0:T(8,128)(2,1)S(1)}, u32[]{:S(2)}, u32[]{:S(2)}) %collective-permute-start) | collective-permute-done | bytes 24608 | tf_op jit(solution)/shard_map/ppermute | solution.py:301
  7.3 4.2 %collective-permute-start.3 = (bf16[2,8,1536]{2,1,0:T(8,128)(2,1)S(1)}, bf16[2,8,1536]{2,1,0:T(8,128)(2,1)S(1)}, u32[]{:S(2)}, u32[]{:S(2)}) collective-permute-start(bf16[2,8,1536]{2,1,0:T(8,128)(2,1)S(1)} %shard_map.101.refs_0_), channel_id=1, source_target_pairs={{0,12},{2,14},{4,8},{6,10},{8,4},{10,6},{12,0},{14,2},{1,13},{3,15... | collective-permute-start | bytes 147464 | tf_op jit(solution)/shard_map/ppermute | solution.py:301
  11.5 0.6 %collective-permute-start.1 = (bf16[2,8,1536]{2,1,0:T(8,128)(2,1)S(1)}, bf16[2,8,1536]{2,1,0:T(8,128)(2,1)S(1)}, u32[]{:S(2)}, u32[]{:S(2)}) collective-permute-start(bf16[2,8,1536]{2,1,0:T(8,128)(2,1)S(1)} %shard_map.101.refs_0_), channel_id=1, source_target_pairs={{0,4},{2,6},{4,0},{6,2},{8,12},{10,14},{12,8},{14,10},{1,5},{3,7},... | collective-permute-start | bytes 147464 | tf_op jit(solution)/shard_map/ppermute | solution.py:301
  12.1 0.5 %collective-permute-start.4 = (f32[8,128]{1,0:T(8,128)S(1)}, f32[8,128]{1,0:T(8,128)S(1)}, u32[]{:S(2)}, u32[]{:S(2)}) collective-permute-start(f32[8,128]{1,0:T(8,128)S(1)} %get-tuple-element.19.refs_2_.refs_7_), channel_id=1, source_target_pairs={{0,1},{1,0},{2,3},{3,2},{4,5},{5,4},{6,7},{7,6},{8,9},{9,8},{10,11... | collective-permute-start | bytes 12296 | tf_op jit(solution)/shard_map/ppermute | solution.py:305
  12.6 1.0 %collective-permute-done.3.refs_2_ = bf16[2,8,1536]{2,1,0:T(8,128)(2,1)S(1)} collective-permute-done((bf16[2,8,1536]{2,1,0:T(8,128)(2,1)S(1)}, bf16[2,8,1536]{2,1,0:T(8,128)(2,1)S(1)}, u32[]{:S(2)}, u32[]{:S(2)}) %collective-permute-start.3) | collective-permute-done | bytes 49184 | tf_op jit(solution)/shard_map/ppermute | solution.py:301
  13.6 2.9 %collective-permute-done.2.refs_1_ = bf16[2,8,1536]{2,1,0:T(8,128)(2,1)S(1)} collective-permute-done((bf16[2,8,1536]{2,1,0:T(8,128)(2,1)S(1)}, bf16[2,8,1536]{2,1,0:T(8,128)(2,1)S(1)}, u32[]{:S(2)}, u32[]{:S(2)}) %collective-permute-start.2) | collective-permute-done | bytes 49184 | tf_op jit(solution)/shard_map/ppermute | solution.py:301
  16.5 0.1 collective-permute-start.6
  16.6 1.2 %shard_map.103.refs_6_ = f32[64,2048]{1,0:T(8,128)S(1)} custom-call(bf16[2,8,1536]{2,1,0:T(8,128)(2,1)S(1)} %shard_map.101.refs_0_, bf16[6,8,1536]{2,1,0:T(8,128)(2,1)S(1)} %shard_map.102.refs_1_, bf16[3072,2048]{1,0:T(8,128)(2,1)S(1)} %copy-done), custom_call_target="tpu_custom_call" | custom-call | flops 402653184 | bytes 6291456 | tf_op jit(solution)/shard_map/pallas_call | solution.py:366
  17.9 0.1 collective-permute-done.6.refs_3_
  18.0 3.5 %shard_map.104 = (bf16[64,2048]{1,0:T(8,128)(2,1)S(1)}, f32[8,128]{1,0:T(8,128)S(1)}) custom-call(bf16[2,8,1536]{2,1,0:T(8,128)(2,1)S(1)} %shard_map.101.refs_0_, bf16[6,8,1536]{2,1,0:T(8,128)(2,1)S(1)} %shard_map.102.refs_1_, bf16[2,8,1536]{2,1,0:T(8,128)(2,1)S(1)} %collective-permute-done.5.refs_2_, ...), custom_call_target="tpu_custom_call" | custom-call | tf_op jit(solution)/shard_map/pallas_call | solution.py:376
  21.5 1.2 %shard_map.107 = bf16[8,8,1536]{2,1,0:T(8,128)(2,1)S(1)} custom-call(bf16[64,2048]{1,0:T(8,128)(2,1)S(1)} %get-tuple-element.24.units_ref, bf16[2048,3072]{1,0:T(8,128)(2,1)S(1)} %bitcast.5), custom_call_target="tpu_custom_call" | custom-call | flops 402653184 | bytes 6291456 | tf_op jit(solution)/shard_map/pallas_call | solution.py:389
  22.8 0.5 %collective-permute-start.8 = (bf16[8,8,1536]{2,1,0:T(8,128)(2,1)S(1)}, bf16[8,8,1536]{2,1,0:T(8,128)(2,1)S(1)}, u32[]{:S(2)}, u32[]{:S(2)}) collective-permute-start(bf16[8,8,1536]{2,1,0:T(8,128)(2,1)S(1)} %shard_map.107), channel_id=1, source_target_pairs={{0,1},{1,0},{2,3},{3,2},{4,5},{5,4},{6,7},{7,6},{8,9},{9,8},{10,11... | collective-permute-start | bytes 589832 | tf_op jit(solution)/shard_map/ppermute | solution.py:305
  23.3 1.2 %shard_map.106.kept_ref = f32[8,8,1536]{2,1,0:T(8,128)S(1)} custom-call(bf16[64,2048]{1,0:T(8,128)(2,1)S(1)} %get-tuple-element.24.units_ref, bf16[2048,3072]{1,0:T(8,128)(2,1)S(1)} %bitcast.5), custom_call_target="tpu_custom_call" | custom-call | flops 402653184 | bytes 6291456 | tf_op jit(solution)/shard_map/pallas_call | solution.py:389
  24.6 0.2 collective-permute-start.9
  24.8 2.0 %collective-permute-start.10 = (bf16[2,8,1536]{2,1,0:T(8,128)(2,1)S(1)}, bf16[2,8,1536]{2,1,0:T(8,128)(2,1)S(1)}, u32[]{:S(2)}, u32[]{:S(2)}) collective-permute-start(bf16[2,8,1536]{2,1,0:T(8,128)(2,1)S(1)} %get-tuple-element.27), channel_id=1, source_target_pairs={{0,8},{2,10},{4,12},{6,14},{8,0},{10,2},{12,4},{14,6},{1,9},{3,11}... | collective-permute-start | bytes 147464 | tf_op jit(solution)/shard_map/ppermute | solution.py:301
  26.7 2.3 %collective-permute-start.11 = (bf16[2,8,1536]{2,1,0:T(8,128)(2,1)S(1)}, bf16[2,8,1536]{2,1,0:T(8,128)(2,1)S(1)}, u32[]{:S(2)}, u32[]{:S(2)}) collective-permute-start(bf16[2,8,1536]{2,1,0:T(8,128)(2,1)S(1)} %get-tuple-element.28), channel_id=1, source_target_pairs={{0,12},{2,14},{4,8},{6,10},{8,4},{10,6},{12,0},{14,2},{1,13},{3,15... | collective-permute-start | bytes 147464 | tf_op jit(solution)/shard_map/ppermute | solution.py:301
  29.0 1.5 %collective-permute-start.7 = (f32[8,128]{1,0:T(8,128)S(1)}, f32[8,128]{1,0:T(8,128)S(1)}, u32[]{:S(2)}, u32[]{:S(2)}) collective-permute-start(f32[8,128]{1,0:T(8,128)S(1)} %get-tuple-element.23.refs_0_), channel_id=1, source_target_pairs={{0,2},{2,0},{4,6},{6,4},{8,10},{10,8},{12,14},{14,12},{1,3},{3,1},... | collective-permute-start | bytes 12296 | tf_op jit(solution)/shard_map/ppermute | solution.py:301
  30.5 2.1 %collective-permute-done.7.refs_1_ = f32[8,128]{1,0:T(8,128)S(1)} collective-permute-done((f32[8,128]{1,0:T(8,128)S(1)}, f32[8,128]{1,0:T(8,128)S(1)}, u32[]{:S(2)}, u32[]{:S(2)}) %collective-permute-start.7) | collective-permute-done | bytes 4128 | tf_op jit(solution)/shard_map/ppermute | solution.py:301
  32.7 0.1 shard_map.109
  32.8 1.6 %collective-permute-start.12 = (bf16[1,8,1536]{2,1,0:T(8,128)(2,1)S(1)}, bf16[1,8,1536]{2,1,0:T(8,128)(2,1)S(1)}, u32[]{:S(2)}, u32[]{:S(2)}) collective-permute-start(bf16[1,8,1536]{2,1,0:T(8,128)(2,1)S(1)} %get-tuple-element.30), channel_id=1, source_target_pairs={{0,2},{2,0},{4,6},{6,4},{8,10},{10,8},{12,14},{14,12},{1,3},{3,1},... | collective-permute-start | bytes 73736 | tf_op jit(solution)/shard_map/ppermute | solution.py:301
  34.4 2.3 %collective-permute-done.12.received_ref = bf16[1,8,1536]{2,1,0:T(8,128)(2,1)S(1)} collective-permute-done((bf16[1,8,1536]{2,1,0:T(8,128)(2,1)S(1)}, bf16[1,8,1536]{2,1,0:T(8,128)(2,1)S(1)}, u32[]{:S(2)}, u32[]{:S(2)}) %collective-permute-start.12) | collective-permute-done | bytes 24608 | tf_op jit(solution)/shard_map/ppermute | solution.py:301
  36.7 0.6 %shard_map.110 = bf16[2,4,1536]{2,1,0:T(4,128)(2,1)} custom-call(bf16[8,1536]{1,0:T(8,128)(2,1)S(1)} %get-tuple-element.18.refs_0_.hidden_ref, f32[1,8,1536]{2,1,0:T(8,128)S(1)} %get-tuple-element.29.kept_ref, bf16[1,8,1536]{2,1,0:T(8,128)(2,1)S(1)} %collective-permute-done.12.received_ref), custom_call_target="tpu_custom_call" | custom-call | tf_op jit(solution)/shard_map/pallas_call | solution.py:428
  (29 shorter events, 0.2 us)
Async XLA Ops:
  0.0 7.3 %copy-start = (bf16[3072,2048]{1,0:T(8,128)(2,1)S(1)}, bf16[3072,2048]{1,0:T(8,128)(2,1)}, u32[]{:S(2)}) copy-start(bf16[3072,2048]{1,0:T(8,128)(2,1)} %refs_5_.1) | copy-start | bytes 37748740
  0.0 16.5 %slice-start = ((s8[12582912]{0:T(1024)(128)(4,1)}), s8[4194304]{0:T(1024)(128)(4,1)S(1)}, s32[]{:S(2)}) async-start(s8[12582912]{0:T(1024)(128)(4,1)} %bitcast.2), calls=%async_computation | async-start | bytes 8388608
  0.0 16.5 %slice-start.1 = ((s8[12582912]{0:T(1024)(128)(4,1)}), s8[4194304]{0:T(1024)(128)(4,1)S(1)}, s32[]{:S(2)}) async-start(s8[12582912]{0:T(1024)(128)(4,1)} %bitcast.2), calls=%async_computation.1 | async-start | bytes 8388608
  2.5 4.8 %collective-permute-start = (bf16[8,1536]{1,0:T(8,128)(2,1)S(1)}, bf16[8,1536]{1,0:T(8,128)(2,1)S(1)}, u32[]{:S(2)}, u32[]{:S(2)}) collective-permute-start(bf16[8,1536]{1,0:T(8,128)(2,1)S(1)} %get-tuple-element.18.refs_0_.hidden_ref), channel_id=1, source_target_pairs={{0,2},{2,0},{4,6},{6,4},{8,10},{10,8},{12,14},{14,12},{1,3},{3,1},... | collective-permute-start | bytes 73736 | tf_op jit(solution)/shard_map/ppermute | solution.py:301
  7.3 9.2 %slice-start.2 = ((s8[12582912]{0:T(1024)(128)(4,1)}), s8[4194304]{0:T(1024)(128)(4,1)S(1)}, s32[]{:S(2)}) async-start(s8[12582912]{0:T(1024)(128)(4,1)} %bitcast.2), calls=%async_computation.2 | async-start | bytes 8388608
  7.3 6.3 %collective-permute-start.3 = (bf16[2,8,1536]{2,1,0:T(8,128)(2,1)S(1)}, bf16[2,8,1536]{2,1,0:T(8,128)(2,1)S(1)}, u32[]{:S(2)}, u32[]{:S(2)}) collective-permute-start(bf16[2,8,1536]{2,1,0:T(8,128)(2,1)S(1)} %shard_map.101.refs_0_), channel_id=1, source_target_pairs={{0,12},{2,14},{4,8},{6,10},{8,4},{10,6},{12,0},{14,2},{1,13},{3,15... | collective-permute-start | bytes 147464 | tf_op jit(solution)/shard_map/ppermute | solution.py:301
  11.5 5.0 %collective-permute-start.2 = (bf16[2,8,1536]{2,1,0:T(8,128)(2,1)S(1)}, bf16[2,8,1536]{2,1,0:T(8,128)(2,1)S(1)}, u32[]{:S(2)}, u32[]{:S(2)}) collective-permute-start(bf16[2,8,1536]{2,1,0:T(8,128)(2,1)S(1)} %shard_map.101.refs_0_), channel_id=1, source_target_pairs={{0,8},{2,10},{4,12},{6,14},{8,0},{10,2},{12,4},{14,6},{1,9},{3,11}... | collective-permute-start | bytes 147464 | tf_op jit(solution)/shard_map/ppermute | solution.py:301
  11.5 5.0 %collective-permute-start.1 = (bf16[2,8,1536]{2,1,0:T(8,128)(2,1)S(1)}, bf16[2,8,1536]{2,1,0:T(8,128)(2,1)S(1)}, u32[]{:S(2)}, u32[]{:S(2)}) collective-permute-start(bf16[2,8,1536]{2,1,0:T(8,128)(2,1)S(1)} %shard_map.101.refs_0_), channel_id=1, source_target_pairs={{0,4},{2,6},{4,0},{6,2},{8,12},{10,14},{12,8},{14,10},{1,5},{3,7},... | collective-permute-start | bytes 147464 | tf_op jit(solution)/shard_map/ppermute | solution.py:301
  12.1 4.4 %collective-permute-start.5 = (bf16[2,8,1536]{2,1,0:T(8,128)(2,1)S(1)}, bf16[2,8,1536]{2,1,0:T(8,128)(2,1)S(1)}, u32[]{:S(2)}, u32[]{:S(2)}) collective-permute-start(bf16[2,8,1536]{2,1,0:T(8,128)(2,1)S(1)} %shard_map.101.refs_0_), channel_id=1, source_target_pairs={{0,1},{1,0},{2,3},{3,2},{4,5},{5,4},{6,7},{7,6},{8,9},{9,8},{10,11... | collective-permute-start | bytes 147464 | tf_op jit(solution)/shard_map/ppermute | solution.py:305
  12.1 4.4 %collective-permute-start.4 = (f32[8,128]{1,0:T(8,128)S(1)}, f32[8,128]{1,0:T(8,128)S(1)}, u32[]{:S(2)}, u32[]{:S(2)}) collective-permute-start(f32[8,128]{1,0:T(8,128)S(1)} %get-tuple-element.19.refs_2_.refs_7_), channel_id=1, source_target_pairs={{0,1},{1,0},{2,3},{3,2},{4,5},{5,4},{6,7},{7,6},{8,9},{9,8},{10,11... | collective-permute-start | bytes 12296 | tf_op jit(solution)/shard_map/ppermute | solution.py:305
  16.5 1.4 %collective-permute-start.6 = (bf16[6,8,1536]{2,1,0:T(8,128)(2,1)S(1)}, bf16[6,8,1536]{2,1,0:T(8,128)(2,1)S(1)}, u32[]{:S(2)}, u32[]{:S(2)}) collective-permute-start(bf16[6,8,1536]{2,1,0:T(8,128)(2,1)S(1)} %shard_map.102.refs_1_), channel_id=1, source_target_pairs={{0,1},{1,0},{2,3},{3,2},{4,5},{5,4},{6,7},{7,6},{8,9},{9,8},{10,11... | collective-permute-start | bytes 442376 | tf_op jit(solution)/shard_map/ppermute | solution.py:305
  16.6 4.9 %slice-start.3 = ((s8[12582912]{0:T(1024)(128)(4,1)}), s8[4194304]{0:T(1024)(128)(4,1)S(1)}, s32[]{:S(2)}) async-start(s8[12582912]{0:T(1024)(128)(4,1)} %bitcast.4), calls=%async_computation.3 | async-start | bytes 8388608
  16.6 4.9 %slice-start.4 = ((s8[12582912]{0:T(1024)(128)(4,1)}), s8[4194304]{0:T(1024)(128)(4,1)S(1)}, s32[]{:S(2)}) async-start(s8[12582912]{0:T(1024)(128)(4,1)} %bitcast.4), calls=%async_computation.4 | async-start | bytes 8388608
  17.9 3.6 %slice-start.5 = ((s8[12582912]{0:T(1024)(128)(4,1)}), s8[4194304]{0:T(1024)(128)(4,1)S(1)}, s32[]{:S(2)}) async-start(s8[12582912]{0:T(1024)(128)(4,1)} %bitcast.4), calls=%async_computation.5 | async-start | bytes 8388608
  22.8 1.8 %collective-permute-start.8 = (bf16[8,8,1536]{2,1,0:T(8,128)(2,1)S(1)}, bf16[8,8,1536]{2,1,0:T(8,128)(2,1)S(1)}, u32[]{:S(2)}, u32[]{:S(2)}) collective-permute-start(bf16[8,8,1536]{2,1,0:T(8,128)(2,1)S(1)} %shard_map.107), channel_id=1, source_target_pairs={{0,1},{1,0},{2,3},{3,2},{4,5},{5,4},{6,7},{7,6},{8,9},{9,8},{10,11... | collective-permute-start | bytes 589832 | tf_op jit(solution)/shard_map/ppermute | solution.py:305
  24.6 8.1 %collective-permute-start.9 = (bf16[2,8,1536]{2,1,0:T(8,128)(2,1)S(1)}, bf16[2,8,1536]{2,1,0:T(8,128)(2,1)S(1)}, u32[]{:S(2)}, u32[]{:S(2)}) collective-permute-start(bf16[2,8,1536]{2,1,0:T(8,128)(2,1)S(1)} %get-tuple-element.26), channel_id=1, source_target_pairs={{0,4},{2,6},{4,0},{6,2},{8,12},{10,14},{12,8},{14,10},{1,5},{3,7},... | collective-permute-start | bytes 147464 | tf_op jit(solution)/shard_map/ppermute | solution.py:301
  24.8 7.9 %collective-permute-start.10 = (bf16[2,8,1536]{2,1,0:T(8,128)(2,1)S(1)}, bf16[2,8,1536]{2,1,0:T(8,128)(2,1)S(1)}, u32[]{:S(2)}, u32[]{:S(2)}) collective-permute-start(bf16[2,8,1536]{2,1,0:T(8,128)(2,1)S(1)} %get-tuple-element.27), channel_id=1, source_target_pairs={{0,8},{2,10},{4,12},{6,14},{8,0},{10,2},{12,4},{14,6},{1,9},{3,11}... | collective-permute-start | bytes 147464 | tf_op jit(solution)/shard_map/ppermute | solution.py:301
  26.7 5.9 %collective-permute-start.11 = (bf16[2,8,1536]{2,1,0:T(8,128)(2,1)S(1)}, bf16[2,8,1536]{2,1,0:T(8,128)(2,1)S(1)}, u32[]{:S(2)}, u32[]{:S(2)}) collective-permute-start(bf16[2,8,1536]{2,1,0:T(8,128)(2,1)S(1)} %get-tuple-element.28), channel_id=1, source_target_pairs={{0,12},{2,14},{4,8},{6,10},{8,4},{10,6},{12,0},{14,2},{1,13},{3,15... | collective-permute-start | bytes 147464 | tf_op jit(solution)/shard_map/ppermute | solution.py:301
  29.0 3.6 %collective-permute-start.7 = (f32[8,128]{1,0:T(8,128)S(1)}, f32[8,128]{1,0:T(8,128)S(1)}, u32[]{:S(2)}, u32[]{:S(2)}) collective-permute-start(f32[8,128]{1,0:T(8,128)S(1)} %get-tuple-element.23.refs_0_), channel_id=1, source_target_pairs={{0,2},{2,0},{4,6},{6,4},{8,10},{10,8},{12,14},{14,12},{1,3},{3,1},... | collective-permute-start | bytes 12296 | tf_op jit(solution)/shard_map/ppermute | solution.py:301
  32.8 3.9 %collective-permute-start.12 = (bf16[1,8,1536]{2,1,0:T(8,128)(2,1)S(1)}, bf16[1,8,1536]{2,1,0:T(8,128)(2,1)S(1)}, u32[]{:S(2)}, u32[]{:S(2)}) collective-permute-start(bf16[1,8,1536]{2,1,0:T(8,128)(2,1)S(1)} %get-tuple-element.30), channel_id=1, source_target_pairs={{0,2},{2,0},{4,6},{6,4},{8,10},{10,8},{12,14},{14,12},{1,3},{3,1},... | collective-permute-start | bytes 73736 | tf_op jit(solution)/shard_map/ppermute | solution.py:301

commit v9 on v8

--- a/solution.py
+++ b/solution.py
@@ -38,7 +38,8 @@
     cache_len = key_ref.shape[2]
     kv_local = key_ref.shape[3] // HD
     group = width // key_ref.shape[3]
-    early = [(query_hbm, query_ref), (lengths_hbm, lengths_ref), (key_hbm, key_ref)]
+    early = [(query_hbm, query_ref), (lengths_hbm, lengths_ref)]
+    early += [(key_hbm.at[b], key_ref.at[b]) for b in range(batches)]
     late = [
         (value_hbm, value_ref),
         (residual_hbm, residual_ref),
@@ -52,7 +53,7 @@
     ]
     for copy in copies:
         copy.start()
-    for copy in copies[: len(early)]:
+    for copy in copies[:2]:
         copy.wait()
 
     def stacked(ref):
@@ -66,21 +67,27 @@
     for r in range(rows):
         limit = jnp.where(row_of == r, lengths_ref[r // per_batch, r % per_batch], limit)
     live = position < limit
-    pieces, all_scores = [], []
+    pieces, all_heads = [], []
     for k in range(kv_local):
         heads = jnp.concatenate(
             [queries[:, (k * group + j) * HD : (k * group + j + 1) * HD] for j in range(group)],
             axis=0,
-        ).astype(jnp.bfloat16)
-        columns = slice(k * HD, (k + 1) * HD)
-        scores = jnp.zeros((tall, cache_len), jnp.float32)
-        for r in range(rows):
-            keys = key_ref[r // per_batch, r % per_batch, :, columns]
-            part = lax.dot_general(
-                heads, keys, (((1,), (1,)), ((), ())), preferred_element_type=jnp.float32
-            )
-            scores = jnp.where(row_of == r, part, scores)
-        all_scores.append(scores)
+        )
+        all_heads.append(heads.astype(jnp.bfloat16))
+    all_scores = [jnp.zeros((tall, cache_len), jnp.float32)] * kv_local
+    for b in range(batches):
+        copies[2 + b].wait()
+        for k in range(kv_local):
+            columns = slice(k * HD, (k + 1) * HD)
+            for r in range(b * per_batch, (b + 1) * per_batch):
+                keys = key_ref[b, r % per_batch, :, columns]
+                part = lax.dot_general(
+                    all_heads[k],
+                    keys,
+                    (((1,), (1,)), ((), ())),
+                    preferred_element_type=jnp.float32,
+                )
+                all_scores[k] = jnp.where(row_of == r, part, all_scores[k])
     for copy in copies[len(early) :]:
         copy.wait()
     for k, scores in enumerate(all_scores):
@@ -323,7 +330,7 @@
     )
     width, units = w_gate.shape
     block = min(512, units)
-    piece = min(512, half)
+    piece = min(768, half)
     count = devices * rows
     owners = devices // experts
     hidden, meta = pl.pallas_call(
@@ -338,7 +345,7 @@
             (pltpu.SMEM if array.dtype == jnp.int32 else pltpu.VMEM)(array.shape, array.dtype)
             for array in inputs
         ]
-        + [pltpu.VMEM((16, units), w_up.dtype), pltpu.SemaphoreType.DMA((8,))],
+        + [pltpu.VMEM((16, units), w_up.dtype), pltpu.SemaphoreType.DMA((7 + batches,))],
         compiler_params=pltpu.CompilerParams(vmem_limit_bytes=6 << 20),
     )(*[far(array) for array in inputs], far(w_up))
 

time: 37.5 us -> 37.4 us (level)
  no operation moved by 1% of the time
where the time goes in v9:
time: 37.4 us; the launch traced here: 37.2 us
  starting transfers between devices  16.5 us (44%)
  Pallas kernels  10.3 us (28%)
  waiting for transfers between devices  10.2 us (27%)
    ppermute x9, starting transfers between devices, swap_devices(): lax.ppermute(value, 'devs', [(d, d ^ offset) for d in range(devices)])  15.3 us
    ppermute x9, waiting for transfers between devices, swap_devices(): lax.ppermute(value, 'devs', [(d, d ^ offset) for d in range(devices)])  10.1 us
    pallas_call x1, Pallas kernels, on_device(): pl.pallas_call(functools.partial(expert_kernel, block, experts, parts), i...  3.49 us
    pallas_call x2, Pallas kernels, project(): pl.pallas_call(functools.partial(down_kernel, piece, own), in_specs=[VMEM...  2.43 us
    pallas_call x1, Pallas kernels, on_device(): pl.pallas_call(attend_kernel, in_specs=[HBM] * 8, out_specs=[VMEM] * 2, o...  2.37 us
    pallas_call x1, Pallas kernels, on_device(): pl.pallas_call(functools.partial(gate_kernel, block), in_specs=[VMEM] * (...  1.23 us
    ppermute x4, starting transfers between devices, swap_cores(): return lax.ppermute(value, 'pair', [(0, 1), (1, 0)])  1.12 us
  transfers between devices with their start and end apart: 13, of which 6 were waited for; matrix products, arithmetic and copies ran while one was open for 0% of the time, Pallas kernels for 7%

profile of v9, /device:TPU:0, one launch (start us, length us, event | category | flops | bytes accessed | tf_op | source)
XLA Modules:
  0.0 37.2 jit_solution(10190870237739389567)
XLA Ops:
  0.0 2.4 %shard_map.100 = (bf16[8,1536]{1,0:T(8,128)(2,1)S(1)}, f32[8,128]{1,0:T(8,128)S(1)}) custom-call(bf16[2,4,1536]{2,1,0:T(4,128)(2,1)} %query_hbm.1, bf16[2,4,256,256]{3,2,1,0:T(8,128)(2,1)} %key_hbm.1, bf16[2,4,256,256]{3,2,1,0:T(8,128)(2,1)} %value_hbm.1, s32[2,4]{1,0:T(2,128)} %lengths_hbm.1, bf16[2,4,1536]{2,1,0:T(4,128)(2,1)} %residual_hbm.1, ...), custom_call_target="tpu_custom_call" | custom-call | tf_op jit(solution)/shard_map/pallas_call | solution.py:336
  2.4 3.0 %collective-permute-start = (bf16[8,1536]{1,0:T(8,128)(2,1)S(1)}, bf16[8,1536]{1,0:T(8,128)(2,1)S(1)}, u32[]{:S(2)}, u32[]{:S(2)}) collective-permute-start(bf16[8,1536]{1,0:T(8,128)(2,1)S(1)} %get-tuple-element.18.refs_0_.hidden_ref), channel_id=1, source_target_pairs={{0,2},{2,0},{4,6},{6,4},{8,10},{10,8},{12,14},{14,12},{1,3},{3,1},... | collective-permute-start | bytes 73736 | tf_op jit(solution)/shard_map/ppermute | solution.py:308
  5.4 1.8 %collective-permute-done.refs_1_ = bf16[8,1536]{1,0:T(8,128)(2,1)S(1)} collective-permute-done((bf16[8,1536]{1,0:T(8,128)(2,1)S(1)}, bf16[8,1536]{1,0:T(8,128)(2,1)S(1)}, u32[]{:S(2)}, u32[]{:S(2)}) %collective-permute-start) | collective-permute-done | bytes 24608 | tf_op jit(solution)/shard_map/ppermute | solution.py:308
  7.2 4.2 %collective-permute-start.3 = (bf16[2,8,1536]{2,1,0:T(8,128)(2,1)S(1)}, bf16[2,8,1536]{2,1,0:T(8,128)(2,1)S(1)}, u32[]{:S(2)}, u32[]{:S(2)}) collective-permute-start(bf16[2,8,1536]{2,1,0:T(8,128)(2,1)S(1)} %shard_map.101.refs_0_), channel_id=1, source_target_pairs={{0,12},{2,14},{4,8},{6,10},{8,4},{10,6},{12,0},{14,2},{1,13},{3,15... | collective-permute-start | bytes 147464 | tf_op jit(solution)/shard_map/ppermute | solution.py:308
  11.4 0.6 %collective-permute-start.1 = (bf16[2,8,1536]{2,1,0:T(8,128)(2,1)S(1)}, bf16[2,8,1536]{2,1,0:T(8,128)(2,1)S(1)}, u32[]{:S(2)}, u32[]{:S(2)}) collective-permute-start(bf16[2,8,1536]{2,1,0:T(8,128)(2,1)S(1)} %shard_map.101.refs_0_), channel_id=1, source_target_pairs={{0,4},{2,6},{4,0},{6,2},{8,12},{10,14},{12,8},{14,10},{1,5},{3,7},... | collective-permute-start | bytes 147464 | tf_op jit(solution)/shard_map/ppermute | solution.py:308
  12.1 0.5 %collective-permute-start.4 = (f32[8,128]{1,0:T(8,128)S(1)}, f32[8,128]{1,0:T(8,128)S(1)}, u32[]{:S(2)}, u32[]{:S(2)}) collective-permute-start(f32[8,128]{1,0:T(8,128)S(1)} %get-tuple-element.19.refs_2_.refs_7_), channel_id=1, source_target_pairs={{0,1},{1,0},{2,3},{3,2},{4,5},{5,4},{6,7},{7,6},{8,9},{9,8},{10,11... | collective-permute-start | bytes 12296 | tf_op jit(solution)/shard_map/ppermute | solution.py:312
  12.6 1.0 %collective-permute-done.3.refs_2_ = bf16[2,8,1536]{2,1,0:T(8,128)(2,1)S(1)} collective-permute-done((bf16[2,8,1536]{2,1,0:T(8,128)(2,1)S(1)}, bf16[2,8,1536]{2,1,0:T(8,128)(2,1)S(1)}, u32[]{:S(2)}, u32[]{:S(2)}) %collective-permute-start.3) | collective-permute-done | bytes 49184 | tf_op jit(solution)/shard_map/ppermute | solution.py:308
  13.5 2.9 %collective-permute-done.2.refs_1_ = bf16[2,8,1536]{2,1,0:T(8,128)(2,1)S(1)} collective-permute-done((bf16[2,8,1536]{2,1,0:T(8,128)(2,1)S(1)}, bf16[2,8,1536]{2,1,0:T(8,128)(2,1)S(1)}, u32[]{:S(2)}, u32[]{:S(2)}) %collective-permute-start.2) | collective-permute-done | bytes 49184 | tf_op jit(solution)/shard_map/ppermute | solution.py:308
  16.5 0.1 collective-permute-start.6
  16.6 1.2 %shard_map.103.refs_6_ = f32[64,2048]{1,0:T(8,128)S(1)} custom-call(bf16[2,8,1536]{2,1,0:T(8,128)(2,1)S(1)} %shard_map.101.refs_0_, bf16[6,8,1536]{2,1,0:T(8,128)(2,1)S(1)} %shard_map.102.refs_1_, bf16[3072,2048]{1,0:T(8,128)(2,1)S(1)} %copy-done), custom_call_target="tpu_custom_call" | custom-call | flops 402653184 | bytes 6291456 | tf_op jit(solution)/shard_map/pallas_call | solution.py:373
  17.8 0.1 collective-permute-done.6.refs_3_
  17.9 3.5 %shard_map.104 = (bf16[64,2048]{1,0:T(8,128)(2,1)S(1)}, f32[8,128]{1,0:T(8,128)S(1)}) custom-call(bf16[2,8,1536]{2,1,0:T(8,128)(2,1)S(1)} %shard_map.101.refs_0_, bf16[6,8,1536]{2,1,0:T(8,128)(2,1)S(1)} %shard_map.102.refs_1_, bf16[2,8,1536]{2,1,0:T(8,128)(2,1)S(1)} %collective-permute-done.5.refs_2_, ...), custom_call_target="tpu_custom_call" | custom-call | tf_op jit(solution)/shard_map/pallas_call | solution.py:383
  21.4 1.2 %shard_map.107 = bf16[8,8,1536]{2,1,0:T(8,128)(2,1)S(1)} custom-call(bf16[64,2048]{1,0:T(8,128)(2,1)S(1)} %get-tuple-element.24.units_ref, bf16[2048,3072]{1,0:T(8,128)(2,1)S(1)} %bitcast.5), custom_call_target="tpu_custom_call" | custom-call | flops 402653184 | bytes 6291456 | tf_op jit(solution)/shard_map/pallas_call | solution.py:396
  22.7 0.5 %collective-permute-start.8 = (bf16[8,8,1536]{2,1,0:T(8,128)(2,1)S(1)}, bf16[8,8,1536]{2,1,0:T(8,128)(2,1)S(1)}, u32[]{:S(2)}, u32[]{:S(2)}) collective-permute-start(bf16[8,8,1536]{2,1,0:T(8,128)(2,1)S(1)} %shard_map.107), channel_id=1, source_target_pairs={{0,1},{1,0},{2,3},{3,2},{4,5},{5,4},{6,7},{7,6},{8,9},{9,8},{10,11... | collective-permute-start | bytes 589832 | tf_op jit(solution)/shard_map/ppermute | solution.py:312
  23.2 1.2 %shard_map.106.kept_ref = f32[8,8,1536]{2,1,0:T(8,128)S(1)} custom-call(bf16[64,2048]{1,0:T(8,128)(2,1)S(1)} %get-tuple-element.24.units_ref, bf16[2048,3072]{1,0:T(8,128)(2,1)S(1)} %bitcast.5), custom_call_target="tpu_custom_call" | custom-call | flops 402653184 | bytes 6291456 | tf_op jit(solution)/shard_map/pallas_call | solution.py:396
  24.5 0.2 collective-permute-start.9
  24.7 2.0 %collective-permute-start.10 = (bf16[2,8,1536]{2,1,0:T(8,128)(2,1)S(1)}, bf16[2,8,1536]{2,1,0:T(8,128)(2,1)S(1)}, u32[]{:S(2)}, u32[]{:S(2)}) collective-permute-start(bf16[2,8,1536]{2,1,0:T(8,128)(2,1)S(1)} %get-tuple-element.27), channel_id=1, source_target_pairs={{0,8},{2,10},{4,12},{6,14},{8,0},{10,2},{12,4},{14,6},{1,9},{3,11}... | collective-permute-start | bytes 147464 | tf_op jit(solution)/shard_map/ppermute | solution.py:308
  26.6 2.3 %collective-permute-start.11 = (bf16[2,8,1536]{2,1,0:T(8,128)(2,1)S(1)}, bf16[2,8,1536]{2,1,0:T(8,128)(2,1)S(1)}, u32[]{:S(2)}, u32[]{:S(2)}) collective-permute-start(bf16[2,8,1536]{2,1,0:T(8,128)(2,1)S(1)} %get-tuple-element.28), channel_id=1, source_target_pairs={{0,12},{2,14},{4,8},{6,10},{8,4},{10,6},{12,0},{14,2},{1,13},{3,15... | collective-permute-start | bytes 147464 | tf_op jit(solution)/shard_map/ppermute | solution.py:308
  28.9 1.5 %collective-permute-start.7 = (f32[8,128]{1,0:T(8,128)S(1)}, f32[8,128]{1,0:T(8,128)S(1)}, u32[]{:S(2)}, u32[]{:S(2)}) collective-permute-start(f32[8,128]{1,0:T(8,128)S(1)} %get-tuple-element.23.refs_0_), channel_id=1, source_target_pairs={{0,2},{2,0},{4,6},{6,4},{8,10},{10,8},{12,14},{14,12},{1,3},{3,1},... | collective-permute-start | bytes 12296 | tf_op jit(solution)/shard_map/ppermute | solution.py:308
  30.4 2.1 %collective-permute-done.7.refs_1_ = f32[8,128]{1,0:T(8,128)S(1)} collective-permute-done((f32[8,128]{1,0:T(8,128)S(1)}, f32[8,128]{1,0:T(8,128)S(1)}, u32[]{:S(2)}, u32[]{:S(2)}) %collective-permute-start.7) | collective-permute-done | bytes 4128 | tf_op jit(solution)/shard_map/ppermute | solution.py:308
  32.6 0.1 shard_map.109
  32.7 1.6 %collective-permute-start.12 = (bf16[1,8,1536]{2,1,0:T(8,128)(2,1)S(1)}, bf16[1,8,1536]{2,1,0:T(8,128)(2,1)S(1)}, u32[]{:S(2)}, u32[]{:S(2)}) collective-permute-start(bf16[1,8,1536]{2,1,0:T(8,128)(2,1)S(1)} %get-tuple-element.30), channel_id=1, source_target_pairs={{0,2},{2,0},{4,6},{6,4},{8,10},{10,8},{12,14},{14,12},{1,3},{3,1},... | collective-permute-start | bytes 73736 | tf_op jit(solution)/shard_map/ppermute | solution.py:308
  34.3 2.3 %collective-permute-done.12.received_ref = bf16[1,8,1536]{2,1,0:T(8,128)(2,1)S(1)} collective-permute-done((bf16[1,8,1536]{2,1,0:T(8,128)(2,1)S(1)}, bf16[1,8,1536]{2,1,0:T(8,128)(2,1)S(1)}, u32[]{:S(2)}, u32[]{:S(2)}) %collective-permute-start.12) | collective-permute-done | bytes 24608 | tf_op jit(solution)/shard_map/ppermute | solution.py:308
  36.6 0.6 %shard_map.110 = bf16[2,4,1536]{2,1,0:T(4,128)(2,1)} custom-call(bf16[8,1536]{1,0:T(8,128)(2,1)S(1)} %get-tuple-element.18.refs_0_.hidden_ref, f32[1,8,1536]{2,1,0:T(8,128)S(1)} %get-tuple-element.29.kept_ref, bf16[1,8,1536]{2,1,0:T(8,128)(2,1)S(1)} %collective-permute-done.12.received_ref), custom_call_target="tpu_custom_call" | custom-call | tf_op jit(solution)/shard_map/pallas_call | solution.py:435
  (29 shorter events, 0.2 us)
Async XLA Ops:
  0.0 7.2 %copy-start = (bf16[3072,2048]{1,0:T(8,128)(2,1)S(1)}, bf16[3072,2048]{1,0:T(8,128)(2,1)}, u32[]{:S(2)}) copy-start(bf16[3072,2048]{1,0:T(8,128)(2,1)} %refs_5_.1) | copy-start | bytes 37748740
  0.0 16.4 %slice-start = ((s8[12582912]{0:T(1024)(128)(4,1)}), s8[4194304]{0:T(1024)(128)(4,1)S(1)}, s32[]{:S(2)}) async-start(s8[12582912]{0:T(1024)(128)(4,1)} %bitcast.2), calls=%async_computation | async-start | bytes 8388608
  0.0 16.4 %slice-start.1 = ((s8[12582912]{0:T(1024)(128)(4,1)}), s8[4194304]{0:T(1024)(128)(4,1)S(1)}, s32[]{:S(2)}) async-start(s8[12582912]{0:T(1024)(128)(4,1)} %bitcast.2), calls=%async_computation.1 | async-start | bytes 8388608
  2.4 4.8 %collective-permute-start = (bf16[8,1536]{1,0:T(8,128)(2,1)S(1)}, bf16[8,1536]{1,0:T(8,128)(2,1)S(1)}, u32[]{:S(2)}, u32[]{:S(2)}) collective-permute-start(bf16[8,1536]{1,0:T(8,128)(2,1)S(1)} %get-tuple-element.18.refs_0_.hidden_ref), channel_id=1, source_target_pairs={{0,2},{2,0},{4,6},{6,4},{8,10},{10,8},{12,14},{14,12},{1,3},{3,1},... | collective-permute-start | bytes 73736 | tf_op jit(solution)/shard_map/ppermute | solution.py:308
  7.2 9.2 %slice-start.2 = ((s8[12582912]{0:T(1024)(128)(4,1)}), s8[4194304]{0:T(1024)(128)(4,1)S(1)}, s32[]{:S(2)}) async-start(s8[12582912]{0:T(1024)(128)(4,1)} %bitcast.2), calls=%async_computation.2 | async-start | bytes 8388608
  7.2 6.3 %collective-permute-start.3 = (bf16[2,8,1536]{2,1,0:T(8,128)(2,1)S(1)}, bf16[2,8,1536]{2,1,0:T(8,128)(2,1)S(1)}, u32[]{:S(2)}, u32[]{:S(2)}) collective-permute-start(bf16[2,8,1536]{2,1,0:T(8,128)(2,1)S(1)} %shard_map.101.refs_0_), channel_id=1, source_target_pairs={{0,12},{2,14},{4,8},{6,10},{8,4},{10,6},{12,0},{14,2},{1,13},{3,15... | collective-permute-start | bytes 147464 | tf_op jit(solution)/shard_map/ppermute | solution.py:308
  11.4 5.0 %collective-permute-start.2 = (bf16[2,8,1536]{2,1,0:T(8,128)(2,1)S(1)}, bf16[2,8,1536]{2,1,0:T(8,128)(2,1)S(1)}, u32[]{:S(2)}, u32[]{:S(2)}) collective-permute-start(bf16[2,8,1536]{2,1,0:T(8,128)(2,1)S(1)} %shard_map.101.refs_0_), channel_id=1, source_target_pairs={{0,8},{2,10},{4,12},{6,14},{8,0},{10,2},{12,4},{14,6},{1,9},{3,11}... | collective-permute-start | bytes 147464 | tf_op jit(solution)/shard_map/ppermute | solution.py:308
  11.4 5.0 %collective-permute-start.1 = (bf16[2,8,1536]{2,1,0:T(8,128)(2,1)S(1)}, bf16[2,8,1536]{2,1,0:T(8,128)(2,1)S(1)}, u32[]{:S(2)}, u32[]{:S(2)}) collective-permute-start(bf16[2,8,1536]{2,1,0:T(8,128)(2,1)S(1)} %shard_map.101.refs_0_), channel_id=1, source_target_pairs={{0,4},{2,6},{4,0},{6,2},{8,12},{10,14},{12,8},{14,10},{1,5},{3,7},... | collective-permute-start | bytes 147464 | tf_op jit(solution)/shard_map/ppermute | solution.py:308
  12.1 4.4 %collective-permute-start.5 = (bf16[2,8,1536]{2,1,0:T(8,128)(2,1)S(1)}, bf16[2,8,1536]{2,1,0:T(8,128)(2,1)S(1)}, u32[]{:S(2)}, u32[]{:S(2)}) collective-permute-start(bf16[2,8,1536]{2,1,0:T(8,128)(2,1)S(1)} %shard_map.101.refs_0_), channel_id=1, source_target_pairs={{0,1},{1,0},{2,3},{3,2},{4,5},{5,4},{6,7},{7,6},{8,9},{9,8},{10,11... | collective-permute-start | bytes 147464 | tf_op jit(solution)/shard_map/ppermute | solution.py:312
  12.1 4.4 %collective-permute-start.4 = (f32[8,128]{1,0:T(8,128)S(1)}, f32[8,128]{1,0:T(8,128)S(1)}, u32[]{:S(2)}, u32[]{:S(2)}) collective-permute-start(f32[8,128]{1,0:T(8,128)S(1)} %get-tuple-element.19.refs_2_.refs_7_), channel_id=1, source_target_pairs={{0,1},{1,0},{2,3},{3,2},{4,5},{5,4},{6,7},{7,6},{8,9},{9,8},{10,11... | collective-permute-start | bytes 12296 | tf_op jit(solution)/shard_map/ppermute | solution.py:312
  16.5 1.4 %collective-permute-start.6 = (bf16[6,8,1536]{2,1,0:T(8,128)(2,1)S(1)}, bf16[6,8,1536]{2,1,0:T(8,128)(2,1)S(1)}, u32[]{:S(2)}, u32[]{:S(2)}) collective-permute-start(bf16[6,8,1536]{2,1,0:T(8,128)(2,1)S(1)} %shard_map.102.refs_1_), channel_id=1, source_target_pairs={{0,1},{1,0},{2,3},{3,2},{4,5},{5,4},{6,7},{7,6},{8,9},{9,8},{10,11... | collective-permute-start | bytes 442376 | tf_op jit(solution)/shard_map/ppermute | solution.py:312
  16.6 4.9 %slice-start.3 = ((s8[12582912]{0:T(1024)(128)(4,1)}), s8[4194304]{0:T(1024)(128)(4,1)S(1)}, s32[]{:S(2)}) async-start(s8[12582912]{0:T(1024)(128)(4,1)} %bitcast.4), calls=%async_computation.3 | async-start | bytes 8388608
  16.6 4.8 %slice-start.4 = ((s8[12582912]{0:T(1024)(128)(4,1)}), s8[4194304]{0:T(1024)(128)(4,1)S(1)}, s32[]{:S(2)}) async-start(s8[12582912]{0:T(1024)(128)(4,1)} %bitcast.4), calls=%async_computation.4 | async-start | bytes 8388608
  17.8 3.6 %slice-start.5 = ((s8[12582912]{0:T(1024)(128)(4,1)}), s8[4194304]{0:T(1024)(128)(4,1)S(1)}, s32[]{:S(2)}) async-start(s8[12582912]{0:T(1024)(128)(4,1)} %bitcast.4), calls=%async_computation.5 | async-start | bytes 8388608
  22.7 1.8 %collective-permute-start.8 = (bf16[8,8,1536]{2,1,0:T(8,128)(2,1)S(1)}, bf16[8,8,1536]{2,1,0:T(8,128)(2,1)S(1)}, u32[]{:S(2)}, u32[]{:S(2)}) collective-permute-start(bf16[8,8,1536]{2,1,0:T(8,128)(2,1)S(1)} %shard_map.107), channel_id=1, source_target_pairs={{0,1},{1,0},{2,3},{3,2},{4,5},{5,4},{6,7},{7,6},{8,9},{9,8},{10,11... | collective-permute-start | bytes 589832 | tf_op jit(solution)/shard_map/ppermute | solution.py:312
  24.5 8.1 %collective-permute-start.9 = (bf16[2,8,1536]{2,1,0:T(8,128)(2,1)S(1)}, bf16[2,8,1536]{2,1,0:T(8,128)(2,1)S(1)}, u32[]{:S(2)}, u32[]{:S(2)}) collective-permute-start(bf16[2,8,1536]{2,1,0:T(8,128)(2,1)S(1)} %get-tuple-element.26), channel_id=1, source_target_pairs={{0,4},{2,6},{4,0},{6,2},{8,12},{10,14},{12,8},{14,10},{1,5},{3,7},... | collective-permute-start | bytes 147464 | tf_op jit(solution)/shard_map/ppermute | solution.py:308
  24.7 7.9 %collective-permute-start.10 = (bf16[2,8,1536]{2,1,0:T(8,128)(2,1)S(1)}, bf16[2,8,1536]{2,1,0:T(8,128)(2,1)S(1)}, u32[]{:S(2)}, u32[]{:S(2)}) collective-permute-start(bf16[2,8,1536]{2,1,0:T(8,128)(2,1)S(1)} %get-tuple-element.27), channel_id=1, source_target_pairs={{0,8},{2,10},{4,12},{6,14},{8,0},{10,2},{12,4},{14,6},{1,9},{3,11}... | collective-permute-start | bytes 147464 | tf_op jit(solution)/shard_map/ppermute | solution.py:308
  26.6 5.9 %collective-permute-start.11 = (bf16[2,8,1536]{2,1,0:T(8,128)(2,1)S(1)}, bf16[2,8,1536]{2,1,0:T(8,128)(2,1)S(1)}, u32[]{:S(2)}, u32[]{:S(2)}) collective-permute-start(bf16[2,8,1536]{2,1,0:T(8,128)(2,1)S(1)} %get-tuple-element.28), channel_id=1, source_target_pairs={{0,12},{2,14},{4,8},{6,10},{8,4},{10,6},{12,0},{14,2},{1,13},{3,15... | collective-permute-start | bytes 147464 | tf_op jit(solution)/shard_map/ppermute | solution.py:308
  28.9 3.6 %collective-permute-start.7 = (f32[8,128]{1,0:T(8,128)S(1)}, f32[8,128]{1,0:T(8,128)S(1)}, u32[]{:S(2)}, u32[]{:S(2)}) collective-permute-start(f32[8,128]{1,0:T(8,128)S(1)} %get-tuple-element.23.refs_0_), channel_id=1, source_target_pairs={{0,2},{2,0},{4,6},{6,4},{8,10},{10,8},{12,14},{14,12},{1,3},{3,1},... | collective-permute-start | bytes 12296 | tf_op jit(solution)/shard_map/ppermute | solution.py:308
  32.7 3.9 %collective-permute-start.12 = (bf16[1,8,1536]{2,1,0:T(8,128)(2,1)S(1)}, bf16[1,8,1536]{2,1,0:T(8,128)(2,1)S(1)}, u32[]{:S(2)}, u32[]{:S(2)}) collective-permute-start(bf16[1,8,1536]{2,1,0:T(8,128)(2,1)S(1)} %get-tuple-element.30), channel_id=1, source_target_pairs={{0,2},{2,0},{4,6},{6,4},{8,10},{10,8},{12,14},{14,12},{1,3},{3,1},... | collective-permute-start | bytes 73736 | tf_op jit(solution)/shard_map/ppermute | solution.py:308
